TPU v7x, 32 devices: a whole 2x2x4 slice. The times are simulated.
32 devices in a mesh: ctx: 8 (over y, x, core), tp: 4 (over z).
Axes of the slice: x: 2, y: 2, z: 4, core: 2. Of those that a mesh axis runs over, the one named last changes fastest.
Arguments:
- stream: bfloat16 [3072, 8192], P('ctx', 'tp'), may hold values from -40 to 40
- pending: bfloat16 [4, 3072, 8192], P('tp', 'ctx'), may hold values from -5 to 5
- norm_gain: bfloat16 [8192], replicated, may hold values from 0.099609375 to 1.8984375
- w_query: bfloat16 [8192, 4096], P('ctx', 'tp'), may hold values from -0.0625 to 0.0625
- w_key: bfloat16 [8192, 1024], P('ctx'), may hold values from -0.375 to 0.375
- w_value: bfloat16 [8192, 1024], P('ctx'), may hold values from -0.1875 to 0.1875
- w_out: bfloat16 [4096, 8192], P('tp', 'ctx'), may hold values from -0.09375 to 0.09375
- prefix_keys: bfloat16 [8, 6144, 128], P(None, 'ctx'), may hold values from -600 to 600
- prefix_values: bfloat16 [8, 6144, 128], P(None, 'ctx'), may hold values from -6 to 6
- prefix_segments: int32 [6144], P('ctx'), may hold values from 0 to 15, never falling along the last dimension, each value on 1 to 768 neighbouring positions
- stretch_segments: int32 [3072], P('ctx'), may hold values from 0 to 15, never falling along the last dimension, each value on 1 to 384 neighbouring positions
- stretch_offset: int32 [1], replicated, may hold values from 6144 to 12287
Outputs:
- output: bfloat16 [3072, 8192], P('ctx', 'tp')
Inputs may be any that keep to these rules, and one draw needn't show every extreme that they name: `prefix_segments`: never falls along the positions; every trajectory 0 to 15 occurs. `stretch_segments`: never falls along the positions; every trajectory 0 to 15 occurs.
All inputs are finite; a program needn't handle non-finite values.
Results may differ from a plain program's by a relative error of at most 0.024.
Values may be sent and summed in bfloat16 or wider, within the bound.
No kernel may reach another device: no remote copies, remote signals or barrier semaphores. Data moves between devices by JAX's collectives and lax.ppermute only.
A program may use at most 256 MiB of HBM per device.

v0:
```python
import functools
import math

import jax
import jax.numpy as jnp
from jax import lax
from jax.experimental import pallas as pl
from jax.experimental.pallas import tpu as pltpu
from jax.sharding import PartitionSpec as P

HQ = 32
KVH = 8
HD = 128
NTRAJ = 16


ROPE_BASE = 500000.0
ROPE_FACTOR = 8.0
LOW_FREQ = 1.0
HIGH_FREQ = 4.0
INITIAL_SPAN = 8192.0
NORM_EPSILON = 1e-05
MASKED = -1e30


def inverse_freqs(head_width):
    pair_index = jnp.arange(head_width // 2, dtype=jnp.float32)
    base_freq = ROPE_BASE ** (-2.0 * pair_index / head_width)
    wavelength = 2.0 * math.pi / base_freq
    smooth = (INITIAL_SPAN / wavelength - LOW_FREQ) / (HIGH_FREQ - LOW_FREQ)
    blended = (1.0 - smooth) * base_freq / ROPE_FACTOR + smooth * base_freq
    return jnp.where(
        wavelength < INITIAL_SPAN / HIGH_FREQ,
        base_freq,
        jnp.where(wavelength > INITIAL_SPAN / LOW_FREQ, base_freq / ROPE_FACTOR, blended),
    )


def rotate(vectors, positions):
    head_width = vectors.shape[-1]
    angles = positions[..., None] * inverse_freqs(head_width)
    cosine = jnp.cos(angles)
    sinus = jnp.sin(angles)
    first_half = vectors[..., : head_width // 2]
    second_half = vectors[..., head_width // 2 :]
    return jnp.concatenate(
        [first_half * cosine - second_half * sinus, second_half * cosine + first_half * sinus],
        axis=-1,
    )


def visibility(key_labels, is_prefix, key_pos, query_segs, query_index):
    earlier = key_labels[None, :] <= query_segs[:, None]
    same = (key_labels[None, :] == query_segs[:, None]) & (key_pos[None, :] <= query_index[:, None])
    return jnp.where(is_prefix[None, :], earlier, same)


def attend_whole(grouped, key_block, value_block, seen):
    scores = jnp.einsum("hrd,hnd->hrn", grouped, key_block, preferred_element_type=jnp.float32) * (
        1.0 / math.sqrt(HD)
    )
    scores = jnp.where(seen[None], scores, MASKED)
    new_max = jnp.max(scores, axis=2)
    weights = jnp.where(seen[None], jnp.exp(scores - new_max[..., None]), 0.0)
    totals = jnp.sum(weights, axis=2)
    numerator = jnp.einsum(
        "hrn,hnd->hrd",
        weights.astype(jnp.bfloat16),
        value_block,
        preferred_element_type=jnp.float32,
    )
    return numerator / totals[..., None]


def per_device_any(
    stream,
    pending,
    norm_gain,
    w_query,
    w_key,
    w_value,
    w_out,
    prefix_keys,
    prefix_values,
    prefix_segments,
    stretch_segments,
    stretch_offset,
):
    tok_rows = stream.shape[0]
    prefix_rows = prefix_keys.shape[1]
    ctx_index = lax.axis_index("ctx")
    tp_index = lax.axis_index("tp")
    gain_wide = norm_gain.astype(jnp.float32)
    whole = lax.all_gather(stream, "tp", axis=1, tiled=True).astype(jnp.float32)
    mean_square = jnp.mean(whole * whole, axis=1, keepdims=True)
    normed = (whole * lax.rsqrt(mean_square + NORM_EPSILON) * gain_wide).astype(jnp.bfloat16)
    q_cols = w_query.shape[1]
    q_heads = q_cols // HD
    full_group = HQ // KVH
    kv_heads = max(1, q_heads // full_group)
    group_size = q_heads // kv_heads
    head_start = tp_index * q_heads // full_group
    kv_cols = kv_heads * HD
    key_slice = lax.dynamic_slice_in_dim(w_key, head_start * HD, kv_cols, 1)
    value_slice = lax.dynamic_slice_in_dim(w_value, head_start * HD, kv_cols, 1)
    pieces = (
        lax.all_gather(w_query, "ctx", axis=0, tiled=True),
        lax.all_gather(key_slice, "ctx", axis=0, tiled=True),
        lax.all_gather(value_slice, "ctx", axis=0, tiled=True),
    )
    query_raw, key_full, value_full = tuple(
        (jnp.dot(normed, piece_rows, preferred_element_type=jnp.float32) for piece_rows in pieces)
    )
    token_index = ctx_index * tok_rows + jnp.arange(tok_rows, dtype=jnp.int32)
    positions = stretch_offset[0].astype(jnp.float32) + token_index.astype(jnp.float32)
    query_rows = rotate(query_raw.reshape(tok_rows, q_heads, HD), positions[:, None]).astype(
        jnp.bfloat16
    )
    new_keys = jnp.transpose(
        rotate(key_full.reshape(tok_rows, kv_heads, HD), positions[:, None]).astype(jnp.bfloat16),
        (1, 0, 2),
    )
    new_values = jnp.transpose(
        value_full.astype(jnp.bfloat16).reshape(tok_rows, kv_heads, HD), (1, 0, 2)
    )
    old_keys = lax.dynamic_slice_in_dim(prefix_keys, head_start, kv_heads, 0)
    old_values = lax.dynamic_slice_in_dim(prefix_values, head_start, kv_heads, 0)
    local_keys = jnp.concatenate([old_keys, new_keys], 1)
    local_values = jnp.concatenate([old_values, new_values], 1)
    key_labels = jnp.concatenate([prefix_segments, stretch_segments])
    key_span = prefix_rows + tok_rows
    grouped = jnp.transpose(
        query_rows.reshape(tok_rows, kv_heads, group_size, HD), (1, 0, 2, 3)
    ).reshape(kv_heads, tok_rows * group_size, HD)
    query_index = jnp.repeat(token_index, group_size)
    query_segs = jnp.repeat(stretch_segments, group_size)
    both = jnp.stack([local_keys, local_values])
    kv_block = lax.all_gather(both, "ctx", axis=2, tiled=True)
    label_block = lax.all_gather(key_labels[None, None, :], "ctx", axis=2, tiled=True)
    key_count = kv_block.shape[2]
    absolute = jnp.arange(key_count, dtype=jnp.int32)
    within = absolute % key_span
    key_pos = absolute // key_span * tok_rows + within - prefix_rows
    seen = visibility(label_block[0, 0], within < prefix_rows, key_pos, query_segs, query_index)
    attended_heads = attend_whole(grouped, kv_block[0], kv_block[1], seen).astype(jnp.bfloat16)
    attended = jnp.transpose(
        attended_heads.reshape(kv_heads, tok_rows, group_size, HD), (1, 0, 2, 3)
    ).reshape(tok_rows, q_cols)
    head_terms = jnp.dot(
        attended,
        lax.all_gather(w_out, "ctx", axis=1, tiled=True),
        preferred_element_type=jnp.float32,
    )
    head_share, pending_share = (
        lax.psum_scatter(
            head_terms.astype(jnp.bfloat16), "tp", scatter_dimension=1, tiled=True
        ).astype(jnp.float32),
        lax.psum_scatter(
            pending[0].astype(jnp.float32).astype(jnp.bfloat16),
            "tp",
            scatter_dimension=1,
            tiled=True,
        ).astype(jnp.float32),
    )
    block_share = head_share + pending_share
    return (stream.astype(jnp.float32) + block_share).astype(jnp.bfloat16)


N_CTX = 8
N_TP = 4
GRANT = 60 * 1024 * 1024


def swap(x, bit):
    return lax.ppermute(x, "ctx", [(c, c ^ bit) for c in range(N_CTX)])


def hop_up(v, pairs):
    return lax.ppermute(v, "tp", [(i, i + 1) for i in pairs])


def hop_down(v, pairs):
    return lax.ppermute(v, "tp", [(N_TP - 1 - i, N_TP - 2 - i) for i in pairs])


def rotated(v, cosine, sinus):
    return v * cosine + pltpu.roll(v, HD // 2, 1) * sinus


HBM = pl.BlockSpec(memory_space=pltpu.HBM)
VMEM = pl.BlockSpec(memory_space=pltpu.VMEM)
SMEM = pl.BlockSpec(memory_space=pltpu.SMEM)
ANY = pl.BlockSpec(memory_space=pl.ANY)
LITTLE = pl.CostEstimate(flops=0, bytes_accessed=1024, transcendentals=0)


def specs_of(arrays):
    return [HBM if a.size > 200000 else ANY for a in arrays]


def move(plan, shapes, ids, sources, arrived=()):
    count = len(sources)

    def kernel(ids_ref, *refs):
        outs, sems = refs[count + len(arrived) : -1], refs[-1]
        waits = []
        for at, (choices, dst) in enumerate(plan(ids_ref, refs[:count], outs)):
            for cond, src in choices:
                copy = pltpu.make_async_copy(src, dst, sems.at[at])
                if cond is None:
                    copy.start()
                else:
                    pl.when(cond)(copy.start)
            waits.append(copy)
        for copy in waits:
            copy.wait()

    return pl.pallas_call(
        kernel,
        out_shape=tuple(jax.ShapeDtypeStruct(shape, jnp.bfloat16) for shape in shapes),
        in_specs=[SMEM] + [HBM] * count + specs_of(arrived),
        out_specs=tuple(VMEM for _ in shapes),
        scratch_shapes=[pltpu.SemaphoreType.DMA((40,))],
        compiler_params=pltpu.CompilerParams(vmem_limit_bytes=GRANT),
        cost_estimate=LITTLE,
        name=plan.__name__,
    )(ids, *sources, *arrived)


def gate(x, *arrived):
    return pl.pallas_call(
        lambda *refs: None,
        out_shape=jax.ShapeDtypeStruct(x.shape, x.dtype),
        in_specs=[HBM] + specs_of(arrived),
        out_specs=HBM,
        input_output_aliases={0: 0},
        compiler_params=pltpu.CompilerParams(vmem_limit_bytes=GRANT),
        cost_estimate=LITTLE,
        name="gate",
    )(x, *arrived)


def pick(z, options, ids, arrived=()):
    distinct = list({id(o): o for o in options}.values())

    def pick_plan(at, src, out):
        yield (
            [(at[2] == i, src[[o is d for d in distinct].index(True)]) for i, o in enumerate(options)],
            out[0],
        )

    return move(pick_plan, (options[0].shape,), ids, distinct, arrived)[0]


def hops(ids, pending, up, down, offset, relay, both, arrived=()):
    tok, feat = up.shape

    def kernel(ids_ref, pending_ref, up_ref, down_ref, *refs):
        out_up, out_down, buf, sems = refs[len(arrived) :]
        z = ids_ref[2]
        todo = []
        for i, (src, out, step, at) in enumerate(
            ((up_ref, out_up, offset, z), (down_ref, out_down, -offset, N_TP - 1 - z))
        ):
            is_relay = functools.reduce(jnp.logical_or, [at == p for p in relay], at < 0)
            is_both = functools.reduce(jnp.logical_or, [at == p for p in both], at < 0)
            place = jnp.clip(z + step, 0, N_TP - 1)
            share = pltpu.make_async_copy(
                pending_ref.at[0, :, pl.ds(multiple(place, feat), feat)], out, sems.at[i]
            )
            passed = pltpu.make_async_copy(src, out, sems.at[i])
            added = pltpu.make_async_copy(src, buf.at[i], sems.at[2 + i])
            pl.when(is_relay)(passed.start)
            pl.when(jnp.logical_not(is_relay))(share.start)
            pl.when(is_both)(added.start)
            todo.append((passed, added, is_both, out, i))
        for passed, added, is_both, out, i in todo:
            passed.wait()

            @pl.when(is_both)
            def _():
                added.wait()
                out[...] += buf[i]

    shape = jax.ShapeDtypeStruct((tok, feat), jnp.bfloat16)
    return pl.pallas_call(
        kernel,
        out_shape=(shape, shape),
        in_specs=[SMEM, HBM, HBM, HBM] + specs_of(arrived),
        out_specs=(VMEM, VMEM),
        scratch_shapes=[
            pltpu.VMEM((2, tok, feat), jnp.bfloat16),
            pltpu.SemaphoreType.DMA((4,)),
        ],
        compiler_params=pltpu.CompilerParams(vmem_limit_bytes=GRANT),
        cost_estimate=LITTLE,
        name="hops",
    )(ids, pending, up, down, *arrived)


def one(src, dst):
    return ([(None, src)], dst)


def multiple(value, of=128):
    return pl.multiple_of(value * of, of)


def project_kernel(scale, at_kv, ids_ref, *refs):
    xs, ws = refs[:8], refs[8:16]
    factor_ref, cos_ref, sin_ref, q_ref, kv_ref, x_buf, w_buf, x_sem, w_sem = refs[16:]
    chip, core = ids_ref[0], ids_ref[1]
    tok, half, cols = xs[0].shape[0], x_buf.shape[-1], ws[0].shape[1]
    fold = half // 2
    mine = pl.multiple_of(core * tok, 128)
    theirs = pl.multiple_of((1 - core) * tok, 128)
    waits = []
    for r in range(4):
        place = ids_ref[3 + r]
        for h in range(2):
            at = 2 * r + h
            waits.append([])
            for i in range(3):
                for m in range(4):
                    src, dst = ws[2 * m + h], w_buf.at[at]
                    if i == 0:
                        src, dst = src.at[pl.ds(0, half)], dst.at[:, pl.ds(0, cols)]
                    else:
                        lanes = pl.ds((i - 1) * 2 * HD, 2 * HD)
                        src = src.at[pl.ds(at_kv, fold), lanes]
                        dst = dst.at[pl.ds((i - 1) * fold, fold), pl.ds(cols, 2 * HD)]
                    copy = pltpu.make_async_copy(src, dst, w_sem.at[3 * at + i])
                    pl.when((place ^ chip) == m)(copy.start)
                waits[at].append(copy)
            features = pl.ds(pl.multiple_of((core ^ h) * half, 128), half)
            for s, rows in ((0, mine), (1, theirs)):
                copy = pltpu.make_async_copy(
                    xs[2 * r + s].at[:, features],
                    x_buf.at[at, pl.ds(rows, tok)],
                    x_sem.at[2 * at + s],
                )
                copy.start()
                waits[at].append(copy)
    acc = 0.0
    for at in range(8):
        for copy in waits[at]:
            copy.wait()
        acc = acc + jnp.dot(x_buf[at], w_buf[at], preferred_element_type=jnp.float32)
    factor = factor_ref[...]
    heads = q_ref.shape[0]
    for h in range(heads + 2):
        v = acc[:, h * HD : (h + 1) * HD] * factor
        if h <= heads:
            v = rotated(v, cos_ref[...], sin_ref[...])
        if h < heads:
            q_ref[h] = (v * scale).astype(jnp.bfloat16)
        else:
            kv_ref[h - heads] = v.astype(jnp.bfloat16)


def project(ids, xs, weights, at_kv, factor, cosine, sinus, scale):
    tok, feat = xs[0].shape
    cols = weights[0].shape[1]
    half = feat // 2
    return pl.pallas_call(
        functools.partial(project_kernel, scale, at_kv),
        out_shape=(
            jax.ShapeDtypeStruct((cols // HD, 2 * tok, HD), jnp.bfloat16),
            jax.ShapeDtypeStruct((2, 2 * tok, HD), jnp.bfloat16),
        ),
        in_specs=[SMEM] + [HBM] * 16 + [VMEM] * 3,
        out_specs=(VMEM, VMEM),
        scratch_shapes=[
            pltpu.VMEM((8, 2 * tok, half), jnp.bfloat16),
            pltpu.VMEM((8, half, cols + 2 * HD), jnp.bfloat16),
            pltpu.SemaphoreType.DMA((16,)),
            pltpu.SemaphoreType.DMA((24,)),
        ],
        compiler_params=pltpu.CompilerParams(vmem_limit_bytes=GRANT),
        cost_estimate=LITTLE,
        name="project",
    )(ids, *xs, *weights, factor, cosine, sinus)


BT = 256
BK = 512
UNROLL = 2
CHAIN = 2


def scores(q, k):
    return lax.dot_general(q, k, (((1,), (1,)), ((), ())), preferred_element_type=jnp.float32)


def absorb(s, v_ext, m, acc):
    new = jnp.maximum(m, jnp.max(s, axis=1, keepdims=True))
    p = jnp.exp2(s - new).astype(jnp.bfloat16)
    acc = acc * jnp.exp2(m - new) + jnp.dot(p, v_ext, preferred_element_type=jnp.float32)
    return new, acc


def prefix_kernel(bound_ref, q_ref, n_ref, kv_ref, *refs):
    m_out, acc_out, v_ext, s_ref, m_ref, acc_ref = refs[-6:]
    b = pl.program_id(0)
    heads, bt = q_ref.shape[0], q_ref.shape[1]
    rows, chains = CHAIN * bt, heads // CHAIN
    big = UNROLL * BK
    last = kv_ref.shape[1] // big - 1

    @pl.when(b == 0)
    def _():
        v_ext[:, :HD] = kv_ref[1]
        v_ext[:, HD:] = jnp.ones_like(kv_ref[1])

    m_ref[...] = jnp.full_like(m_ref, MASKED)
    acc_ref[...] = jnp.zeros_like(acc_ref)
    n_rows = jnp.concatenate([n_ref[:, :1]] * CHAIN, axis=0)

    def query(g):
        return q_ref[g * CHAIN : (g + 1) * CHAIN].reshape(rows, HD)

    s_ref[...] = scores(query(0), kv_ref[0, :BK, :])
    items = [(u, g) for u in range(UNROLL) for g in range(chains)]

    def body(kb, masked):
        start = pl.multiple_of(kb * big, big)
        follow = pl.multiple_of(jnp.minimum(kb + 1, last) * big, big)
        ms = [m_ref[g][:, :1] for g in range(chains)]
        accs = [acc_ref[g] for g in range(chains)]
        s = s_ref[...]
        for t, (u, g) in enumerate(items):
            if t + 1 < len(items):
                at, who = start + items[t + 1][0] * BK, items[t + 1][1]
            else:
                at, who = follow, 0
            ahead = scores(query(who), kv_ref[0, pl.ds(at, BK), :])
            if masked:
                col = lax.broadcasted_iota(jnp.int32, s.shape, 1) + (start + u * BK)
                s = jnp.where(col < n_rows, s, MASKED)
            v = v_ext[pl.ds(start + u * BK, BK), :]
            ms[g], accs[g] = absorb(s, v, ms[g], accs[g])
            s = ahead
        s_ref[...] = s
        for g in range(chains):
            m_ref[g] = jnp.broadcast_to(ms[g], (rows, 128))
            acc_ref[g] = accs[g]

    full = bound_ref[0, b] // big
    some = (bound_ref[1, b] + big - 1) // big
    lax.fori_loop(0, full, lambda kb, c: (body(kb, False), c)[1], 0)
    lax.fori_loop(full, some, lambda kb, c: (body(kb, True), c)[1], 0)
    m_out[0] = m_ref[...]
    acc_out[0] = acc_ref[...]


def attend_prefix(bounds, q, group, n_tok, kv, arrived=()):
    heads, tokens = CHAIN, q.shape[1]
    blocks = tokens // BT
    chains, rows = heads // CHAIN, CHAIN * BT
    keys = kv.shape[1]
    return pl.pallas_call(
        prefix_kernel,
        out_shape=(
            jax.ShapeDtypeStruct((blocks, chains, rows, 128), jnp.float32),
            jax.ShapeDtypeStruct((blocks, chains, rows, 2 * HD), jnp.float32),
        ),
        grid_spec=pltpu.PrefetchScalarGridSpec(
            num_scalar_prefetch=1,
            grid=(blocks,),
            in_specs=[
                pl.BlockSpec((heads, BT, HD), lambda b, *_: (group, b, 0)),
                pl.BlockSpec((BT, 128), lambda b, *_: (b, 0)),
                pl.BlockSpec((2, keys, HD), lambda b, *_: (0, 0, 0)),
            ]
            + specs_of(arrived),
            out_specs=(
                pl.BlockSpec((1, chains, rows, 128), lambda b, *_: (b, 0, 0, 0)),
                pl.BlockSpec((1, chains, rows, 2 * HD), lambda b, *_: (b, 0, 0, 0)),
            ),
            scratch_shapes=[
                pltpu.VMEM((keys, 2 * HD), jnp.bfloat16),
                pltpu.VMEM((rows, BK), jnp.float32),
                pltpu.VMEM((chains, rows, 128), jnp.float32),
                pltpu.VMEM((chains, rows, 2 * HD), jnp.float32),
            ],
        ),
        compiler_params=pltpu.CompilerParams(vmem_limit_bytes=GRANT),
        cost_estimate=LITTLE,
        name="attend_prefix",
    )(bounds, q, n_tok, kv, *arrived)


def new_kernel(halo, q_ref, lo_ref, k_ref, v_ref, *refs):
    states, out_ref = refs[:-1], refs[-1]
    b = pl.program_id(0)
    heads, bt = q_ref.shape[0], q_ref.shape[1]
    rows = CHAIN * bt
    span = halo + bt
    start = pl.multiple_of(b * bt, bt)
    k = k_ref[pl.ds(start, span), :]
    v = v_ref[pl.ds(start, span), :]
    v_ext = jnp.concatenate([v, jnp.ones_like(v)], axis=1)
    lo = jnp.concatenate([lo_ref[:, :1]] * CHAIN, axis=0)

    def hide(s):
        col = lax.broadcasted_iota(jnp.int32, s.shape, 1)
        row = lax.broadcasted_iota(jnp.int32, s.shape, 0) % bt
        return jnp.where((col + start >= lo) & (col <= row + halo), s, MASKED)

    for g in range(heads // CHAIN):
        q = q_ref[g * CHAIN : (g + 1) * CHAIN].reshape(rows, HD)
        _, acc = absorb(
            hide(scores(q, k)), v_ext, states[2 * g][0, 0][:, :1], states[2 * g + 1][0, 0]
        )
        mixed = (acc[:, :HD] / acc[:, HD:]).astype(jnp.bfloat16)
        for h in range(CHAIN):
            at = (g * CHAIN + h) * HD
            out_ref[:, at : at + HD] = mixed[h * bt : (h + 1) * bt]


def attend_new(q, lo_tok, k, v, states):
    heads, tokens, _ = q.shape
    blocks = tokens // BT
    chains, rows = heads // CHAIN, CHAIN * BT
    halo = k.shape[0] - tokens
    whole = lambda b: (0, 0)
    return pl.pallas_call(
        functools.partial(new_kernel, halo),
        out_shape=jax.ShapeDtypeStruct((tokens, heads * HD), jnp.bfloat16),
        grid=(blocks,),
        in_specs=[
            pl.BlockSpec((heads, BT, HD), lambda b: (0, b, 0)),
            pl.BlockSpec((BT, 128), lambda b: (b, 0)),
            pl.BlockSpec(k.shape, whole),
            pl.BlockSpec(v.shape, whole),
        ]
        + [
            pl.BlockSpec((1, 1, rows, 128), lambda b: (b, 0, 0, 0)),
            pl.BlockSpec((1, 1, rows, 2 * HD), lambda b: (b, 0, 0, 0)),
        ]
        * chains,
        out_specs=pl.BlockSpec((BT, heads * HD), lambda b: (b, 0)),
        compiler_params=pltpu.CompilerParams(vmem_limit_bytes=GRANT),
        cost_estimate=LITTLE,
        name="attend_new",
    )(q, lo_tok, k, v, *states)


def out_kernel(ids_ref, *refs):
    xs, ws = refs[:8], refs[8:13]
    out_ref, x_buf, w_buf, x_sem, w_sem = refs[13:]
    chip, core, z = ids_ref[0], ids_ref[1], ids_ref[2]
    width = xs[0].shape[1]
    rows = w_buf.shape[1] // 4
    top = ws[3].shape[0]
    for r in range(4):
        near = ids_ref[3 + r] ^ z
        for m in range(4):
            to = w_buf.at[r, pl.ds(pl.multiple_of((chip ^ m) * rows, 128), rows)]
            sem = w_sem.at[4 * r + m]
            if m < 3:
                src = ws[m].at[pl.ds(pl.multiple_of(near * rows, 128), rows)]
                pltpu.make_async_copy(src, to, sem).start()
            else:

                @pl.when(near < 2)
                def _():
                    src = ws[3].at[pl.ds(pl.multiple_of(near * rows, 128), rows)]
                    pltpu.make_async_copy(src, to, sem).start()

                @pl.when(near >= 2)
                def _():
                    src = ws[4].at[pl.ds(pl.multiple_of(near * rows - top, 128), rows)]
                    pltpu.make_async_copy(src, to, sem).start()

        for s in range(2):
            at = pl.multiple_of((core ^ s) * width, 128)
            pltpu.make_async_copy(
                xs[2 * r + s], x_buf.at[r, :, pl.ds(at, width)], x_sem.at[2 * r + s]
            ).start()
    acc = None
    for r in range(4):
        for m in range(4):
            pltpu.make_async_copy(
                ws[0].at[pl.ds(0, rows)], w_buf.at[r, pl.ds(0, rows)], w_sem.at[4 * r + m]
            ).wait()
        for s in range(2):
            pltpu.make_async_copy(
                xs[0], x_buf.at[r, :, pl.ds(0, width)], x_sem.at[2 * r + s]
            ).wait()
        term = jnp.dot(x_buf[r], w_buf[r], preferred_element_type=jnp.float32)
        acc = term if acc is None else acc + term
    out_ref[...] = acc.astype(jnp.bfloat16)


def out_project(ids, xs, ws):
    tokens, width = xs[0].shape
    depth, cols = ws[0].shape
    return pl.pallas_call(
        out_kernel,
        out_shape=jax.ShapeDtypeStruct((tokens, cols), jnp.bfloat16),
        in_specs=[SMEM] + [HBM] * 13,
        out_specs=VMEM,
        scratch_shapes=[
            pltpu.VMEM((4, tokens, 2 * width), jnp.bfloat16),
            pltpu.VMEM((4, depth, cols), jnp.bfloat16),
            pltpu.SemaphoreType.DMA((8,)),
            pltpu.SemaphoreType.DMA((16,)),
        ],
        compiler_params=pltpu.CompilerParams(vmem_limit_bytes=GRANT),
        cost_estimate=LITTLE,
        name="out_project",
    )(ids, *xs, *ws)


def per_device(
    stream,
    pending,
    norm_gain,
    w_query,
    w_key,
    w_value,
    w_out,
    prefix_keys,
    prefix_values,
    prefix_segments,
    stretch_segments,
    stretch_offset,
):
    tok, feat = stream.shape
    chip_tok = 2 * tok
    c = lax.axis_index("ctx")
    z = lax.axis_index("tp")
    chip, core = c // 2, c % 2
    first = core == 0
    depth = feat * N_TP

    wide = stream.astype(jnp.float32)
    here = jnp.stack([chip, core, z]).astype(jnp.int32)
    every = (0, 1, 2)

    gain = lax.dynamic_slice_in_dim(norm_gain, z * feat, feat, 0).astype(jnp.float32)
    scaled = (wide * gain[None, :]).astype(jnp.bfloat16)
    u1, d1 = hop_up(scaled, every), hop_down(scaled, every)

    labels = jnp.arange(NTRAJ, dtype=jnp.int32)
    counts = jnp.concatenate(
        [
            jnp.sum((prefix_segments[:, None] <= labels).astype(jnp.int32), axis=0),
            jnp.sum((stretch_segments[:, None] < labels).astype(jnp.int32), axis=0),
        ]
    )
    notes = jnp.concatenate([counts // 32, counts % 32])
    cols = w_query.shape[1] // 2
    notes = jnp.stack(
        [jnp.pad(v, (0, cols - v.shape[0])) for v in (stretch_segments, notes)]
        + [jnp.zeros((cols,), jnp.int32)] * 14
    ).astype(jnp.bfloat16)

    token_index = chip * chip_tok + jnp.arange(chip_tok, dtype=jnp.int32)
    positions = stretch_offset[0].astype(jnp.float32) + token_index.astype(jnp.float32)
    angles = positions[:, None] * inverse_freqs(HD)
    cosine, sinus = jnp.cos(angles), jnp.sin(angles)
    cosine = jnp.concatenate([cosine, cosine], axis=1)
    sinus = jnp.concatenate([-sinus, sinus], axis=1)

    def squares(part, place):
        g = lax.dynamic_slice_in_dim(norm_gain, place * feat, feat, 0).astype(jnp.float32)
        return jnp.sum(jnp.square(part.astype(jnp.float32) / g[None, :]), axis=1, keepdims=True)

    q_heads = w_query.shape[1] // HD // 2
    q_cols = q_heads * HD
    n_q = w_query.shape[0]
    fold = prefix_keys.shape[1] // 2
    n_both = n_q + fold
    n_kv = w_key.shape[0] // 2
    n_piece = w_out.shape[0] // 4

    def first_plan(at, src, out):
        w_q, w_k, w_v, keys, values, said = src
        for dst, j in ((out[0], at[1]), (out[1], 1 - at[1])):
            head = 2 * at[2] + j
            yield one(w_q.at[:, pl.ds(multiple(j, q_cols), q_cols)], dst.at[pl.ds(0, n_q)])
            for i, a in enumerate((keys, keys, values, values)):
                part = a.at[head, pl.ds((i % 2) * fold, fold)]
                yield one(part, dst.at[pl.ds(n_q, fold), pl.ds(i * HD, HD)])
            for i, a in enumerate((w_k, w_v, w_k, w_v)):
                part = a.at[pl.ds((i // 2) * n_kv, n_kv), pl.ds(multiple(head), HD)]
                yield one(part, dst.at[pl.ds(n_both, n_kv), pl.ds(i * HD, HD)])
            yield one(said, dst.at[pl.ds(n_both + n_kv, said.shape[0])])

    own, give = move(
        first_plan,
        ((n_both + n_kv + notes.shape[0], q_cols),) * 2,
        here,
        (w_query, w_key, w_value, prefix_keys, prefix_values, notes),
    )
    places = jnp.stack(
        [z, jnp.where(z < 2, z + 1, z - 1), jnp.where(z < 2, z + 2, z - 2), jnp.where(z % 2 == 1, 0, 3)]
    ).astype(jnp.int32)
    ids = jnp.concatenate([here, places])

    x1, y1, given = swap(own, 2), swap(own, 4), swap(give, 1)
    mine = squares(scaled, z)
    near = pick(z, (d1, d1, u1, u1), here, (cosine, sinus, mine))
    over1 = swap(near, 1)

    up, down = hops(here, pending, u1, d1, 3, (1, 2, 3), (), (x1, y1, given, over1))
    u2, d2 = hop_up(up, every), hop_down(down, every)

    given = gate(given, u1, d1, x1, y1, over1)
    x2, y2, over0 = swap(given, 2), swap(given, 4), swap(gate(scaled, given), 1)
    mine = mine + squares(near, places[1])
    theirs = squares(over1, places[1])
    second = pick(z, (d2, d2, u2, u2), here, (over0, mine, theirs))

    up, down = hops(here, pending, u2, d2, 2, (2,), (1,), (x2, y2, over0, second))
    u3, d3 = hop_up(up, every), hop_down(down, every)

    x1, y2 = gate(x1, u2, d2, x2, over0, second), gate(y2, u2, d2, x2, over0, second)
    far_own, far_other = swap(x1, 4), swap(y2, 2)
    over2 = swap(second, 1)
    mine = mine + squares(second, places[2])
    theirs = theirs + squares(over0, z)
    up, down = hops(here, pending, u3, d3, 1, (), (1, 2, 3), (over2,))
    u4, d4 = hop_up(up, every), hop_down(down, every)
    third = pick(z, (d3, u1, d1, u3), here, (up, mine, theirs))
    over3 = swap(third, 1)

    mine = mine + squares(third, places[3])
    theirs = theirs + squares(over2, places[2]) + squares(over3, places[3])
    total = jnp.where(first, jnp.concatenate([mine, theirs]), jnp.concatenate([theirs, mine]))
    factor = lax.rsqrt(total * (1.0 / depth) + NORM_EPSILON)
    factor = jnp.broadcast_to(factor, (chip_tok, 128))
    xs = [scaled, over0, near, over1, second, over2, third, over3]
    own_rows = (own, given, x1, x2, y1, y2, far_own, far_other)

    said = [rows[n_both + n_kv : n_both + n_kv + 2].astype(jnp.float32) for rows in own_rows]
    total = sum(v[1, : 4 * NTRAJ] for v in said).astype(jnp.int32)
    total = total[: 2 * NTRAJ] * 32 + total[2 * NTRAJ :]
    segs = [v[0, :tok].astype(jnp.int32) for v in said[:2]]
    segs = jnp.where(first, jnp.concatenate(segs), jnp.concatenate(segs[::-1]))
    onehot = (segs[:, None] == labels).astype(jnp.int32)
    n_tok = jnp.sum(onehot * total[:NTRAJ], axis=1)
    lo_tok = jnp.sum(onehot * total[NTRAJ:], axis=1) - chip * chip_tok + tok
    blocked = n_tok.reshape(chip_tok // BT, BT)
    bounds = jnp.stack([blocked[:, 0], blocked[:, -1]])
    n_wide = jnp.broadcast_to(n_tok[:, None], (chip_tok, 128))
    lo_wide = jnp.broadcast_to(lo_tok[:, None], (chip_tok, 128))

    def prefix_plan(at, src, out):
        for m in range(4):
            for j in range(2):
                start = ((at[0] ^ m) * 2 + (at[1] ^ j)) * 2 * fold
                rows = src[2 * m + j]
                for i in range(4):
                    dst = out[0].at[i // 2, pl.ds(pl.multiple_of(start + (i % 2) * fold, 128), fold)]
                    yield one(rows.at[pl.ds(n_q, fold), pl.ds(i * HD, HD)], dst)

    (kv,) = move(prefix_plan, ((2, N_CTX * 2 * fold, HD),), here, own_rows, (third,))

    def piece_plan(at, src, out):
        for r, dst in enumerate(out):
            rows = pl.ds(multiple(at[0] ^ r, n_piece), n_piece)
            for i in range(2):
                part = src[0].at[rows, pl.ds(i * q_cols, q_cols)]
                yield one(part, dst.at[pl.ds(i * n_piece, n_piece)])

    by_chip = move(
        piece_plan, ((2 * n_piece, q_cols),) * 4, here, (w_out,), (far_own, far_other, third, kv)
    )
    by_chip = (by_chip[0],) + tuple(swap(by_chip[r], 2 * r) for r in (1, 2, 3))

    scale = math.log2(math.e) / math.sqrt(HD)
    q, kv_new = project(ids, xs, own_rows, n_both, factor, cosine, sinus, scale)
    before = lax.ppermute(kv_new[:, tok:], "ctx", [(i, i + 2) for i in range(N_CTX - 2)])

    def pieces_plan(at, src, out):
        for r, dst in enumerate(out):
            near = (at[2] ^ r) ^ at[0]
            yield ([(near == m, src[m]) for m in range(4)], dst)

    pieces = list(move(pieces_plan, ((2 * n_piece, q_cols),) * 4, here, by_chip, (q,)))
    for r in (1, 2, 3):
        pieces[r] = lax.ppermute(pieces[r], "tp", [(i, i ^ r) for i in range(N_TP)])
    part_a = attend_prefix(bounds, q, 0, n_wide, kv, (pieces[0],))
    part_b = attend_prefix(bounds, q, 1, n_wide, kv, (part_a[0], before, u4, d4))
    k_near = jnp.concatenate([before[0], kv_new[0]], axis=0)
    v_near = jnp.concatenate([before[1], kv_new[1]], axis=0)
    attended = attend_new(q, lo_wide, k_near, v_near, part_a + part_b)

    def block_plan(at, src, out):
        for r, part in enumerate(src):
            for i in range(2):
                dst = out[0].at[pl.ds(r * n_piece, n_piece), pl.ds(i * q_cols, q_cols)]
                yield one(part.at[pl.ds(i * n_piece, n_piece)], dst)

    (block,) = move(block_plan, ((4 * n_piece, 2 * q_cols),), here, pieces, (part_b[0],))
    half = block.shape[0] // 2
    wo_x, wo_y = swap(block, 2), swap(block, 4)
    u1, d1 = hop_up(attended, every), hop_down(attended, every)
    near = pick(z, (d1, d1, u1, u1), here, (wo_x, wo_y))

    def far_plan(at, src, out):
        yield one(src[0].at[pl.ds(0, half)], out[0])
        yield one(src[1].at[pl.ds(half, half)], out[1])

    to_y, to_x = move(
        far_plan, ((half, block.shape[1]),) * 2, here, (wo_x, wo_y), (near,)
    )
    wo_parts = (block, wo_x, wo_y, swap(to_y, 4), swap(to_x, 2))
    u2, d2 = hop_up(gate(u1, near), (1, 2)), hop_down(gate(d1, near), (1, 2))
    second = pick(z, (d2, d2, u2, u2), here)
    u3, d3 = hop_up(gate(u2, *wo_parts[3:]), (2,)), hop_down(gate(d2, *wo_parts[3:]), (2,))
    third = pick(z, (d3, u1, d1, u3), here)
    hs = []
    for part in (attended, near, second, third):
        hs += [part, swap(part, 1)]
    projected = out_project(ids, hs, wo_parts)
    mine = lax.dynamic_slice_in_dim(projected, core * tok, tok, 0)
    theirs = swap(lax.dynamic_slice_in_dim(projected, (1 - core) * tok, tok, 0), 1)
    head_share = jnp.where(
        first,
        jnp.concatenate([mine, theirs], axis=1),
        jnp.concatenate([theirs, mine], axis=1),
    ).astype(jnp.float32)
    pending_share = (
        lax.dynamic_slice_in_dim(pending[0], z * feat, feat, 1).astype(jnp.float32)
        + jnp.where(z == 0, 0, u4).astype(jnp.float32)
        + jnp.where(z == 3, 0, d4).astype(jnp.float32)
    )
    return (wide + (head_share + pending_share)).astype(jnp.bfloat16)


def solution(mesh):
    in_specs = (
        P("ctx", "tp"),
        P("tp", "ctx", None),
        P(),
        P("ctx", "tp"),
        P("ctx", None),
        P("ctx", None),
        P("tp", "ctx"),
        P(None, "ctx", None),
        P(None, "ctx", None),
        P("ctx"),
        P("ctx"),
        P(),
    )
    out_specs = P("ctx", "tp")
    small = mesh.shape["ctx"] == N_CTX and mesh.shape["tp"] == N_TP
    return jax.shard_map(
        per_device if small else per_device_any,
        mesh=mesh,
        in_specs=in_specs,
        out_specs=out_specs,
        check_vma=False,
    )
```

profile of v0, /device:TPU:0, one launch (start us, length us, event | category | flops | bytes accessed | tf_op | source)
XLA Modules:
  0.0 424.3 jit_solution(14312364069234813271)
XLA Ops:
  5.1 5.0 %collective-permute-start.1 = (bf16[384,2048]{1,0:T(8,128)(2,1)}, bf16[384,2048]{1,0:T(8,128)(2,1)S(1)}, u32[]{:S(2)}, u32[]{:S(2)}) collective-permute-start(bf16[384,2048]{1,0:T(8,128)(2,1)} %get-tuple-element.66.refs_0_), channel_id=1, source_target_pairs={{0,1},{1,2},{2,3},{4,5},{5,6},{6,7},{8,9},{9,10},{10,11},{12,13},{... | collective-permute-start | bytes 4718600 | tf_op jit(solution)/shard_map/ppermute | solution.py:179
  13.8 5.0 %first_plan.1 = (bf16[1936,512]{1,0:T(8,128)(2,1)}, bf16[1936,512]{1,0:T(8,128)(2,1)}) custom-call(s32[3]{0:T(128)} %pad_add_fusion.1.ids_ref, bf16[1024,1024]{1,0:T(8,128)(2,1)} %refs_0_.2, bf16[1024,1024]{1,0:T(8,128)(2,1)} %refs_1_.1, bf16[1024,1024]{1,0:T(8,128)(2,1)} %refs_2_.1, bf16[8,768,128]{2,1,0:T(8,128)(2,1)} %refs_3_.1, ...), custom_call_target="tpu_custom_call" | custom-call | bytes 1024 | tf_op jit(solution)/shard_map/first_plan/pallas_call | solution.py:218
  29.7 14.3 %collective-permute-done.1.refs_1_.up_ref = bf16[384,2048]{1,0:T(8,128)(2,1)S(1)} collective-permute-done((bf16[384,2048]{1,0:T(8,128)(2,1)}, bf16[384,2048]{1,0:T(8,128)(2,1)S(1)}, u32[]{:S(2)}, u32[]{:S(2)}) %collective-permute-start.1) | collective-permute-done | bytes 1572896 | tf_op jit(solution)/shard_map/ppermute | solution.py:179
  54.7 9.1 %collective-permute-done.3.refs_3_.refs_0_ = bf16[1936,512]{1,0:T(8,128)(2,1)} collective-permute-done((bf16[1936,512]{1,0:T(8,128)(2,1)}, bf16[1936,512]{1,0:T(8,128)(2,1)}, u32[]{:S(2)}, u32[]{:S(2)}) %collective-permute-start.3) | collective-permute-done | bytes 1982496 | tf_op jit(solution)/shard_map/ppermute | solution.py:175
  73.2 6.0 %collective-permute-start.8 = (bf16[384,2048]{1,0:T(8,128)(2,1)}, bf16[384,2048]{1,0:T(8,128)(2,1)}, u32[]{:S(2)}, u32[]{:S(2)}) collective-permute-start(bf16[384,2048]{1,0:T(8,128)(2,1)} %get-tuple-element.32), channel_id=1, source_target_pairs={{0,1},{1,2},{2,3},{4,5},{5,6},{6,7},{8,9},{9,10},{10,11},{12,13},{... | collective-permute-start | bytes 4718600 | tf_op jit(solution)/shard_map/ppermute | solution.py:179
  90.1 21.3 %collective-permute-done.7.refs_0_.down_ref.refs_2_ = bf16[384,2048]{1,0:T(8,128)(2,1)} collective-permute-done((bf16[384,2048]{1,0:T(8,128)(2,1)}, bf16[384,2048]{1,0:T(8,128)(2,1)}, u32[]{:S(2)}, u32[]{:S(2)}) %collective-permute-start.7) | collective-permute-done | bytes 1572896 | tf_op jit(solution)/shard_map/ppermute | solution.py:183
  116.3 8.2 %collective-permute-done.10.refs_0_.refs_3_.refs_11_ = bf16[1936,512]{1,0:T(8,128)(2,1)} collective-permute-done((bf16[1936,512]{1,0:T(8,128)(2,1)S(1)}, bf16[1936,512]{1,0:T(8,128)(2,1)}, u32[]{:S(2)}, u32[]{:S(2)}) %collective-permute-start.10) | collective-permute-done | bytes 1982496 | tf_op jit(solution)/shard_map/ppermute | solution.py:175
  130.4 5.7 %collective-permute-start.13 = (bf16[384,2048]{1,0:T(8,128)(2,1)}, bf16[384,2048]{1,0:T(8,128)(2,1)}, u32[]{:S(2)}, u32[]{:S(2)}) collective-permute-start(bf16[384,2048]{1,0:T(8,128)(2,1)} %get-tuple-element.34), channel_id=1, source_target_pairs={{0,1},{1,2},{2,3},{4,5},{5,6},{6,7},{8,9},{9,10},{10,11},{12,13},{... | collective-permute-start | bytes 4718600 | tf_op jit(solution)/shard_map/ppermute | solution.py:179
  144.7 21.9 %collective-permute-done.12.down_ref.refs_0_ = bf16[384,2048]{1,0:T(8,128)(2,1)} collective-permute-done((bf16[384,2048]{1,0:T(8,128)(2,1)}, bf16[384,2048]{1,0:T(8,128)(2,1)}, u32[]{:S(2)}, u32[]{:S(2)}) %collective-permute-start.12) | collective-permute-done | bytes 1572896 | tf_op jit(solution)/shard_map/ppermute | solution.py:183
  167.8 4.9 %hops.5 = (bf16[384,2048]{1,0:T(8,128)(2,1)}, bf16[384,2048]{1,0:T(8,128)(2,1)}) custom-call(s32[3]{0:T(128)} %pad_add_fusion.1.ids_ref, bf16[1,384,8192]{2,1,0:T(8,128)(2,1)} %pending_ref.5, bf16[384,2048]{1,0:T(8,128)(2,1)} %collective-permute-done.13.up_ref.refs_3_, bf16[384,2048]{1,0:T(8,128)(2,1)} %collective-permute-done.12.down_ref.refs_0_, ...), custom_call_target="tpu_custom_call" | custom-call | bytes 1024 | tf_op jit(solution)/shard_map/hops/pallas_call | solution.py:286
  177.7 5.1 %collective-permute-start.21 = (bf16[384,2048]{1,0:T(8,128)(2,1)}, bf16[384,2048]{1,0:T(8,128)(2,1)S(1)}, u32[]{:S(2)}, u32[]{:S(2)}) collective-permute-start(bf16[384,2048]{1,0:T(8,128)(2,1)} %get-tuple-element.35.refs_4_), channel_id=1, source_target_pairs={{0,1},{1,2},{2,3},{4,5},{5,6},{6,7},{8,9},{9,10},{10,11},{12,13},{... | collective-permute-start | bytes 4718600 | tf_op jit(solution)/shard_map/ppermute | solution.py:179
  184.3 4.7 %prefix_plan.1.refs_4_.kv_ref = bf16[2,6144,128]{2,1,0:T(8,128)(2,1)} custom-call(s32[3]{0:T(128)} %pad_add_fusion.1.ids_ref, bf16[1936,512]{1,0:T(8,128)(2,1)} %get-tuple-element.30.refs_8_.refs_0_, bf16[1936,512]{1,0:T(8,128)(2,1)} %gate.8.refs_1_.refs_9_, bf16[1936,512]{1,0:T(8,128)(2,1)} %gate.10.refs_10_.refs_2_, ...), custom_call_target="tpu_custom_call" | custom-call | bytes 1024 | tf_op jit(solution)/shard_map/prefix_plan/pallas_call | solution.py:218
  200.7 23.5 %project.1 = (bf16[4,768,128]{2,1,0:T(8,128)(2,1)}, bf16[2,768,128]{2,1,0:T(8,128)(2,1)}) custom-call(s32[7]{0:T(128)} %concatenate.59.ids_ref, bf16[384,2048]{1,0:T(8,128)(2,1)} %get-tuple-element.66.refs_0_, bf16[384,2048]{1,0:T(8,128)(2,1)} %copy-done, bf16[384,2048]{1,0:T(8,128)(2,1)} %pick_plan.6.refs_2_, bf16[384,2048]{1,0:T(8,128)(2,1)} %copy-done.7, ...), custom_call_target="tpu_custom_call" | custom-call | bytes 1024 | tf_op jit(solution)/shard_map/project/pallas_call | solution.py:365
  242.1 12.8 %attend_prefix.2 = (f32[3,1,512,128]{3,2,1,0:T(8,128)}, f32[3,1,512,256]{3,2,1,0:T(8,128)}) custom-call(s32[2,3]{1,0:T(2,128)} %pad_add_fusion.bound_ref, bf16[4,768,128]{2,1,0:T(8,128)(2,1)} %get-tuple-element.36.refs_4_.q_ref, s32[768,128]{1,0:T(8,128)} %broadcast_in_dim.18.n_ref, bf16[2,6144,128]{2,1,0:T(8,128)(2,1)} %prefix_plan.1.refs_4_.kv_ref, ...), custom_call_target="tpu_custom_call" | custom-call | bytes 1024 | tf_op jit(solution)/shard_map/attend_prefix/pallas_call | solution.py:461
  255.6 12.8 %attend_prefix.3 = (f32[3,1,512,128]{3,2,1,0:T(8,128)}, f32[3,1,512,256]{3,2,1,0:T(8,128)}) custom-call(s32[2,3]{1,0:T(2,128)} %pad_add_fusion.bound_ref, bf16[4,768,128]{2,1,0:T(8,128)(2,1)} %get-tuple-element.36.refs_4_.q_ref, s32[768,128]{1,0:T(8,128)} %broadcast_in_dim.18.n_ref, bf16[2,6144,128]{2,1,0:T(8,128)(2,1)} %prefix_plan.1.refs_4_.kv_ref, ...), custom_call_target="tpu_custom_call" | custom-call | bytes 1024 | tf_op jit(solution)/shard_map/attend_prefix/pallas_call | solution.py:461
  277.2 7.5 %collective-permute-start.29 = (bf16[1024,1024]{1,0:T(8,128)(2,1)}, bf16[1024,1024]{1,0:T(8,128)(2,1)S(1)}, u32[]{:S(2)}, u32[]{:S(2)}) collective-permute-start(bf16[1024,1024]{1,0:T(8,128)(2,1)} %block_plan.1.refs_8_), channel_id=1, source_target_pairs={{0,8},{4,12},{8,0},{12,4},{16,24},{20,28},{24,16},{28,20},{1,9},{5... | collective-permute-start | bytes 6291464 | tf_op jit(solution)/shard_map/ppermute | solution.py:175
  284.7 11.0 %collective-permute-start.30 = (bf16[1024,1024]{1,0:T(8,128)(2,1)}, bf16[1024,1024]{1,0:T(8,128)(2,1)}, u32[]{:S(2)}, u32[]{:S(2)}) collective-permute-start(bf16[1024,1024]{1,0:T(8,128)(2,1)} %block_plan.1.refs_8_), channel_id=1, source_target_pairs={{0,16},{4,20},{8,24},{12,28},{16,0},{20,4},{24,8},{28,12},{1,17},{... | collective-permute-start | bytes 6291464 | tf_op jit(solution)/shard_map/ppermute | solution.py:175
  298.2 6.8 %attend_new.1.refs_0_ = bf16[768,512]{1,0:T(8,128)(2,1)} custom-call(bf16[4,768,128]{2,1,0:T(8,128)(2,1)} %get-tuple-element.36.refs_4_.q_ref, s32[768,128]{1,0:T(8,128)} %broadcast_in_dim.17.lo_ref, bf16[1152,128]{1,0:T(8,128)(2,1)} %pad_maximum_fusion.2.k_ref, bf16[1152,128]{1,0:T(8,128)(2,1)} %pad_maximum_fusion.3.v_ref, ...), custom_call_target="tpu_custom_call" | custom-call | bytes 1024 | tf_op jit(solution)/shard_map/attend_new/pallas_call | solution.py:527
  310.9 13.6 %collective-permute-done.24.refs_0_.refs_2_ = bf16[768,512]{1,0:T(8,128)(2,1)S(1)} collective-permute-done((bf16[768,512]{1,0:T(8,128)(2,1)}, bf16[768,512]{1,0:T(8,128)(2,1)S(1)}, u32[]{:S(2)}, u32[]{:S(2)}) %collective-permute-start.24) | collective-permute-done | bytes 786464 | tf_op jit(solution)/shard_map/ppermute | solution.py:183
  328.9 11.2 %collective-permute-done.30.refs_3_.refs_1_.refs_10_ = bf16[1024,1024]{1,0:T(8,128)(2,1)} collective-permute-done((bf16[1024,1024]{1,0:T(8,128)(2,1)}, bf16[1024,1024]{1,0:T(8,128)(2,1)}, u32[]{:S(2)}, u32[]{:S(2)}) %collective-permute-start.30) | collective-permute-done | bytes 2097184 | tf_op jit(solution)/shard_map/ppermute | solution.py:175
  355.3 15.8 %collective-permute-done.32.refs_0_ = bf16[768,512]{1,0:T(8,128)(2,1)S(1)} collective-permute-done((bf16[768,512]{1,0:T(8,128)(2,1)}, bf16[768,512]{1,0:T(8,128)(2,1)S(1)}, u32[]{:S(2)}, u32[]{:S(2)}) %collective-permute-start.32) | collective-permute-done | bytes 786464 | tf_op jit(solution)/shard_map/ppermute | solution.py:183
  381.1 14.1 %collective-permute-done.37.refs_0_ = bf16[768,512]{1,0:T(8,128)(2,1)} collective-permute-done((bf16[768,512]{1,0:T(8,128)(2,1)}, bf16[768,512]{1,0:T(8,128)(2,1)}, u32[]{:S(2)}, u32[]{:S(2)}) %collective-permute-start.37) | collective-permute-done | bytes 786464 | tf_op jit(solution)/shard_map/ppermute | solution.py:183
  400.9 12.8 %out_project.1 = bf16[768,1024]{1,0:T(8,128)(2,1)} custom-call(s32[7]{0:T(128)} %concatenate.59.ids_ref, bf16[768,512]{1,0:T(8,128)(2,1)} %attend_new.1.refs_0_, bf16[768,512]{1,0:T(8,128)(2,1)} %copy-done.24, bf16[768,512]{1,0:T(8,128)(2,1)} %pick_plan.9.refs_1_.refs_2_, bf16[768,512]{1,0:T(8,128)(2,1)} %collective-permute-done.31.refs_3_, ...), custom_call_target="tpu_custom_call" | custom-call | bytes 1024 | tf_op jit(solution)/shard_map/out_project/pallas_call | solution.py:599
  419.2 4.7 %fusion.1 = bf16[384,2048]{1,0:T(8,128)(2,1)} fusion(bf16[384,2048]{1,0:T(8,128)(2,1)S(1)} %copy-done.18, bf16[384,1024]{1,0:T(8,128)(2,1)} %collective-permute-done.40, bf16[384,1024]{1,0:T(8,128)(2,1)} %get-tuple-element.67, bf16[384,2048]{1,0:T(8,128)(2,1)} %collective-permute-done.22.refs_3_, bf16[384,2048]{1,0:T(8,128)(2,1)S(1)} %copy-done.17, ...), kind=kLoop, calls=%fused_computation.3 | loop fusion | flops 16515072 | bytes 9437191 | tf_op jit(solution)/shard_map/convert_element_type | solution.py:832
  (245 shorter events, 164.4 us)
Async XLA Ops:
  5.1 38.9 %collective-permute-start.1 = (bf16[384,2048]{1,0:T(8,128)(2,1)}, bf16[384,2048]{1,0:T(8,128)(2,1)S(1)}, u32[]{:S(2)}, u32[]{:S(2)}) collective-permute-start(bf16[384,2048]{1,0:T(8,128)(2,1)} %get-tuple-element.66.refs_0_), channel_id=1, source_target_pairs={{0,1},{1,2},{2,3},{4,5},{5,6},{6,7},{8,9},{9,10},{10,11},{12,13},{... | collective-permute-start | bytes 4718600 | tf_op jit(solution)/shard_map/ppermute | solution.py:179
  10.1 38.1 %collective-permute-start.2 = (bf16[384,2048]{1,0:T(8,128)(2,1)}, bf16[384,2048]{1,0:T(8,128)(2,1)}, u32[]{:S(2)}, u32[]{:S(2)}) collective-permute-start(bf16[384,2048]{1,0:T(8,128)(2,1)} %get-tuple-element.66.refs_0_), channel_id=1, source_target_pairs={{3,2},{2,1},{1,0},{7,6},{6,5},{5,4},{11,10},{10,9},{9,8},{15,14},{... | collective-permute-start | bytes 4718600 | tf_op jit(solution)/shard_map/ppermute | solution.py:183
  18.8 45.0 %collective-permute-start.3 = (bf16[1936,512]{1,0:T(8,128)(2,1)}, bf16[1936,512]{1,0:T(8,128)(2,1)}, u32[]{:S(2)}, u32[]{:S(2)}) collective-permute-start(bf16[1936,512]{1,0:T(8,128)(2,1)} %get-tuple-element.30.refs_8_.refs_0_), channel_id=1, source_target_pairs={{0,8},{4,12},{8,0},{12,4},{16,24},{20,28},{24,16},{28,20},{1,9},{5... | collective-permute-start | bytes 5947400 | tf_op jit(solution)/shard_map/ppermute | solution.py:175
  20.4 44.7 %collective-permute-start.4 = (bf16[1936,512]{1,0:T(8,128)(2,1)}, bf16[1936,512]{1,0:T(8,128)(2,1)}, u32[]{:S(2)}, u32[]{:S(2)}) collective-permute-start(bf16[1936,512]{1,0:T(8,128)(2,1)} %get-tuple-element.30.refs_8_.refs_0_), channel_id=1, source_target_pairs={{0,16},{4,20},{8,24},{12,28},{16,0},{20,4},{24,8},{28,12},{1,17},{... | collective-permute-start | bytes 5947400 | tf_op jit(solution)/shard_map/ppermute | solution.py:175
  21.9 43.2 %collective-permute-start = (bf16[1936,512]{1,0:T(8,128)(2,1)}, bf16[1936,512]{1,0:T(8,128)(2,1)S(1)}, u32[]{:S(2)}, u32[]{:S(2)}) collective-permute-start(bf16[1936,512]{1,0:T(8,128)(2,1)} %get-tuple-element.29), channel_id=1, source_target_pairs={{0,4},{4,0},{8,12},{12,8},{16,20},{20,16},{24,28},{28,24},{1,5},{5... | collective-permute-start | bytes 5947400 | tf_op jit(solution)/shard_map/ppermute | solution.py:175
  71.8 39.6 %collective-permute-start.7 = (bf16[384,2048]{1,0:T(8,128)(2,1)}, bf16[384,2048]{1,0:T(8,128)(2,1)}, u32[]{:S(2)}, u32[]{:S(2)}) collective-permute-start(bf16[384,2048]{1,0:T(8,128)(2,1)} %get-tuple-element.31), channel_id=1, source_target_pairs={{3,2},{2,1},{1,0},{7,6},{6,5},{5,4},{11,10},{10,9},{9,8},{15,14},{... | collective-permute-start | bytes 4718600 | tf_op jit(solution)/shard_map/ppermute | solution.py:183
  73.2 39.4 %collective-permute-start.8 = (bf16[384,2048]{1,0:T(8,128)(2,1)}, bf16[384,2048]{1,0:T(8,128)(2,1)}, u32[]{:S(2)}, u32[]{:S(2)}) collective-permute-start(bf16[384,2048]{1,0:T(8,128)(2,1)} %get-tuple-element.32), channel_id=1, source_target_pairs={{0,1},{1,2},{2,3},{4,5},{5,6},{6,7},{8,9},{9,10},{10,11},{12,13},{... | collective-permute-start | bytes 4718600 | tf_op jit(solution)/shard_map/ppermute | solution.py:179
  79.3 45.3 %collective-permute-start.10 = (bf16[1936,512]{1,0:T(8,128)(2,1)S(1)}, bf16[1936,512]{1,0:T(8,128)(2,1)}, u32[]{:S(2)}, u32[]{:S(2)}) collective-permute-start(bf16[1936,512]{1,0:T(8,128)(2,1)S(1)} %copy-done.4), channel_id=1, source_target_pairs={{0,8},{4,12},{8,0},{12,4},{16,24},{20,28},{24,16},{28,20},{1,9},{5... | collective-permute-start | bytes 5947400 | tf_op jit(solution)/shard_map/ppermute | solution.py:175
  79.8 45.0 %collective-permute-start.11 = (bf16[1936,512]{1,0:T(8,128)(2,1)S(1)}, bf16[1936,512]{1,0:T(8,128)(2,1)}, u32[]{:S(2)}, u32[]{:S(2)}) collective-permute-start(bf16[1936,512]{1,0:T(8,128)(2,1)S(1)} %copy-done.4), channel_id=1, source_target_pairs={{0,16},{4,20},{8,24},{12,28},{16,0},{20,4},{24,8},{28,12},{1,17},{... | collective-permute-start | bytes 5947400 | tf_op jit(solution)/shard_map/ppermute | solution.py:175
  129.1 37.5 %collective-permute-start.12 = (bf16[384,2048]{1,0:T(8,128)(2,1)}, bf16[384,2048]{1,0:T(8,128)(2,1)}, u32[]{:S(2)}, u32[]{:S(2)}) collective-permute-start(bf16[384,2048]{1,0:T(8,128)(2,1)} %get-tuple-element.33), channel_id=1, source_target_pairs={{3,2},{2,1},{1,0},{7,6},{6,5},{5,4},{11,10},{10,9},{9,8},{15,14},{... | collective-permute-start | bytes 4718600 | tf_op jit(solution)/shard_map/ppermute | solution.py:183
  130.4 37.4 %collective-permute-start.13 = (bf16[384,2048]{1,0:T(8,128)(2,1)}, bf16[384,2048]{1,0:T(8,128)(2,1)}, u32[]{:S(2)}, u32[]{:S(2)}) collective-permute-start(bf16[384,2048]{1,0:T(8,128)(2,1)} %get-tuple-element.34), channel_id=1, source_target_pairs={{0,1},{1,2},{2,3},{4,5},{5,6},{6,7},{8,9},{9,10},{10,11},{12,13},{... | collective-permute-start | bytes 4718600 | tf_op jit(solution)/shard_map/ppermute | solution.py:179
  138.0 46.3 %collective-permute-start.15 = (bf16[1936,512]{1,0:T(8,128)(2,1)}, bf16[1936,512]{1,0:T(8,128)(2,1)}, u32[]{:S(2)}, u32[]{:S(2)}) collective-permute-start(bf16[1936,512]{1,0:T(8,128)(2,1)} %gate.10.refs_10_.refs_2_), channel_id=1, source_target_pairs={{0,16},{4,20},{8,24},{12,28},{16,0},{20,4},{24,8},{28,12},{1,17},{... | collective-permute-start | bytes 5947400 | tf_op jit(solution)/shard_map/ppermute | solution.py:175
  139.5 44.8 %collective-permute-start.16 = (bf16[1936,512]{1,0:T(8,128)(2,1)}, bf16[1936,512]{1,0:T(8,128)(2,1)}, u32[]{:S(2)}, u32[]{:S(2)}) collective-permute-start(bf16[1936,512]{1,0:T(8,128)(2,1)} %gate.11.refs_13_.refs_5_), channel_id=1, source_target_pairs={{0,8},{4,12},{8,0},{12,4},{16,24},{20,28},{24,16},{28,20},{1,9},{5... | collective-permute-start | bytes 5947400 | tf_op jit(solution)/shard_map/ppermute | solution.py:175
  177.7 59.4 %collective-permute-start.21 = (bf16[384,2048]{1,0:T(8,128)(2,1)}, bf16[384,2048]{1,0:T(8,128)(2,1)S(1)}, u32[]{:S(2)}, u32[]{:S(2)}) collective-permute-start(bf16[384,2048]{1,0:T(8,128)(2,1)} %get-tuple-element.35.refs_4_), channel_id=1, source_target_pairs={{0,1},{1,2},{2,3},{4,5},{5,6},{6,7},{8,9},{9,10},{10,11},{12,13},{... | collective-permute-start | bytes 4718600 | tf_op jit(solution)/shard_map/ppermute | solution.py:179
  182.8 72.1 %collective-permute-start.22 = (bf16[384,2048]{1,0:T(8,128)(2,1)}, bf16[384,2048]{1,0:T(8,128)(2,1)}, u32[]{:S(2)}, u32[]{:S(2)}) collective-permute-start(bf16[384,2048]{1,0:T(8,128)(2,1)} %get-tuple-element.45), channel_id=1, source_target_pairs={{3,2},{2,1},{1,0},{7,6},{6,5},{5,4},{11,10},{10,9},{9,8},{15,14},{... | collective-permute-start | bytes 4718600 | tf_op jit(solution)/shard_map/ppermute | solution.py:183
  193.0 31.2 %collective-permute-start.18 = (bf16[512,512]{1,0:T(8,128)(2,1)}, bf16[512,512]{1,0:T(8,128)(2,1)S(1)}, u32[]{:S(2)}, u32[]{:S(2)}) collective-permute-start(bf16[512,512]{1,0:T(8,128)(2,1)} %get-tuple-element.39), channel_id=1, source_target_pairs={{0,8},{4,12},{8,0},{12,4},{16,24},{20,28},{24,16},{28,20},{1,9},{5... | collective-permute-start | bytes 1572872 | tf_op jit(solution)/shard_map/ppermute | solution.py:175
  194.5 29.7 %collective-permute-start.19 = (bf16[512,512]{1,0:T(8,128)(2,1)}, bf16[512,512]{1,0:T(8,128)(2,1)}, u32[]{:S(2)}, u32[]{:S(2)}) collective-permute-start(bf16[512,512]{1,0:T(8,128)(2,1)} %get-tuple-element.40), channel_id=1, source_target_pairs={{0,16},{4,20},{8,24},{12,28},{16,0},{20,4},{24,8},{28,12},{1,17},{... | collective-permute-start | bytes 1572872 | tf_op jit(solution)/shard_map/ppermute | solution.py:175
  196.8 27.4 %collective-permute-start.20 = (bf16[512,512]{1,0:T(8,128)(2,1)}, bf16[512,512]{1,0:T(8,128)(2,1)}, u32[]{:S(2)}, u32[]{:S(2)}) collective-permute-start(bf16[512,512]{1,0:T(8,128)(2,1)} %get-tuple-element.41), channel_id=1, source_target_pairs={{0,24},{4,28},{8,16},{12,20},{16,8},{20,12},{24,0},{28,4},{1,25},{... | collective-permute-start | bytes 1572872 | tf_op jit(solution)/shard_map/ppermute | solution.py:175
  228.9 39.6 %collective-permute-start.26 = (bf16[512,512]{1,0:T(8,128)(2,1)}, bf16[512,512]{1,0:T(8,128)(2,1)S(1)}, u32[]{:S(2)}, u32[]{:S(2)}) collective-permute-start(bf16[512,512]{1,0:T(8,128)(2,1)} %get-tuple-element.48), channel_id=1, source_target_pairs={{0,1},{1,0},{2,3},{3,2},{4,5},{5,4},{6,7},{7,6},{8,9},{9,8},{10,11... | collective-permute-start | bytes 1572872 | tf_op jit(solution)/shard_map/ppermute | solution.py:785
  232.5 39.9 %collective-permute-start.27 = (bf16[512,512]{1,0:T(8,128)(2,1)}, bf16[512,512]{1,0:T(8,128)(2,1)S(1)}, u32[]{:S(2)}, u32[]{:S(2)}) collective-permute-start(bf16[512,512]{1,0:T(8,128)(2,1)} %get-tuple-element.49), channel_id=1, source_target_pairs={{0,2},{1,3},{2,0},{3,1},{4,6},{5,7},{6,4},{7,5},{8,10},{9,11},{10,... | collective-permute-start | bytes 1572872 | tf_op jit(solution)/shard_map/ppermute | solution.py:785
  236.9 35.5 %collective-permute-start.28 = (bf16[512,512]{1,0:T(8,128)(2,1)}, bf16[512,512]{1,0:T(8,128)(2,1)}, u32[]{:S(2)}, u32[]{:S(2)}) collective-permute-start(bf16[512,512]{1,0:T(8,128)(2,1)} %get-tuple-element.50), channel_id=1, source_target_pairs={{0,3},{1,2},{2,1},{3,0},{4,7},{5,6},{6,5},{7,4},{8,11},{9,10},{10,... | collective-permute-start | bytes 1572872 | tf_op jit(solution)/shard_map/ppermute | solution.py:785
  277.2 51.7 %collective-permute-start.29 = (bf16[1024,1024]{1,0:T(8,128)(2,1)}, bf16[1024,1024]{1,0:T(8,128)(2,1)S(1)}, u32[]{:S(2)}, u32[]{:S(2)}) collective-permute-start(bf16[1024,1024]{1,0:T(8,128)(2,1)} %block_plan.1.refs_8_), channel_id=1, source_target_pairs={{0,8},{4,12},{8,0},{12,4},{16,24},{20,28},{24,16},{28,20},{1,9},{5... | collective-permute-start | bytes 6291464 | tf_op jit(solution)/shard_map/ppermute | solution.py:175
  284.7 55.4 %collective-permute-start.30 = (bf16[1024,1024]{1,0:T(8,128)(2,1)}, bf16[1024,1024]{1,0:T(8,128)(2,1)}, u32[]{:S(2)}, u32[]{:S(2)}) collective-permute-start(bf16[1024,1024]{1,0:T(8,128)(2,1)} %block_plan.1.refs_8_), channel_id=1, source_target_pairs={{0,16},{4,20},{8,24},{12,28},{16,0},{20,4},{24,8},{28,12},{1,17},{... | collective-permute-start | bytes 6291464 | tf_op jit(solution)/shard_map/ppermute | solution.py:175
  347.3 27.8 %collective-permute-start.35 = (bf16[512,1024]{1,0:T(8,128)(2,1)}, bf16[512,1024]{1,0:T(8,128)(2,1)S(1)}, u32[]{:S(2)}, u32[]{:S(2)}) collective-permute-start(bf16[512,1024]{1,0:T(8,128)(2,1)} %get-tuple-element.51), channel_id=1, source_target_pairs={{0,16},{4,20},{8,24},{12,28},{16,0},{20,4},{24,8},{28,12},{1,17},{... | collective-permute-start | bytes 3145736 | tf_op jit(solution)/shard_map/ppermute | solution.py:175
  (65 other events, 661.7 us)
where the time goes:
time: 432 us; the launch traced here: 424 us
  waiting for transfers between devices  151 us (35%)
  Pallas kernels  128 us (30%)
  starting transfers between devices  85.3 us (20%)
  other arithmetic  29.4 us (7%)
  local copies, waits for them, and re-layouts  29 us (7%)
    ppermute x7, waiting for transfers between devices, hop_down(): return lax.ppermute(v, 'tp', [(N_TP - 1 - i, N_TP - 2 - i) for i in pairs])  90.9 us
    pallas_call x12, Pallas kernels, move(): pl.pallas_call(kernel, out_shape=tuple((jax.ShapeDtypeStruct(shape, jnp.b...  45.5 us
    ppermute x23, waiting for transfers between devices, swap(): return lax.ppermute(x, 'ctx', [(c, c ^ bit) for c in range(N_CTX)])  38.2 us
    ppermute x23, starting transfers between devices, swap(): return lax.ppermute(x, 'ctx', [(c, c ^ bit) for c in range(N_CTX)])  34.7 us
    ppermute x7, starting transfers between devices, hop_up(): return lax.ppermute(v, 'tp', [(i, i + 1) for i in pairs])  29.8 us
    pallas_call x2, Pallas kernels, attend_prefix(): pl.pallas_call(prefix_kernel, out_shape=(jax.ShapeDtypeStruct((blocks, ch...  25.7 us
    pallas_call x1, Pallas kernels, project(): pl.pallas_call(functools.partial(project_kernel, scale, at_kv), out_shape...  23.5 us
    ppermute x7, waiting for transfers between devices, hop_up(): return lax.ppermute(v, 'tp', [(i, i + 1) for i in pairs])  17.9 us
  transfers between devices with their start and end apart: 41, of which 19 were waited for; matrix products, arithmetic and copies ran while one was open for 9% of the time, Pallas kernels for 23%

commit v1 on v0

--- a/solution.py
+++ b/solution.py
@@ -306,45 +306,49 @@
     return pl.multiple_of(value * of, of)
 
 
+AHEAD = 3
+
+
 def project_kernel(scale, at_kv, ids_ref, *refs):
     xs, ws = refs[:8], refs[8:16]
     factor_ref, cos_ref, sin_ref, q_ref, kv_ref, x_buf, w_buf, x_sem, w_sem = refs[16:]
     chip, core = ids_ref[0], ids_ref[1]
-    tok, half, cols = xs[0].shape[0], x_buf.shape[-1], ws[0].shape[1]
+    tok, half, cols = xs[7].shape[0], x_buf.shape[-1], ws[0].shape[1]
     fold = half // 2
     mine = pl.multiple_of(core * tok, 128)
     theirs = pl.multiple_of((1 - core) * tok, 128)
-    waits = []
-    for r in range(4):
+
+    def fetch(at):
+        r, h = at // 2, at % 2
         place = ids_ref[3 + r]
-        for h in range(2):
-            at = 2 * r + h
-            waits.append([])
-            for i in range(3):
-                for m in range(4):
-                    src, dst = ws[2 * m + h], w_buf.at[at]
-                    if i == 0:
-                        src, dst = src.at[pl.ds(0, half)], dst.at[:, pl.ds(0, cols)]
-                    else:
-                        lanes = pl.ds((i - 1) * 2 * HD, 2 * HD)
-                        src = src.at[pl.ds(at_kv, fold), lanes]
-                        dst = dst.at[pl.ds((i - 1) * fold, fold), pl.ds(cols, 2 * HD)]
-                    copy = pltpu.make_async_copy(src, dst, w_sem.at[3 * at + i])
-                    pl.when((place ^ chip) == m)(copy.start)
-                waits[at].append(copy)
-            features = pl.ds(pl.multiple_of((core ^ h) * half, 128), half)
-            for s, rows in ((0, mine), (1, theirs)):
-                copy = pltpu.make_async_copy(
-                    xs[2 * r + s].at[:, features],
-                    x_buf.at[at, pl.ds(rows, tok)],
-                    x_sem.at[2 * at + s],
-                )
-                copy.start()
-                waits[at].append(copy)
+        waits = []
+        for i in range(3):
+            for m in range(4):
+                src, dst = ws[2 * m + h], w_buf.at[at]
+                if i == 0:
+                    src, dst = src.at[pl.ds(0, half)], dst.at[:, pl.ds(0, cols)]
+                else:
+                    lanes = pl.ds((i - 1) * 2 * HD, 2 * HD)
+                    src = src.at[pl.ds(at_kv, fold), lanes]
+                    dst = dst.at[pl.ds((i - 1) * fold, fold), pl.ds(cols, 2 * HD)]
+                copy = pltpu.make_async_copy(src, dst, w_sem.at[3 * at + i])
+                pl.when((place ^ chip) == m)(copy.start)
+            waits.append(copy)
+        features = pl.ds(pl.multiple_of((core ^ h) * half, 128), half)
+        for s, rows in ((0, mine), (1, theirs)):
+            src = xs[2 * r + s].at[pl.ds(tok if r == 1 else 0, tok), features]
+            copy = pltpu.make_async_copy(src, x_buf.at[at, pl.ds(rows, tok)], x_sem.at[2 * at + s])
+            copy.start()
+            waits.append(copy)
+        return waits
+
+    ahead = [fetch(at) for at in range(AHEAD)]
     acc = 0.0
     for at in range(8):
-        for copy in waits[at]:
+        for copy in ahead[at]:
             copy.wait()
+        if at + AHEAD < 8:
+            ahead.append(fetch(at + AHEAD))
         acc = acc + jnp.dot(x_buf[at], w_buf[at], preferred_element_type=jnp.float32)
     factor = factor_ref[...]
     heads = q_ref.shape[0]
@@ -359,7 +363,7 @@
 
 
 def project(ids, xs, weights, at_kv, factor, cosine, sinus, scale):
-    tok, feat = xs[0].shape
+    tok, feat = xs[7].shape
     cols = weights[0].shape[1]
     half = feat // 2
     return pl.pallas_call(
@@ -383,8 +387,7 @@
 
 
 BT = 256
-BK = 512
-UNROLL = 2
+BK = 1024
 CHAIN = 2
 
 
@@ -399,13 +402,13 @@
     return new, acc
 
 
-def prefix_kernel(bound_ref, q_ref, n_ref, kv_ref, *refs):
-    m_out, acc_out, v_ext, s_ref, m_ref, acc_ref = refs[-6:]
+def attend_kernel(
+    halo, bound_ref, q_ref, n_ref, lo_ref, kv_ref, k_ref, v_ref, out_ref, v_ext, s_ref, m_ref, acc_ref
+):
     b = pl.program_id(0)
     heads, bt = q_ref.shape[0], q_ref.shape[1]
     rows, chains = CHAIN * bt, heads // CHAIN
-    big = UNROLL * BK
-    last = kv_ref.shape[1] // big - 1
+    last = kv_ref.shape[1] // BK - 1
 
     @pl.when(b == 0)
     def _():
@@ -414,30 +417,26 @@
 
     m_ref[...] = jnp.full_like(m_ref, MASKED)
     acc_ref[...] = jnp.zeros_like(acc_ref)
-    n_rows = jnp.concatenate([n_ref[:, :1]] * CHAIN, axis=0)
 
     def query(g):
         return q_ref[g * CHAIN : (g + 1) * CHAIN].reshape(rows, HD)
 
     s_ref[...] = scores(query(0), kv_ref[0, :BK, :])
-    items = [(u, g) for u in range(UNROLL) for g in range(chains)]
 
     def body(kb, masked):
-        start = pl.multiple_of(kb * big, big)
-        follow = pl.multiple_of(jnp.minimum(kb + 1, last) * big, big)
+        start = pl.multiple_of(kb * BK, BK)
+        follow = pl.multiple_of(jnp.minimum(kb + 1, last) * BK, BK)
         ms = [m_ref[g][:, :1] for g in range(chains)]
         accs = [acc_ref[g] for g in range(chains)]
         s = s_ref[...]
-        for t, (u, g) in enumerate(items):
-            if t + 1 < len(items):
-                at, who = start + items[t + 1][0] * BK, items[t + 1][1]
-            else:
-                at, who = follow, 0
+        v = v_ext[pl.ds(start, BK), :]
+        for g in range(chains):
+            at, who = (start, g + 1) if g + 1 < chains else (follow, 0)
             ahead = scores(query(who), kv_ref[0, pl.ds(at, BK), :])
             if masked:
-                col = lax.broadcasted_iota(jnp.int32, s.shape, 1) + (start + u * BK)
+                n_rows = jnp.concatenate([n_ref[:, :1]] * CHAIN, axis=0)
+                col = lax.broadcasted_iota(jnp.int32, s.shape, 1) + start
                 s = jnp.where(col < n_rows, s, MASKED)
-            v = v_ext[pl.ds(start + u * BK, BK), :]
             ms[g], accs[g] = absorb(s, v, ms[g], accs[g])
             s = ahead
         s_ref[...] = s
@@ -445,38 +444,55 @@
             m_ref[g] = jnp.broadcast_to(ms[g], (rows, 128))
             acc_ref[g] = accs[g]
 
-    full = bound_ref[0, b] // big
-    some = (bound_ref[1, b] + big - 1) // big
+    full = bound_ref[0, b] // BK
+    some = (bound_ref[1, b] + BK - 1) // BK
     lax.fori_loop(0, full, lambda kb, c: (body(kb, False), c)[1], 0)
     lax.fori_loop(full, some, lambda kb, c: (body(kb, True), c)[1], 0)
-    m_out[0] = m_ref[...]
-    acc_out[0] = acc_ref[...]
-
-
-def attend_prefix(bounds, q, group, n_tok, kv, arrived=()):
-    heads, tokens = CHAIN, q.shape[1]
-    blocks = tokens // BT
+
+    span = halo + bt
+    start = pl.multiple_of(b * bt, bt)
+    k = k_ref[pl.ds(start, span), :]
+    v = v_ref[pl.ds(start, span), :]
+    v = jnp.concatenate([v, jnp.ones_like(v)], axis=1)
+    lo = jnp.concatenate([lo_ref[:, :1]] * CHAIN, axis=0)
+    col = lax.broadcasted_iota(jnp.int32, (rows, span), 1)
+    row = lax.broadcasted_iota(jnp.int32, (rows, span), 0) % bt
+    seen = (col + start >= lo) & (col <= row + halo)
+    for g in range(chains):
+        s = jnp.where(seen, scores(query(g), k), MASKED)
+        _, acc = absorb(s, v, m_ref[g][:, :1], acc_ref[g])
+        mixed = (acc[:, :HD] / acc[:, HD:]).astype(jnp.bfloat16)
+        for h in range(CHAIN):
+            at = (g * CHAIN + h) * HD
+            out_ref[:, at : at + HD] = mixed[h * bt : (h + 1) * bt]
+
+
+def attend(bounds, q, n_tok, lo_tok, kv, k, v, arrived=()):
+    heads, tokens = q.shape[:2]
     chains, rows = heads // CHAIN, CHAIN * BT
     keys = kv.shape[1]
+    halo = k.shape[0] - tokens
+    count = len(arrived)
+
+    def kernel(*refs):
+        attend_kernel(halo, *refs[:7], *refs[7 + count :])
+
     return pl.pallas_call(
-        prefix_kernel,
-        out_shape=(
-            jax.ShapeDtypeStruct((blocks, chains, rows, 128), jnp.float32),
-            jax.ShapeDtypeStruct((blocks, chains, rows, 2 * HD), jnp.float32),
-        ),
+        kernel,
+        out_shape=jax.ShapeDtypeStruct((tokens, heads * HD), jnp.bfloat16),
         grid_spec=pltpu.PrefetchScalarGridSpec(
             num_scalar_prefetch=1,
-            grid=(blocks,),
+            grid=(tokens // BT,),
             in_specs=[
-                pl.BlockSpec((heads, BT, HD), lambda b, *_: (group, b, 0)),
+                pl.BlockSpec((heads, BT, HD), lambda b, *_: (0, b, 0)),
+                pl.BlockSpec((BT, 128), lambda b, *_: (b, 0)),
                 pl.BlockSpec((BT, 128), lambda b, *_: (b, 0)),
                 pl.BlockSpec((2, keys, HD), lambda b, *_: (0, 0, 0)),
+                pl.BlockSpec(k.shape, lambda b, *_: (0, 0)),
+                pl.BlockSpec(v.shape, lambda b, *_: (0, 0)),
             ]
             + specs_of(arrived),
-            out_specs=(
-                pl.BlockSpec((1, chains, rows, 128), lambda b, *_: (b, 0, 0, 0)),
-                pl.BlockSpec((1, chains, rows, 2 * HD), lambda b, *_: (b, 0, 0, 0)),
-            ),
+            out_specs=pl.BlockSpec((BT, heads * HD), lambda b, *_: (b, 0)),
             scratch_shapes=[
                 pltpu.VMEM((keys, 2 * HD), jnp.bfloat16),
                 pltpu.VMEM((rows, BK), jnp.float32),
@@ -486,69 +502,13 @@
         ),
         compiler_params=pltpu.CompilerParams(vmem_limit_bytes=GRANT),
         cost_estimate=LITTLE,
-        name="attend_prefix",
-    )(bounds, q, n_tok, kv, *arrived)
-
-
-def new_kernel(halo, q_ref, lo_ref, k_ref, v_ref, *refs):
-    states, out_ref = refs[:-1], refs[-1]
-    b = pl.program_id(0)
-    heads, bt = q_ref.shape[0], q_ref.shape[1]
-    rows = CHAIN * bt
-    span = halo + bt
-    start = pl.multiple_of(b * bt, bt)
-    k = k_ref[pl.ds(start, span), :]
-    v = v_ref[pl.ds(start, span), :]
-    v_ext = jnp.concatenate([v, jnp.ones_like(v)], axis=1)
-    lo = jnp.concatenate([lo_ref[:, :1]] * CHAIN, axis=0)
-
-    def hide(s):
-        col = lax.broadcasted_iota(jnp.int32, s.shape, 1)
-        row = lax.broadcasted_iota(jnp.int32, s.shape, 0) % bt
-        return jnp.where((col + start >= lo) & (col <= row + halo), s, MASKED)
-
-    for g in range(heads // CHAIN):
-        q = q_ref[g * CHAIN : (g + 1) * CHAIN].reshape(rows, HD)
-        _, acc = absorb(
-            hide(scores(q, k)), v_ext, states[2 * g][0, 0][:, :1], states[2 * g + 1][0, 0]
-        )
-        mixed = (acc[:, :HD] / acc[:, HD:]).astype(jnp.bfloat16)
-        for h in range(CHAIN):
-            at = (g * CHAIN + h) * HD
-            out_ref[:, at : at + HD] = mixed[h * bt : (h + 1) * bt]
-
-
-def attend_new(q, lo_tok, k, v, states):
-    heads, tokens, _ = q.shape
-    blocks = tokens // BT
-    chains, rows = heads // CHAIN, CHAIN * BT
-    halo = k.shape[0] - tokens
-    whole = lambda b: (0, 0)
-    return pl.pallas_call(
-        functools.partial(new_kernel, halo),
-        out_shape=jax.ShapeDtypeStruct((tokens, heads * HD), jnp.bfloat16),
-        grid=(blocks,),
-        in_specs=[
-            pl.BlockSpec((heads, BT, HD), lambda b: (0, b, 0)),
-            pl.BlockSpec((BT, 128), lambda b: (b, 0)),
-            pl.BlockSpec(k.shape, whole),
-            pl.BlockSpec(v.shape, whole),
-        ]
-        + [
-            pl.BlockSpec((1, 1, rows, 128), lambda b: (b, 0, 0, 0)),
-            pl.BlockSpec((1, 1, rows, 2 * HD), lambda b: (b, 0, 0, 0)),
-        ]
-        * chains,
-        out_specs=pl.BlockSpec((BT, heads * HD), lambda b: (b, 0)),
-        compiler_params=pltpu.CompilerParams(vmem_limit_bytes=GRANT),
-        cost_estimate=LITTLE,
-        name="attend_new",
-    )(q, lo_tok, k, v, *states)
+        name="attend",
+    )(bounds, q, n_tok, lo_tok, kv, k, v, *arrived)
 
 
 def out_kernel(ids_ref, *refs):
     xs, ws = refs[:8], refs[8:13]
-    out_ref, x_buf, w_buf, x_sem, w_sem = refs[13:]
+    keep_ref, give_ref, x_buf, w_buf, o_buf, x_sem, w_sem = refs[13:]
     chip, core, z = ids_ref[0], ids_ref[1], ids_ref[2]
     width = xs[0].shape[1]
     rows = w_buf.shape[1] // 4
@@ -590,7 +550,10 @@
             ).wait()
         term = jnp.dot(x_buf[r], w_buf[r], preferred_element_type=jnp.float32)
         acc = term if acc is None else acc + term
-    out_ref[...] = acc.astype(jnp.bfloat16)
+    o_buf[...] = acc.astype(jnp.bfloat16)
+    half = keep_ref.shape[0]
+    keep_ref[...] = o_buf[pl.ds(pl.multiple_of(core * half, 128), half)]
+    give_ref[...] = o_buf[pl.ds(pl.multiple_of((1 - core) * half, 128), half)]
 
 
 def out_project(ids, xs, ws):
@@ -598,12 +561,13 @@
     depth, cols = ws[0].shape
     return pl.pallas_call(
         out_kernel,
-        out_shape=jax.ShapeDtypeStruct((tokens, cols), jnp.bfloat16),
+        out_shape=(jax.ShapeDtypeStruct((tokens // 2, cols), jnp.bfloat16),) * 2,
         in_specs=[SMEM] + [HBM] * 13,
-        out_specs=VMEM,
+        out_specs=(VMEM, VMEM),
         scratch_shapes=[
             pltpu.VMEM((4, tokens, 2 * width), jnp.bfloat16),
             pltpu.VMEM((4, depth, cols), jnp.bfloat16),
+            pltpu.VMEM((tokens, cols), jnp.bfloat16),
             pltpu.SemaphoreType.DMA((8,)),
             pltpu.SemaphoreType.DMA((16,)),
         ],
@@ -702,27 +666,40 @@
 
     x1, y1, given = swap(own, 2), swap(own, 4), swap(give, 1)
     mine = squares(scaled, z)
-    near = pick(z, (d1, d1, u1, u1), here, (cosine, sinus, mine))
+
+    up, down = hops(here, pending, u1, d1, 3, (1, 2, 3), (), (cosine, sinus, mine, given))
+    u2, d2 = hop_up(up, every), hop_down(down, every)
+
+    given = gate(given, x1, y1)
+    x2, y2 = swap(given, 2), swap(given, 4)
+
+    def near_plan(at, src, out):
+        yield one(src[0], out[0].at[pl.ds(0, tok)])
+        yield ([(at[2] < 2, src[1]), (at[2] >= 2, src[2])], out[0].at[pl.ds(tok, tok)])
+
+    (near,) = move(near_plan, ((chip_tok, feat),), here, (scaled, d1, u1), (up,))
     over1 = swap(near, 1)
-
-    up, down = hops(here, pending, u1, d1, 3, (1, 2, 3), (), (x1, y1, given, over1))
-    u2, d2 = hop_up(up, every), hop_down(down, every)
-
-    given = gate(given, u1, d1, x1, y1, over1)
-    x2, y2, over0 = swap(given, 2), swap(given, 4), swap(gate(scaled, given), 1)
-    mine = mine + squares(near, places[1])
-    theirs = squares(over1, places[1])
-    second = pick(z, (d2, d2, u2, u2), here, (over0, mine, theirs))
-
-    up, down = hops(here, pending, u2, d2, 2, (2,), (1,), (x2, y2, over0, second))
-    u3, d3 = hop_up(up, every), hop_down(down, every)
-
-    x1, y2 = gate(x1, u2, d2, x2, over0, second), gate(y2, u2, d2, x2, over0, second)
+    mine = mine + squares(near[tok:], places[1])
+    theirs = squares(over1[:tok], z) + squares(over1[tok:], places[1])
+
+    up, down = hops(here, pending, u2, d2, 2, (2,), (1,))
+    turn = swap(gate(notes, x2, y2), 1)
+    u3, d3 = hop_up(gate(up, turn), every), hop_down(gate(down, turn), every)
+
+    x1, y2 = gate(x1, x2, y2), gate(y2, x2)
     far_own, far_other = swap(x1, 4), swap(y2, 2)
+    def piece_plan(at, src, out):
+        for r, dst in enumerate(out):
+            rows = pl.ds(multiple(at[0] ^ r, n_piece), n_piece)
+            for i in range(2):
+                part = src[0].at[rows, pl.ds(i * q_cols, q_cols)]
+                yield one(part, dst.at[pl.ds(i * n_piece, n_piece)])
+
+    by_chip = move(piece_plan, ((2 * n_piece, q_cols),) * 4, here, (w_out,), (up,))
+    second = pick(z, (d2, d2, u2, u2), here, (up, by_chip[0]))
     over2 = swap(second, 1)
     mine = mine + squares(second, places[2])
-    theirs = theirs + squares(over0, z)
-    up, down = hops(here, pending, u3, d3, 1, (), (1, 2, 3), (over2,))
+    up, down = hops(here, pending, u3, d3, 1, (), (1, 2, 3))
     u4, d4 = hop_up(up, every), hop_down(down, every)
     third = pick(z, (d3, u1, d1, u3), here, (up, mine, theirs))
     over3 = swap(third, 1)
@@ -732,7 +709,7 @@
     total = jnp.where(first, jnp.concatenate([mine, theirs]), jnp.concatenate([theirs, mine]))
     factor = lax.rsqrt(total * (1.0 / depth) + NORM_EPSILON)
     factor = jnp.broadcast_to(factor, (chip_tok, 128))
-    xs = [scaled, over0, near, over1, second, over2, third, over3]
+    xs = [near, over1, near, over1, second, over2, third, over3]
     own_rows = (own, given, x1, x2, y1, y2, far_own, far_other)
 
     said = [rows[n_both + n_kv : n_both + n_kv + 2].astype(jnp.float32) for rows in own_rows]
@@ -759,18 +736,9 @@
 
     (kv,) = move(prefix_plan, ((2, N_CTX * 2 * fold, HD),), here, own_rows, (third,))
 
-    def piece_plan(at, src, out):
-        for r, dst in enumerate(out):
-            rows = pl.ds(multiple(at[0] ^ r, n_piece), n_piece)
-            for i in range(2):
-                part = src[0].at[rows, pl.ds(i * q_cols, q_cols)]
-                yield one(part, dst.at[pl.ds(i * n_piece, n_piece)])
-
-    by_chip = move(
-        piece_plan, ((2 * n_piece, q_cols),) * 4, here, (w_out,), (far_own, far_other, third, kv)
-    )
-    by_chip = (by_chip[0],) + tuple(swap(by_chip[r], 2 * r) for r in (1, 2, 3))
-
+    by_chip = (by_chip[0],) + tuple(
+        swap(gate(by_chip[r], far_own, far_other, over2), 2 * r) for r in (1, 2, 3)
+    )
     scale = math.log2(math.e) / math.sqrt(HD)
     q, kv_new = project(ids, xs, own_rows, n_both, factor, cosine, sinus, scale)
     before = lax.ppermute(kv_new[:, tok:], "ctx", [(i, i + 2) for i in range(N_CTX - 2)])
@@ -780,14 +748,12 @@
             near = (at[2] ^ r) ^ at[0]
             yield ([(near == m, src[m]) for m in range(4)], dst)
 
-    pieces = list(move(pieces_plan, ((2 * n_piece, q_cols),) * 4, here, by_chip, (q,)))
+    pieces = list(move(pieces_plan, ((2 * n_piece, q_cols),) * 4, here, by_chip, (q, u4, d4)))
     for r in (1, 2, 3):
         pieces[r] = lax.ppermute(pieces[r], "tp", [(i, i ^ r) for i in range(N_TP)])
-    part_a = attend_prefix(bounds, q, 0, n_wide, kv, (pieces[0],))
-    part_b = attend_prefix(bounds, q, 1, n_wide, kv, (part_a[0], before, u4, d4))
     k_near = jnp.concatenate([before[0], kv_new[0]], axis=0)
     v_near = jnp.concatenate([before[1], kv_new[1]], axis=0)
-    attended = attend_new(q, lo_wide, k_near, v_near, part_a + part_b)
+    attended = attend(bounds, q, n_wide, lo_wide, kv, k_near, v_near, (pieces[0],))
 
     def block_plan(at, src, out):
         for r, part in enumerate(src):
@@ -795,30 +761,29 @@
                 dst = out[0].at[pl.ds(r * n_piece, n_piece), pl.ds(i * q_cols, q_cols)]
                 yield one(part.at[pl.ds(i * n_piece, n_piece)], dst)
 
-    (block,) = move(block_plan, ((4 * n_piece, 2 * q_cols),), here, pieces, (part_b[0],))
+    (block,) = move(block_plan, ((4 * n_piece, 2 * q_cols),), here, pieces, (attended,))
     half = block.shape[0] // 2
     wo_x, wo_y = swap(block, 2), swap(block, 4)
     u1, d1 = hop_up(attended, every), hop_down(attended, every)
-    near = pick(z, (d1, d1, u1, u1), here, (wo_x, wo_y))
+    near = pick(z, (d1, d1, u1, u1), here)
 
     def far_plan(at, src, out):
         yield one(src[0].at[pl.ds(0, half)], out[0])
         yield one(src[1].at[pl.ds(half, half)], out[1])
 
     to_y, to_x = move(
-        far_plan, ((half, block.shape[1]),) * 2, here, (wo_x, wo_y), (near,)
+        far_plan, ((half, block.shape[1]),) * 2, here, (wo_x, wo_y), (near, u4, d4)
     )
     wo_parts = (block, wo_x, wo_y, swap(to_y, 4), swap(to_x, 2))
-    u2, d2 = hop_up(gate(u1, near), (1, 2)), hop_down(gate(d1, near), (1, 2))
+    u2, d2 = hop_up(u1, (1, 2)), hop_down(d1, (1, 2))
     second = pick(z, (d2, d2, u2, u2), here)
-    u3, d3 = hop_up(gate(u2, *wo_parts[3:]), (2,)), hop_down(gate(d2, *wo_parts[3:]), (2,))
+    u3, d3 = hop_up(gate(u2, to_y), (2,)), hop_down(gate(d2, to_y), (2,))
     third = pick(z, (d3, u1, d1, u3), here)
     hs = []
     for part in (attended, near, second, third):
         hs += [part, swap(part, 1)]
-    projected = out_project(ids, hs, wo_parts)
-    mine = lax.dynamic_slice_in_dim(projected, core * tok, tok, 0)
-    theirs = swap(lax.dynamic_slice_in_dim(projected, (1 - core) * tok, tok, 0), 1)
+    mine, theirs = out_project(ids, hs, wo_parts)
+    theirs = swap(theirs, 1)
     head_share = jnp.where(
         first,
         jnp.concatenate([mine, theirs], axis=1),

time: 432 us -> 385 us (0.89)
  starting transfers between devices: 85.3 us -> 72 us
  local copies, waits for them, and re-layouts: 29 us -> 18.2 us
  Pallas kernels: 128 us -> 118 us
  waiting for transfers between devices: 151 us -> 143 us
    ppermute x23, waiting for transfers between devices: 38.2 us -> 12.8 us  [swap(): return lax.ppermute(x, 'ctx', [(c, c ^ bit) for c in range(N_CTX)])]
    ppermute x23, starting transfers between devices: 34.7 us -> 23.2 us  [swap(): return lax.ppermute(x, 'ctx', [(c, c ^ bit) for c in range(N_CTX)])]
    pallas_call x4 -> x2, Pallas kernels: 45.3 us -> 36.4 us  [the longest x1 23.6 us: attend(): pl.pallas_call(kernel, out_shape=jax.ShapeDtypeStruct((tokens, heads * HD...]
    ppermute x7, waiting for transfers between devices: 90.9 us -> 98.5 us  [hop_down(): return lax.ppermute(v, 'tp', [(N_TP - 1 - i, N_TP - 2 - i) for i in pairs])]
    unnamed x99 -> x76, local copies, waits for them, and re-layouts: 13.6 us -> 7.26 us
    ppermute x3, waiting for transfers between devices: 3.93 us -> 9.08 us  [per_device(): pieces[r] = lax.ppermute(pieces[r], 'tp', [(i, i ^ r) for i in range(N_TP)])]
    ppermute x7, waiting for transfers between devices: 17.9 us -> 22.9 us  [hop_up(): return lax.ppermute(v, 'tp', [(i, i + 1) for i in pairs])]
    reduce_sum x5 -> x4, other arithmetic: 12.7 us -> 11.1 us  [squares(): jnp.sum(jnp.square(part.astype(jnp.float32) / g[None, :]), axis=1, keepdi...]
  transfers between devices with their start and end apart: 41 -> 41, of which waited for: 19 -> 16; matrix products, arithmetic and copies ran while one was open for 9% -> 8% of each run, Pallas kernels for 23% -> 24%
where the time goes in v1:
time: 385 us; the launch traced here: 382 us
  waiting for transfers between devices  143 us (37%)
  Pallas kernels  118 us (31%)
  starting transfers between devices  72 us (19%)
  other arithmetic  28.8 us (7%)
  local copies, waits for them, and re-layouts  18.2 us (5%)
    ppermute x7, waiting for transfers between devices, hop_down(): return lax.ppermute(v, 'tp', [(N_TP - 1 - i, N_TP - 2 - i) for i in pairs])  98.5 us
    pallas_call x12, Pallas kernels, move(): pl.pallas_call(kernel, out_shape=tuple((jax.ShapeDtypeStruct(shape, jnp.b...  46.3 us
    ppermute x7, starting transfers between devices, hop_up(): return lax.ppermute(v, 'tp', [(i, i + 1) for i in pairs])  30.9 us
    pallas_call x1, Pallas kernels, attend(): pl.pallas_call(kernel, out_shape=jax.ShapeDtypeStruct((tokens, heads * HD...  23.6 us
    ppermute x23, starting transfers between devices, swap(): return lax.ppermute(x, 'ctx', [(c, c ^ bit) for c in range(N_CTX)])  23.2 us
    ppermute x7, waiting for transfers between devices, hop_up(): return lax.ppermute(v, 'tp', [(i, i + 1) for i in pairs])  22.9 us
    pallas_call x1, Pallas kernels, project(): pl.pallas_call(functools.partial(project_kernel, scale, at_kv), out_shape...  21.7 us
    pallas_call x3, Pallas kernels, hops(): pl.pallas_call(kernel, out_shape=(shape, shape), in_specs=[SMEM, HBM, HBM...  13.5 us
  transfers between devices with their start and end apart: 41, of which 16 were waited for; matrix products, arithmetic and copies ran while one was open for 8% of the time, Pallas kernels for 24%

profile of v1, /device:TPU:0, one launch (start us, length us, event | category | flops | bytes accessed | tf_op | source)
XLA Modules:
  0.0 381.6 jit_solution(11292700529011607532)
XLA Ops:
  4.4 5.1 %first_plan.1 = (bf16[1936,512]{1,0:T(8,128)(2,1)}, bf16[1936,512]{1,0:T(8,128)(2,1)}) custom-call(s32[3]{0:T(128)} %pad_add_fusion.1.ids_ref, bf16[1024,1024]{1,0:T(8,128)(2,1)} %refs_0_.2, bf16[1024,1024]{1,0:T(8,128)(2,1)} %refs_1_.1, bf16[1024,1024]{1,0:T(8,128)(2,1)} %refs_2_.1, bf16[8,768,128]{2,1,0:T(8,128)(2,1)} %refs_3_.1, ...), custom_call_target="tpu_custom_call" | custom-call | bytes 1024 | tf_op jit(solution)/shard_map/first_plan/pallas_call | solution.py:218
  14.9 6.3 %collective-permute-start.8 = (bf16[384,2048]{1,0:T(8,128)(2,1)}, bf16[384,2048]{1,0:T(8,128)(2,1)}, u32[]{:S(2)}, u32[]{:S(2)}) collective-permute-start(bf16[384,2048]{1,0:T(8,128)(2,1)} %get-tuple-element.63.refs_0_), channel_id=1, source_target_pairs={{0,1},{1,2},{2,3},{4,5},{5,6},{6,7},{8,9},{9,10},{10,11},{12,13},{... | collective-permute-start | bytes 4718600 | tf_op jit(solution)/shard_map/ppermute | solution.py:179
  30.8 22.6 %collective-permute-done.7.down_ref.refs_1_.refs_2_ = bf16[384,2048]{1,0:T(8,128)(2,1)S(1)} collective-permute-done((bf16[384,2048]{1,0:T(8,128)(2,1)}, bf16[384,2048]{1,0:T(8,128)(2,1)S(1)}, u32[]{:S(2)}, u32[]{:S(2)}) %collective-permute-start.7) | collective-permute-done | bytes 1572896 | tf_op jit(solution)/shard_map/ppermute | solution.py:183
  56.0 4.3 %hops.3 = (bf16[384,2048]{1,0:T(8,128)(2,1)}, bf16[384,2048]{1,0:T(8,128)(2,1)}) custom-call(s32[3]{0:T(128)} %pad_add_fusion.1.ids_ref, bf16[1,384,8192]{2,1,0:T(8,128)(2,1)} %pending_ref.5, bf16[384,2048]{1,0:T(8,128)(2,1)} %collective-permute-done.8.up_ref.refs_2_.refs_1_, bf16[384,2048]{1,0:T(8,128)(2,1)} %copy-done.5, ...), custom_call_target="tpu_custom_call" | custom-call | bytes 1024 | tf_op jit(solution)/shard_map/hops/pallas_call | solution.py:286
  60.3 4.5 %near_plan.1.refs_0_.refs_2_ = bf16[768,2048]{1,0:T(8,128)(2,1)} custom-call(s32[3]{0:T(128)} %pad_add_fusion.1.ids_ref, bf16[384,2048]{1,0:T(8,128)(2,1)} %get-tuple-element.63.refs_0_, bf16[384,2048]{1,0:T(8,128)(2,1)} %copy-done.5, bf16[384,2048]{1,0:T(8,128)(2,1)} %collective-permute-done.8.up_ref.refs_2_.refs_1_, ...), custom_call_target="tpu_custom_call" | custom-call | bytes 1024 | tf_op jit(solution)/shard_map/near_plan/pallas_call | solution.py:218
  71.5 5.7 %collective-permute-start.11 = (bf16[384,2048]{1,0:T(8,128)(2,1)}, bf16[384,2048]{1,0:T(8,128)(2,1)}, u32[]{:S(2)}, u32[]{:S(2)}) collective-permute-start(bf16[384,2048]{1,0:T(8,128)(2,1)} %get-tuple-element.29.refs_3_), channel_id=1, source_target_pairs={{0,1},{1,2},{2,3},{4,5},{5,6},{6,7},{8,9},{9,10},{10,11},{12,13},{... | collective-permute-start | bytes 4718600 | tf_op jit(solution)/shard_map/ppermute | solution.py:179
  77.2 30.0 %collective-permute-done.10.down_ref.refs_0_ = bf16[384,2048]{1,0:T(8,128)(2,1)S(1)} collective-permute-done((bf16[384,2048]{1,0:T(8,128)(2,1)}, bf16[384,2048]{1,0:T(8,128)(2,1)S(1)}, u32[]{:S(2)}, u32[]{:S(2)}) %collective-permute-start.10) | collective-permute-done | bytes 1572896 | tf_op jit(solution)/shard_map/ppermute | solution.py:183
  108.5 4.3 %hops.4 = (bf16[384,2048]{1,0:T(8,128)(2,1)}, bf16[384,2048]{1,0:T(8,128)(2,1)}) custom-call(s32[3]{0:T(128)} %pad_add_fusion.1.ids_ref, bf16[1,384,8192]{2,1,0:T(8,128)(2,1)} %pending_ref.5, bf16[384,2048]{1,0:T(8,128)(2,1)} %collective-permute-done.11.up_ref.refs_1_, bf16[384,2048]{1,0:T(8,128)(2,1)} %copy-done.11), custom_call_target="tpu_custom_call" | custom-call | bytes 1024 | tf_op jit(solution)/shard_map/hops/pallas_call | solution.py:286
  125.7 6.1 %collective-permute-start.15 = (bf16[384,2048]{1,0:T(8,128)(2,1)}, bf16[384,2048]{1,0:T(8,128)(2,1)}, u32[]{:S(2)}, u32[]{:S(2)}) collective-permute-start(bf16[384,2048]{1,0:T(8,128)(2,1)} %gate.16), channel_id=1, source_target_pairs={{0,1},{1,2},{2,3},{4,5},{5,6},{6,7},{8,9},{9,10},{10,11},{12,13},{... | collective-permute-start | bytes 4718600 | tf_op jit(solution)/shard_map/ppermute | solution.py:179
  143.9 20.3 %collective-permute-done.15.up_ref.refs_3_ = bf16[384,2048]{1,0:T(8,128)(2,1)} collective-permute-done((bf16[384,2048]{1,0:T(8,128)(2,1)}, bf16[384,2048]{1,0:T(8,128)(2,1)}, u32[]{:S(2)}, u32[]{:S(2)}) %collective-permute-start.15) | collective-permute-done | bytes 1572896 | tf_op jit(solution)/shard_map/ppermute | solution.py:179
  164.2 5.3 %collective-permute-done.14.down_ref.refs_0_ = bf16[384,2048]{1,0:T(8,128)(2,1)} collective-permute-done((bf16[384,2048]{1,0:T(8,128)(2,1)}, bf16[384,2048]{1,0:T(8,128)(2,1)}, u32[]{:S(2)}, u32[]{:S(2)}) %collective-permute-start.14) | collective-permute-done | bytes 1572896 | tf_op jit(solution)/shard_map/ppermute | solution.py:183
  169.5 4.9 %hops.5 = (bf16[384,2048]{1,0:T(8,128)(2,1)}, bf16[384,2048]{1,0:T(8,128)(2,1)}) custom-call(s32[3]{0:T(128)} %pad_add_fusion.1.ids_ref, bf16[1,384,8192]{2,1,0:T(8,128)(2,1)} %pending_ref.5, bf16[384,2048]{1,0:T(8,128)(2,1)} %collective-permute-done.15.up_ref.refs_3_, bf16[384,2048]{1,0:T(8,128)(2,1)} %collective-permute-done.14.down_ref.refs_0_), custom_call_target="tpu_custom_call" | custom-call | bytes 1024 | tf_op jit(solution)/shard_map/hops/pallas_call | solution.py:286
  189.3 4.8 %prefix_plan.1.refs_4_ = bf16[2,6144,128]{2,1,0:T(8,128)(2,1)} custom-call(s32[3]{0:T(128)} %pad_add_fusion.1.ids_ref, bf16[1936,512]{1,0:T(8,128)(2,1)} %get-tuple-element.27.refs_8_.refs_0_, bf16[1936,512]{1,0:T(8,128)(2,1)} %gate.11.refs_9_.refs_1_, bf16[1936,512]{1,0:T(8,128)(2,1)} %gate.12.refs_10_.refs_2_, bf16[1936,512]{1,0:T(8,128)(2,1)} %copy-done.1, ...), custom_call_target="tpu_custom_call" | custom-call | bytes 1024 | tf_op jit(solution)/shard_map/prefix_plan/pallas_call | solution.py:218
  198.8 21.7 %project.1 = (bf16[4,768,128]{2,1,0:T(8,128)(2,1)}, bf16[2,768,128]{2,1,0:T(8,128)(2,1)}) custom-call(s32[7]{0:T(128)} %concatenate.59.ids_ref, bf16[768,2048]{1,0:T(8,128)(2,1)} %near_plan.1.refs_0_.refs_2_, bf16[768,2048]{1,0:T(8,128)(2,1)} %collective-permute-done.9.refs_1_.refs_3_, bf16[768,2048]{1,0:T(8,128)(2,1)} %near_plan.1.refs_0_.refs_2_, ...), custom_call_target="tpu_custom_call" | custom-call | bytes 1024 | tf_op jit(solution)/shard_map/project/pallas_call | solution.py:369
  225.9 4.0 %pieces_plan.1 = (bf16[512,512]{1,0:T(8,128)(2,1)}, bf16[512,512]{1,0:T(8,128)(2,1)}, bf16[512,512]{1,0:T(8,128)(2,1)}, bf16[512,512]{1,0:T(8,128)(2,1)}) custom-call(s32[3]{0:T(128)} %pad_add_fusion.1.ids_ref, bf16[512,512]{1,0:T(8,128)(2,1)} %get-tuple-element.32.refs_3_.refs_0_, bf16[512,512]{1,0:T(8,128)(2,1)} %copy-done.19, ...), custom_call_target="tpu_custom_call" | custom-call | bytes 1024 | tf_op jit(solution)/shard_map/pieces_plan/pallas_call | solution.py:218
  238.4 23.6 %attend.1.refs_4_.refs_0_ = bf16[768,512]{1,0:T(8,128)(2,1)} custom-call(s32[2,3]{1,0:T(2,128)} %pad_add_fusion.refs_0_, bf16[4,768,128]{2,1,0:T(8,128)(2,1)} %get-tuple-element.35.refs_4_.refs_1_, s32[768,128]{1,0:T(8,128)} %broadcast_in_dim.14.refs_2_, s32[768,128]{1,0:T(8,128)} %broadcast_in_dim.15.refs_3_, bf16[2,6144,128]{2,1,0:T(8,128)(2,1)} %prefix_plan.1.refs_4_, ...), custom_call_target="tpu_custom_call" | custom-call | bytes 1024 | tf_op jit(solution)/shard_map/attend/pallas_call | solution.py:480
  261.9 9.1 %collective-permute-done.31.refs_2_ = bf16[512,512]{1,0:T(8,128)(2,1)S(1)} collective-permute-done((bf16[512,512]{1,0:T(8,128)(2,1)}, bf16[512,512]{1,0:T(8,128)(2,1)S(1)}, u32[]{:S(2)}, u32[]{:S(2)}) %collective-permute-start.31) | collective-permute-done | bytes 524320 | tf_op jit(solution)/shard_map/ppermute | solution.py:753
  278.1 5.7 %collective-permute-start.34 = (bf16[1024,1024]{1,0:T(8,128)(2,1)}, bf16[1024,1024]{1,0:T(8,128)(2,1)}, u32[]{:S(2)}, u32[]{:S(2)}) collective-permute-start(bf16[1024,1024]{1,0:T(8,128)(2,1)} %block_plan.1.refs_8_), channel_id=1, source_target_pairs={{0,16},{4,20},{8,24},{12,28},{16,0},{20,4},{24,8},{28,12},{1,17},{... | collective-permute-start | bytes 6291464 | tf_op jit(solution)/shard_map/ppermute | solution.py:175
  285.0 6.6 %collective-permute-start.25 = (bf16[768,512]{1,0:T(8,128)(2,1)S(1)}, bf16[768,512]{1,0:T(8,128)(2,1)}, u32[]{:S(2)}, u32[]{:S(2)}) collective-permute-start(bf16[768,512]{1,0:T(8,128)(2,1)S(1)} %copy-done.8), channel_id=1, source_target_pairs={{0,1},{1,2},{2,3},{4,5},{5,6},{6,7},{8,9},{9,10},{10,11},{12,13},{... | collective-permute-start | bytes 2359304 | tf_op jit(solution)/shard_map/ppermute | solution.py:179
  291.7 12.5 %collective-permute-done.24.refs_0_.refs_2_ = bf16[768,512]{1,0:T(8,128)(2,1)S(1)} collective-permute-done((bf16[768,512]{1,0:T(8,128)(2,1)S(1)}, bf16[768,512]{1,0:T(8,128)(2,1)S(1)}, u32[]{:S(2)}, u32[]{:S(2)}) %collective-permute-start.24) | collective-permute-done | bytes 786464 | tf_op jit(solution)/shard_map/ppermute | solution.py:183
  310.1 12.6 %collective-permute-done.27.refs_0_ = bf16[768,512]{1,0:T(8,128)(2,1)} collective-permute-done((bf16[768,512]{1,0:T(8,128)(2,1)S(1)}, bf16[768,512]{1,0:T(8,128)(2,1)}, u32[]{:S(2)}, u32[]{:S(2)}) %collective-permute-start.27) | collective-permute-done | bytes 786464 | tf_op jit(solution)/shard_map/ppermute | solution.py:183
  337.9 15.5 %collective-permute-done.35.refs_0_ = bf16[768,512]{1,0:T(8,128)(2,1)} collective-permute-done((bf16[768,512]{1,0:T(8,128)(2,1)}, bf16[768,512]{1,0:T(8,128)(2,1)}, u32[]{:S(2)}, u32[]{:S(2)}) %collective-permute-start.35) | collective-permute-done | bytes 786464 | tf_op jit(solution)/shard_map/ppermute | solution.py:183
  361.9 12.9 %out_project.1 = (bf16[384,1024]{1,0:T(8,128)(2,1)}, bf16[384,1024]{1,0:T(8,128)(2,1)}) custom-call(s32[7]{0:T(128)} %concatenate.59.ids_ref, bf16[768,512]{1,0:T(8,128)(2,1)} %attend.1.refs_4_.refs_0_, bf16[768,512]{1,0:T(8,128)(2,1)} %collective-permute-done.23.refs_1_, bf16[768,512]{1,0:T(8,128)(2,1)} %pick_plan.7.refs_2_, ...), custom_call_target="tpu_custom_call" | custom-call | bytes 1024 | tf_op jit(solution)/shard_map/out_project/pallas_call | solution.py:562
  377.3 4.2 %fusion.1 = bf16[384,2048]{1,0:T(8,128)(2,1)} fusion(bf16[384,2048]{1,0:T(8,128)(2,1)S(1)} %copy-done.10, bf16[384,1024]{1,0:T(8,128)(2,1)S(1)} %collective-permute-done.40, bf16[384,1024]{1,0:T(8,128)(2,1)} %get-tuple-element.47, bf16[384,2048]{1,0:T(8,128)(2,1)} %collective-permute-done.22.refs_6_.refs_4_, ...), kind=kLoop, calls=%fused_computation.3 | loop fusion | flops 16515072 | bytes 9437191 | tf_op jit(solution)/shard_map/convert_element_type | solution.py:797
  (219 shorter events, 127.6 us)
Async XLA Ops:
  9.5 45.1 %collective-permute-start = (bf16[1936,512]{1,0:T(8,128)(2,1)}, bf16[1936,512]{1,0:T(8,128)(2,1)S(1)}, u32[]{:S(2)}, u32[]{:S(2)}) collective-permute-start(bf16[1936,512]{1,0:T(8,128)(2,1)} %get-tuple-element.28), channel_id=1, source_target_pairs={{0,4},{4,0},{8,12},{12,8},{16,20},{20,16},{24,28},{28,24},{1,5},{5... | collective-permute-start | bytes 5947400 | tf_op jit(solution)/shard_map/ppermute | solution.py:175
  13.6 39.7 %collective-permute-start.7 = (bf16[384,2048]{1,0:T(8,128)(2,1)}, bf16[384,2048]{1,0:T(8,128)(2,1)S(1)}, u32[]{:S(2)}, u32[]{:S(2)}) collective-permute-start(bf16[384,2048]{1,0:T(8,128)(2,1)} %get-tuple-element.63.refs_0_), channel_id=1, source_target_pairs={{3,2},{2,1},{1,0},{7,6},{6,5},{5,4},{11,10},{10,9},{9,8},{15,14},{... | collective-permute-start | bytes 4718600 | tf_op jit(solution)/shard_map/ppermute | solution.py:183
  14.9 39.7 %collective-permute-start.8 = (bf16[384,2048]{1,0:T(8,128)(2,1)}, bf16[384,2048]{1,0:T(8,128)(2,1)}, u32[]{:S(2)}, u32[]{:S(2)}) collective-permute-start(bf16[384,2048]{1,0:T(8,128)(2,1)} %get-tuple-element.63.refs_0_), channel_id=1, source_target_pairs={{0,1},{1,2},{2,3},{4,5},{5,6},{6,7},{8,9},{9,10},{10,11},{12,13},{... | collective-permute-start | bytes 4718600 | tf_op jit(solution)/shard_map/ppermute | solution.py:179
  21.2 45.6 %collective-permute-start.1 = (bf16[1936,512]{1,0:T(8,128)(2,1)}, bf16[1936,512]{1,0:T(8,128)(2,1)}, u32[]{:S(2)}, u32[]{:S(2)}) collective-permute-start(bf16[1936,512]{1,0:T(8,128)(2,1)} %get-tuple-element.27.refs_8_.refs_0_), channel_id=1, source_target_pairs={{0,8},{4,12},{8,0},{12,4},{16,24},{20,28},{24,16},{28,20},{1,9},{5... | collective-permute-start | bytes 5947400 | tf_op jit(solution)/shard_map/ppermute | solution.py:175
  23.2 45.0 %collective-permute-start.2 = (bf16[1936,512]{1,0:T(8,128)(2,1)}, bf16[1936,512]{1,0:T(8,128)(2,1)}, u32[]{:S(2)}, u32[]{:S(2)}) collective-permute-start(bf16[1936,512]{1,0:T(8,128)(2,1)} %get-tuple-element.27.refs_8_.refs_0_), channel_id=1, source_target_pairs={{0,16},{4,20},{8,24},{12,28},{16,0},{20,4},{24,8},{28,12},{1,17},{... | collective-permute-start | bytes 5947400 | tf_op jit(solution)/shard_map/ppermute | solution.py:175
  64.9 67.0 %collective-permute-start.9 = (bf16[768,2048]{1,0:T(8,128)(2,1)}, bf16[768,2048]{1,0:T(8,128)(2,1)}, u32[]{:S(2)}, u32[]{:S(2)}) collective-permute-start(bf16[768,2048]{1,0:T(8,128)(2,1)} %near_plan.1.refs_0_.refs_2_), channel_id=1, source_target_pairs={{0,4},{4,0},{8,12},{12,8},{16,20},{20,16},{24,28},{28,24},{1,5},{5... | collective-permute-start | bytes 9437192 | tf_op jit(solution)/shard_map/ppermute | solution.py:175
  68.2 52.9 %collective-permute-start.3 = (bf16[1936,512]{1,0:T(8,128)(2,1)}, bf16[1936,512]{1,0:T(8,128)(2,1)S(1)}, u32[]{:S(2)}, u32[]{:S(2)}) collective-permute-start(bf16[1936,512]{1,0:T(8,128)(2,1)} %gate.11.refs_9_.refs_1_), channel_id=1, source_target_pairs={{0,8},{4,12},{8,0},{12,4},{16,24},{20,28},{24,16},{28,20},{1,9},{5... | collective-permute-start | bytes 5947400 | tf_op jit(solution)/shard_map/ppermute | solution.py:175
  68.6 52.5 %collective-permute-start.4 = (bf16[1936,512]{1,0:T(8,128)(2,1)}, bf16[1936,512]{1,0:T(8,128)(2,1)}, u32[]{:S(2)}, u32[]{:S(2)}) collective-permute-start(bf16[1936,512]{1,0:T(8,128)(2,1)} %gate.11.refs_9_.refs_1_), channel_id=1, source_target_pairs={{0,16},{4,20},{8,24},{12,28},{16,0},{20,4},{24,8},{28,12},{1,17},{... | collective-permute-start | bytes 5947400 | tf_op jit(solution)/shard_map/ppermute | solution.py:175
  70.2 37.0 %collective-permute-start.10 = (bf16[384,2048]{1,0:T(8,128)(2,1)}, bf16[384,2048]{1,0:T(8,128)(2,1)S(1)}, u32[]{:S(2)}, u32[]{:S(2)}) collective-permute-start(bf16[384,2048]{1,0:T(8,128)(2,1)} %get-tuple-element.30), channel_id=1, source_target_pairs={{3,2},{2,1},{1,0},{7,6},{6,5},{5,4},{11,10},{10,9},{9,8},{15,14},{... | collective-permute-start | bytes 4718600 | tf_op jit(solution)/shard_map/ppermute | solution.py:183
  71.5 37.0 %collective-permute-start.11 = (bf16[384,2048]{1,0:T(8,128)(2,1)}, bf16[384,2048]{1,0:T(8,128)(2,1)}, u32[]{:S(2)}, u32[]{:S(2)}) collective-permute-start(bf16[384,2048]{1,0:T(8,128)(2,1)} %get-tuple-element.29.refs_3_), channel_id=1, source_target_pairs={{0,1},{1,2},{2,3},{4,5},{5,6},{6,7},{8,9},{9,10},{10,11},{12,13},{... | collective-permute-start | bytes 4718600 | tf_op jit(solution)/shard_map/ppermute | solution.py:179
  124.1 59.8 %collective-permute-start.5 = (bf16[1936,512]{1,0:T(8,128)(2,1)}, bf16[1936,512]{1,0:T(8,128)(2,1)S(1)}, u32[]{:S(2)}, u32[]{:S(2)}) collective-permute-start(bf16[1936,512]{1,0:T(8,128)(2,1)} %gate.12.refs_10_.refs_2_), channel_id=1, source_target_pairs={{0,16},{4,20},{8,24},{12,28},{16,0},{20,4},{24,8},{28,12},{1,17},{... | collective-permute-start | bytes 5947400 | tf_op jit(solution)/shard_map/ppermute | solution.py:175
  124.6 59.3 %collective-permute-start.6 = (bf16[1936,512]{1,0:T(8,128)(2,1)}, bf16[1936,512]{1,0:T(8,128)(2,1)}, u32[]{:S(2)}, u32[]{:S(2)}) collective-permute-start(bf16[1936,512]{1,0:T(8,128)(2,1)} %gate.13.refs_13_.refs_5_), channel_id=1, source_target_pairs={{0,8},{4,12},{8,0},{12,4},{16,24},{20,28},{24,16},{28,20},{1,9},{5... | collective-permute-start | bytes 5947400 | tf_op jit(solution)/shard_map/ppermute | solution.py:175
  125.7 38.6 %collective-permute-start.15 = (bf16[384,2048]{1,0:T(8,128)(2,1)}, bf16[384,2048]{1,0:T(8,128)(2,1)}, u32[]{:S(2)}, u32[]{:S(2)}) collective-permute-start(bf16[384,2048]{1,0:T(8,128)(2,1)} %gate.16), channel_id=1, source_target_pairs={{0,1},{1,2},{2,3},{4,5},{5,6},{6,7},{8,9},{9,10},{10,11},{12,13},{... | collective-permute-start | bytes 4718600 | tf_op jit(solution)/shard_map/ppermute | solution.py:179
  131.8 37.7 %collective-permute-start.14 = (bf16[384,2048]{1,0:T(8,128)(2,1)}, bf16[384,2048]{1,0:T(8,128)(2,1)}, u32[]{:S(2)}, u32[]{:S(2)}) collective-permute-start(bf16[384,2048]{1,0:T(8,128)(2,1)} %gate.15), channel_id=1, source_target_pairs={{3,2},{2,1},{1,0},{7,6},{6,5},{5,4},{11,10},{10,9},{9,8},{15,14},{... | collective-permute-start | bytes 4718600 | tf_op jit(solution)/shard_map/ppermute | solution.py:183
  178.8 46.2 %collective-permute-start.21 = (bf16[384,2048]{1,0:T(8,128)(2,1)}, bf16[384,2048]{1,0:T(8,128)(2,1)}, u32[]{:S(2)}, u32[]{:S(2)}) collective-permute-start(bf16[384,2048]{1,0:T(8,128)(2,1)} %get-tuple-element.34.refs_4_), channel_id=1, source_target_pairs={{0,1},{1,2},{2,3},{4,5},{5,6},{6,7},{8,9},{9,10},{10,11},{12,13},{... | collective-permute-start | bytes 4718600 | tf_op jit(solution)/shard_map/ppermute | solution.py:179
  182.4 42.6 %collective-permute-start.22 = (bf16[384,2048]{1,0:T(8,128)(2,1)}, bf16[384,2048]{1,0:T(8,128)(2,1)}, u32[]{:S(2)}, u32[]{:S(2)}) collective-permute-start(bf16[384,2048]{1,0:T(8,128)(2,1)} %get-tuple-element.40), channel_id=1, source_target_pairs={{3,2},{2,1},{1,0},{7,6},{6,5},{5,4},{11,10},{10,9},{9,8},{15,14},{... | collective-permute-start | bytes 4718600 | tf_op jit(solution)/shard_map/ppermute | solution.py:183
  185.2 36.2 %collective-permute-start.20 = (bf16[512,512]{1,0:T(8,128)(2,1)}, bf16[512,512]{1,0:T(8,128)(2,1)S(1)}, u32[]{:S(2)}, u32[]{:S(2)}) collective-permute-start(bf16[512,512]{1,0:T(8,128)(2,1)} %gate.19), channel_id=1, source_target_pairs={{0,24},{4,28},{8,16},{12,20},{16,8},{20,12},{24,0},{28,4},{1,25},{... | collective-permute-start | bytes 1572872 | tf_op jit(solution)/shard_map/ppermute | solution.py:175
  187.9 37.1 %collective-permute-start.19 = (bf16[512,512]{1,0:T(8,128)(2,1)}, bf16[512,512]{1,0:T(8,128)(2,1)S(1)}, u32[]{:S(2)}, u32[]{:S(2)}) collective-permute-start(bf16[512,512]{1,0:T(8,128)(2,1)} %gate.18), channel_id=1, source_target_pairs={{0,16},{4,20},{8,24},{12,28},{16,0},{20,4},{24,8},{28,12},{1,17},{... | collective-permute-start | bytes 1572872 | tf_op jit(solution)/shard_map/ppermute | solution.py:175
  195.0 30.0 %collective-permute-start.18 = (bf16[512,512]{1,0:T(8,128)(2,1)}, bf16[512,512]{1,0:T(8,128)(2,1)S(1)}, u32[]{:S(2)}, u32[]{:S(2)}) collective-permute-start(bf16[512,512]{1,0:T(8,128)(2,1)} %gate.17), channel_id=1, source_target_pairs={{0,8},{4,12},{8,0},{12,4},{16,24},{20,28},{24,16},{28,20},{1,9},{5... | collective-permute-start | bytes 1572872 | tf_op jit(solution)/shard_map/ppermute | solution.py:175
  229.9 32.0 %collective-permute-start.30 = (bf16[512,512]{1,0:T(8,128)(2,1)}, bf16[512,512]{1,0:T(8,128)(2,1)S(1)}, u32[]{:S(2)}, u32[]{:S(2)}) collective-permute-start(bf16[512,512]{1,0:T(8,128)(2,1)} %get-tuple-element.42), channel_id=1, source_target_pairs={{0,1},{1,0},{2,3},{3,2},{4,5},{5,4},{6,7},{7,6},{8,9},{9,8},{10,11... | collective-permute-start | bytes 1572872 | tf_op jit(solution)/shard_map/ppermute | solution.py:753
  232.6 38.4 %collective-permute-start.31 = (bf16[512,512]{1,0:T(8,128)(2,1)}, bf16[512,512]{1,0:T(8,128)(2,1)S(1)}, u32[]{:S(2)}, u32[]{:S(2)}) collective-permute-start(bf16[512,512]{1,0:T(8,128)(2,1)} %get-tuple-element.43), channel_id=1, source_target_pairs={{0,2},{1,3},{2,0},{3,1},{4,6},{5,7},{6,4},{7,5},{8,10},{9,11},{10,... | collective-permute-start | bytes 1572872 | tf_op jit(solution)/shard_map/ppermute | solution.py:753
  232.9 38.2 %collective-permute-start.32 = (bf16[512,512]{1,0:T(8,128)(2,1)}, bf16[512,512]{1,0:T(8,128)(2,1)S(1)}, u32[]{:S(2)}, u32[]{:S(2)}) collective-permute-start(bf16[512,512]{1,0:T(8,128)(2,1)} %get-tuple-element.44), channel_id=1, source_target_pairs={{0,3},{1,2},{2,1},{3,0},{4,7},{5,6},{6,5},{7,4},{8,11},{9,10},{10,... | collective-permute-start | bytes 1572872 | tf_op jit(solution)/shard_map/ppermute | solution.py:753
  276.4 49.4 %collective-permute-start.33 = (bf16[1024,1024]{1,0:T(8,128)(2,1)}, bf16[1024,1024]{1,0:T(8,128)(2,1)S(1)}, u32[]{:S(2)}, u32[]{:S(2)}) collective-permute-start(bf16[1024,1024]{1,0:T(8,128)(2,1)} %block_plan.1.refs_8_), channel_id=1, source_target_pairs={{0,8},{4,12},{8,0},{12,4},{16,24},{20,28},{24,16},{28,20},{1,9},{5... | collective-permute-start | bytes 6291464 | tf_op jit(solution)/shard_map/ppermute | solution.py:175
  278.1 50.1 %collective-permute-start.34 = (bf16[1024,1024]{1,0:T(8,128)(2,1)}, bf16[1024,1024]{1,0:T(8,128)(2,1)}, u32[]{:S(2)}, u32[]{:S(2)}) collective-permute-start(bf16[1024,1024]{1,0:T(8,128)(2,1)} %block_plan.1.refs_8_), channel_id=1, source_target_pairs={{0,16},{4,20},{8,24},{12,28},{16,0},{20,4},{24,8},{28,12},{1,17},{... | collective-permute-start | bytes 6291464 | tf_op jit(solution)/shard_map/ppermute | solution.py:175
  (55 other events, 460.8 us)

commit v2 on v1

--- a/solution.py
+++ b/solution.py
@@ -309,10 +309,19 @@
 AHEAD = 3
 
 
+def part_choices(r, z):
+    return (
+        [(None, 0, 0)],
+        [(None, 0, 1)],
+        [(None, 1, 0)],
+        [(z == 0, 3, 0), (z == 3, 2, 0), ((z == 1) | (z == 2), 0, 2)],
+    )[r]
+
+
 def project_kernel(scale, at_kv, ids_ref, *refs):
     xs, ws = refs[:8], refs[8:16]
     factor_ref, cos_ref, sin_ref, q_ref, kv_ref, x_buf, w_buf, x_sem, w_sem = refs[16:]
-    chip, core = ids_ref[0], ids_ref[1]
+    chip, core, z = ids_ref[0], ids_ref[1], ids_ref[2]
     tok, half, cols = xs[7].shape[0], x_buf.shape[-1], ws[0].shape[1]
     fold = half // 2
     mine = pl.multiple_of(core * tok, 128)
@@ -336,9 +345,15 @@
             waits.append(copy)
         features = pl.ds(pl.multiple_of((core ^ h) * half, 128), half)
         for s, rows in ((0, mine), (1, theirs)):
-            src = xs[2 * r + s].at[pl.ds(tok if r == 1 else 0, tok), features]
-            copy = pltpu.make_async_copy(src, x_buf.at[at, pl.ds(rows, tok)], x_sem.at[2 * at + s])
-            copy.start()
+            for cond, index, group in part_choices(r, z):
+                src = xs[2 * index + s].at[pl.ds(group * tok, tok), features]
+                copy = pltpu.make_async_copy(
+                    src, x_buf.at[at, pl.ds(rows, tok)], x_sem.at[2 * at + s]
+                )
+                if cond is None:
+                    copy.start()
+                else:
+                    pl.when(cond)(copy.start)
             waits.append(copy)
         return waits
 
@@ -402,18 +417,34 @@
     return new, acc
 
 
-def attend_kernel(
-    halo, bound_ref, q_ref, n_ref, lo_ref, kv_ref, k_ref, v_ref, out_ref, v_ext, s_ref, m_ref, acc_ref
-):
+def attend_kernel(halo, at_old, bound_ref, ids_ref, q_ref, n_ref, lo_ref, k_ref, v_ref, *refs):
+    bundles, (out_ref, k_old, v_ext, s_ref, m_ref, acc_ref, sems) = refs[:8], refs[-7:]
     b = pl.program_id(0)
     heads, bt = q_ref.shape[0], q_ref.shape[1]
     rows, chains = CHAIN * bt, heads // CHAIN
-    last = kv_ref.shape[1] // BK - 1
+    last = k_old.shape[0] // BK - 1
+    fold = k_old.shape[0] // (2 * N_CTX)
 
     @pl.when(b == 0)
     def _():
-        v_ext[:, :HD] = kv_ref[1]
-        v_ext[:, HD:] = jnp.ones_like(kv_ref[1])
+        copies = []
+        for index, bundle in enumerate(bundles):
+            place = ((ids_ref[0] ^ (index // 2)) * 2 + (ids_ref[1] ^ (index % 2))) * 2 * fold
+            for i in range(4):
+                dst = (k_old, v_ext)[i // 2]
+                to = pl.ds(pl.multiple_of(place + (i % 2) * fold, 128), fold)
+                copies.append(
+                    pltpu.make_async_copy(
+                        bundle.at[pl.ds(at_old, fold), pl.ds(i * HD, HD)],
+                        dst.at[to, pl.ds(0, HD)],
+                        sems.at[4 * index + i],
+                    )
+                )
+        for copy in copies:
+            copy.start()
+        v_ext[:, HD:] = jnp.ones((v_ext.shape[0], HD), jnp.bfloat16)
+        for copy in copies:
+            copy.wait()
 
     m_ref[...] = jnp.full_like(m_ref, MASKED)
     acc_ref[...] = jnp.zeros_like(acc_ref)
@@ -421,7 +452,7 @@
     def query(g):
         return q_ref[g * CHAIN : (g + 1) * CHAIN].reshape(rows, HD)
 
-    s_ref[...] = scores(query(0), kv_ref[0, :BK, :])
+    s_ref[...] = scores(query(0), k_old[:BK, :])
 
     def body(kb, masked):
         start = pl.multiple_of(kb * BK, BK)
@@ -432,7 +463,7 @@
         v = v_ext[pl.ds(start, BK), :]
         for g in range(chains):
             at, who = (start, g + 1) if g + 1 < chains else (follow, 0)
-            ahead = scores(query(who), kv_ref[0, pl.ds(at, BK), :])
+            ahead = scores(query(who), k_old[pl.ds(at, BK), :])
             if masked:
                 n_rows = jnp.concatenate([n_ref[:, :1]] * CHAIN, axis=0)
                 col = lax.broadcasted_iota(jnp.int32, s.shape, 1) + start
@@ -467,72 +498,55 @@
             out_ref[:, at : at + HD] = mixed[h * bt : (h + 1) * bt]
 
 
-def attend(bounds, q, n_tok, lo_tok, kv, k, v, arrived=()):
+def attend(bounds, ids, q, n_tok, lo_tok, k, v, bundles, at_old, keys, arrived=()):
     heads, tokens = q.shape[:2]
     chains, rows = heads // CHAIN, CHAIN * BT
-    keys = kv.shape[1]
     halo = k.shape[0] - tokens
-    count = len(arrived)
-
-    def kernel(*refs):
-        attend_kernel(halo, *refs[:7], *refs[7 + count :])
-
     return pl.pallas_call(
-        kernel,
+        functools.partial(attend_kernel, halo, at_old),
         out_shape=jax.ShapeDtypeStruct((tokens, heads * HD), jnp.bfloat16),
         grid_spec=pltpu.PrefetchScalarGridSpec(
-            num_scalar_prefetch=1,
+            num_scalar_prefetch=2,
             grid=(tokens // BT,),
             in_specs=[
                 pl.BlockSpec((heads, BT, HD), lambda b, *_: (0, b, 0)),
                 pl.BlockSpec((BT, 128), lambda b, *_: (b, 0)),
                 pl.BlockSpec((BT, 128), lambda b, *_: (b, 0)),
-                pl.BlockSpec((2, keys, HD), lambda b, *_: (0, 0, 0)),
                 pl.BlockSpec(k.shape, lambda b, *_: (0, 0)),
                 pl.BlockSpec(v.shape, lambda b, *_: (0, 0)),
             ]
+            + [HBM] * 8
             + specs_of(arrived),
             out_specs=pl.BlockSpec((BT, heads * HD), lambda b, *_: (b, 0)),
             scratch_shapes=[
+                pltpu.VMEM((keys, HD), jnp.bfloat16),
                 pltpu.VMEM((keys, 2 * HD), jnp.bfloat16),
                 pltpu.VMEM((rows, BK), jnp.float32),
                 pltpu.VMEM((chains, rows, 128), jnp.float32),
                 pltpu.VMEM((chains, rows, 2 * HD), jnp.float32),
+                pltpu.SemaphoreType.DMA((32,)),
             ],
         ),
         compiler_params=pltpu.CompilerParams(vmem_limit_bytes=GRANT),
         cost_estimate=LITTLE,
         name="attend",
-    )(bounds, q, n_tok, lo_tok, kv, k, v, *arrived)
+    )(bounds, ids, q, n_tok, lo_tok, k, v, *bundles, *arrived)
 
 
 def out_kernel(ids_ref, *refs):
-    xs, ws = refs[:8], refs[8:13]
-    keep_ref, give_ref, x_buf, w_buf, o_buf, x_sem, w_sem = refs[13:]
+    xs, ws = refs[:8], refs[8:16]
+    keep_ref, give_ref, x_buf, w_buf, o_buf, x_sem, w_sem = refs[16:]
     chip, core, z = ids_ref[0], ids_ref[1], ids_ref[2]
     width = xs[0].shape[1]
     rows = w_buf.shape[1] // 4
-    top = ws[3].shape[0]
     for r in range(4):
         near = ids_ref[3 + r] ^ z
         for m in range(4):
             to = w_buf.at[r, pl.ds(pl.multiple_of((chip ^ m) * rows, 128), rows)]
-            sem = w_sem.at[4 * r + m]
-            if m < 3:
-                src = ws[m].at[pl.ds(pl.multiple_of(near * rows, 128), rows)]
-                pltpu.make_async_copy(src, to, sem).start()
-            else:
-
-                @pl.when(near < 2)
-                def _():
-                    src = ws[3].at[pl.ds(pl.multiple_of(near * rows, 128), rows)]
-                    pltpu.make_async_copy(src, to, sem).start()
-
-                @pl.when(near >= 2)
-                def _():
-                    src = ws[4].at[pl.ds(pl.multiple_of(near * rows - top, 128), rows)]
-                    pltpu.make_async_copy(src, to, sem).start()
-
+            for i in range(2):
+                src = ws[2 * m + i].at[pl.ds(pl.multiple_of((near % 2) * rows, 128), rows)]
+                copy = pltpu.make_async_copy(src, to, w_sem.at[4 * r + m])
+                pl.when(near // 2 == i)(copy.start)
         for s in range(2):
             at = pl.multiple_of((core ^ s) * width, 128)
             pltpu.make_async_copy(
@@ -558,11 +572,11 @@
 
 def out_project(ids, xs, ws):
     tokens, width = xs[0].shape
-    depth, cols = ws[0].shape
+    depth, cols = 2 * ws[0].shape[0], ws[0].shape[1]
     return pl.pallas_call(
         out_kernel,
         out_shape=(jax.ShapeDtypeStruct((tokens // 2, cols), jnp.bfloat16),) * 2,
-        in_specs=[SMEM] + [HBM] * 13,
+        in_specs=[SMEM] + [HBM] * 16,
         out_specs=(VMEM, VMEM),
         scratch_shapes=[
             pltpu.VMEM((4, tokens, 2 * width), jnp.bfloat16),
@@ -605,7 +619,6 @@
 
     gain = lax.dynamic_slice_in_dim(norm_gain, z * feat, feat, 0).astype(jnp.float32)
     scaled = (wide * gain[None, :]).astype(jnp.bfloat16)
-    u1, d1 = hop_up(scaled, every), hop_down(scaled, every)
 
     labels = jnp.arange(NTRAJ, dtype=jnp.int32)
     counts = jnp.concatenate(
@@ -665,29 +678,11 @@
     ids = jnp.concatenate([here, places])
 
     x1, y1, given = swap(own, 2), swap(own, 4), swap(give, 1)
+    turn = swap(gate(notes, own), 1)
+    scaled = gate(scaled, turn)
+    u1, d1 = hop_up(scaled, every), hop_down(scaled, every)
     mine = squares(scaled, z)
 
-    up, down = hops(here, pending, u1, d1, 3, (1, 2, 3), (), (cosine, sinus, mine, given))
-    u2, d2 = hop_up(up, every), hop_down(down, every)
-
-    given = gate(given, x1, y1)
-    x2, y2 = swap(given, 2), swap(given, 4)
-
-    def near_plan(at, src, out):
-        yield one(src[0], out[0].at[pl.ds(0, tok)])
-        yield ([(at[2] < 2, src[1]), (at[2] >= 2, src[2])], out[0].at[pl.ds(tok, tok)])
-
-    (near,) = move(near_plan, ((chip_tok, feat),), here, (scaled, d1, u1), (up,))
-    over1 = swap(near, 1)
-    mine = mine + squares(near[tok:], places[1])
-    theirs = squares(over1[:tok], z) + squares(over1[tok:], places[1])
-
-    up, down = hops(here, pending, u2, d2, 2, (2,), (1,))
-    turn = swap(gate(notes, x2, y2), 1)
-    u3, d3 = hop_up(gate(up, turn), every), hop_down(gate(down, turn), every)
-
-    x1, y2 = gate(x1, x2, y2), gate(y2, x2)
-    far_own, far_other = swap(x1, 4), swap(y2, 2)
     def piece_plan(at, src, out):
         for r, dst in enumerate(out):
             rows = pl.ds(multiple(at[0] ^ r, n_piece), n_piece)
@@ -695,21 +690,56 @@
                 part = src[0].at[rows, pl.ds(i * q_cols, q_cols)]
                 yield one(part, dst.at[pl.ds(i * n_piece, n_piece)])
 
-    by_chip = move(piece_plan, ((2 * n_piece, q_cols),) * 4, here, (w_out,), (up,))
-    second = pick(z, (d2, d2, u2, u2), here, (up, by_chip[0]))
+    by_chip = move(
+        piece_plan,
+        ((2 * n_piece, q_cols),) * 4,
+        here,
+        (w_out,),
+        (own,),
+    )
+    up, down = hops(here, pending, u1, d1, 3, (1, 2, 3), (), (cosine, sinus, mine, given, by_chip[0]))
+    u2, d2 = hop_up(up, every), hop_down(down, every)
+
+    def near_plan(at, src, out):
+        own_part, up_part, down_part = src
+        low = at[2] < 2
+        high = at[2] >= 2
+        yield one(own_part, out[0].at[pl.ds(0, tok)])
+        yield ([(low, down_part), (high, up_part)], out[0].at[pl.ds(tok, tok)])
+        yield ([(low, up_part), (high, down_part)], out[0].at[pl.ds(2 * tok, tok)])
+
+    (near,) = move(near_plan, ((3 * tok, feat),), here, (scaled, u1, d1), (up,))
+    given = gate(given, x1, y1, near)
+    x2, y2 = swap(given, 2), swap(given, 4)
+    over1 = swap(near, 1)
+    mine = mine + squares(near[tok : 2 * tok], places[1])
+    theirs = squares(over1[:tok], z) + squares(over1[tok : 2 * tok], places[1])
+    mine_near = squares(near[2 * tok :], places[3])
+    theirs_near = squares(over1[2 * tok :], places[3])
+
+    up, down = hops(here, pending, u2, d2, 2, (2,), (1,))
+    second = pick(z, (d2, d2, u2, u2), here, (up,))
+    u3, d3 = hop_up(gate(up, second), every), hop_down(gate(down, second), every)
+    x1, y2 = gate(x1, x2, y2), gate(y2, x2)
+    far_own, far_other = swap(x1, 4), swap(y2, 2)
+
     over2 = swap(second, 1)
     mine = mine + squares(second, places[2])
-    up, down = hops(here, pending, u3, d3, 1, (), (1, 2, 3))
+    theirs = theirs + squares(over2, places[2])
+
+    su3, sd3 = swap(u3, 1), swap(d3, 1)
+    up, down = hops(here, pending, u3, d3, 1, (), (1, 2, 3), (over2, mine, theirs))
     u4, d4 = hop_up(up, every), hop_down(down, every)
-    third = pick(z, (d3, u1, d1, u3), here, (up, mine, theirs))
-    over3 = swap(third, 1)
-
-    mine = mine + squares(third, places[3])
-    theirs = theirs + squares(over2, places[2]) + squares(over3, places[3])
+    mine = mine + jnp.where(
+        z == 0, squares(d3, places[3]), jnp.where(z == 3, squares(u3, places[3]), mine_near)
+    )
+    theirs = theirs + jnp.where(
+        z == 0, squares(sd3, places[3]), jnp.where(z == 3, squares(su3, places[3]), theirs_near)
+    )
     total = jnp.where(first, jnp.concatenate([mine, theirs]), jnp.concatenate([theirs, mine]))
     factor = lax.rsqrt(total * (1.0 / depth) + NORM_EPSILON)
     factor = jnp.broadcast_to(factor, (chip_tok, 128))
-    xs = [near, over1, near, over1, second, over2, third, over3]
+    xs = [near, over1, second, over2, u3, su3, d3, sd3]
     own_rows = (own, given, x1, x2, y1, y2, far_own, far_other)
 
     said = [rows[n_both + n_kv : n_both + n_kv + 2].astype(jnp.float32) for rows in own_rows]
@@ -725,19 +755,8 @@
     n_wide = jnp.broadcast_to(n_tok[:, None], (chip_tok, 128))
     lo_wide = jnp.broadcast_to(lo_tok[:, None], (chip_tok, 128))
 
-    def prefix_plan(at, src, out):
-        for m in range(4):
-            for j in range(2):
-                start = ((at[0] ^ m) * 2 + (at[1] ^ j)) * 2 * fold
-                rows = src[2 * m + j]
-                for i in range(4):
-                    dst = out[0].at[i // 2, pl.ds(pl.multiple_of(start + (i % 2) * fold, 128), fold)]
-                    yield one(rows.at[pl.ds(n_q, fold), pl.ds(i * HD, HD)], dst)
-
-    (kv,) = move(prefix_plan, ((2, N_CTX * 2 * fold, HD),), here, own_rows, (third,))
-
     by_chip = (by_chip[0],) + tuple(
-        swap(gate(by_chip[r], far_own, far_other, over2), 2 * r) for r in (1, 2, 3)
+        swap(gate(by_chip[r], far_own, far_other), 2 * r) for r in (1, 2, 3)
     )
     scale = math.log2(math.e) / math.sqrt(HD)
     q, kv_new = project(ids, xs, own_rows, n_both, factor, cosine, sinus, scale)
@@ -753,32 +772,39 @@
         pieces[r] = lax.ppermute(pieces[r], "tp", [(i, i ^ r) for i in range(N_TP)])
     k_near = jnp.concatenate([before[0], kv_new[0]], axis=0)
     v_near = jnp.concatenate([before[1], kv_new[1]], axis=0)
-    attended = attend(bounds, q, n_wide, lo_wide, kv, k_near, v_near, (pieces[0],))
+    attended = attend(
+        bounds,
+        here,
+        q,
+        n_wide,
+        lo_wide,
+        k_near,
+        v_near,
+        own_rows,
+        n_q,
+        N_CTX * prefix_keys.shape[1],
+        (pieces[0],),
+    )
 
     def block_plan(at, src, out):
         for r, part in enumerate(src):
             for i in range(2):
-                dst = out[0].at[pl.ds(r * n_piece, n_piece), pl.ds(i * q_cols, q_cols)]
+                dst = out[r // 2].at[pl.ds((r % 2) * n_piece, n_piece), pl.ds(i * q_cols, q_cols)]
                 yield one(part.at[pl.ds(i * n_piece, n_piece)], dst)
 
-    (block,) = move(block_plan, ((4 * n_piece, 2 * q_cols),), here, pieces, (attended,))
-    half = block.shape[0] // 2
-    wo_x, wo_y = swap(block, 2), swap(block, 4)
+    wo_a, wo_b = move(block_plan, ((2 * n_piece, 2 * q_cols),) * 2, here, pieces, (attended,))
+    wo_xa, wo_yb = swap(wo_a, 2), swap(wo_b, 4)
+    wo_xb, wo_ya = swap(wo_b, 2), swap(wo_a, 4)
+
+    attended = gate(attended, *pieces[1:])
     u1, d1 = hop_up(attended, every), hop_down(attended, every)
     near = pick(z, (d1, d1, u1, u1), here)
 
-    def far_plan(at, src, out):
-        yield one(src[0].at[pl.ds(0, half)], out[0])
-        yield one(src[1].at[pl.ds(half, half)], out[1])
-
-    to_y, to_x = move(
-        far_plan, ((half, block.shape[1]),) * 2, here, (wo_x, wo_y), (near, u4, d4)
-    )
-    wo_parts = (block, wo_x, wo_y, swap(to_y, 4), swap(to_x, 2))
-    u2, d2 = hop_up(u1, (1, 2)), hop_down(d1, (1, 2))
+    wo_parts = (wo_a, wo_b, wo_xa, wo_xb, wo_ya, wo_yb, swap(wo_xa, 4), swap(wo_yb, 2))
+    u2, d2 = hop_up(gate(u1, wo_xa, wo_yb), (1, 2)), hop_down(gate(d1, wo_xa, wo_yb), (1, 2))
     second = pick(z, (d2, d2, u2, u2), here)
-    u3, d3 = hop_up(gate(u2, to_y), (2,)), hop_down(gate(d2, to_y), (2,))
-    third = pick(z, (d3, u1, d1, u3), here)
+    u3, d3 = hop_up(gate(u2, wo_xb, wo_ya), (2,)), hop_down(gate(d2, wo_xb, wo_ya), (2,))
+    third = pick(z, (d3, u1, d1, u3), here, wo_parts[6:])
     hs = []
     for part in (attended, near, second, third):
         hs += [part, swap(part, 1)]

time: 385 us -> 386 us (level)
  Pallas kernels: 118 us -> 104 us
  waiting for transfers between devices: 143 us -> 155 us
  local copies, waits for them, and re-layouts: 18.2 us -> 22.7 us
    ppermute x7, waiting for transfers between devices: 98.5 us -> 59.3 us  [hop_down(): return lax.ppermute(v, 'tp', [(N_TP - 1 - i, N_TP - 2 - i) for i in pairs])]
    ppermute x23 -> x26, waiting for transfers between devices: 12.8 us -> 40.6 us  [swap(): return lax.ppermute(x, 'ctx', [(c, c ^ bit) for c in range(N_CTX)])]
    ppermute x7, waiting for transfers between devices: 22.9 us -> 46.6 us  [hop_up(): return lax.ppermute(v, 'tp', [(i, i + 1) for i in pairs])]
    pallas_call x12 -> x9, Pallas kernels: 46.3 us -> 34.7 us  [move(): pl.pallas_call(kernel, out_shape=tuple((jax.ShapeDtypeStruct(shape, jnp.b...]
    ppermute x7, starting transfers between devices: 30.9 us -> 26.2 us  [hop_up(): return lax.ppermute(v, 'tp', [(i, i + 1) for i in pairs])]
    unnamed x76 -> x72, local copies, waits for them, and re-layouts: 7.26 us -> 11 us
    ppermute x23 -> x26, starting transfers between devices: 23.2 us -> 25.7 us  [swap(): return lax.ppermute(x, 'ctx', [(c, c ^ bit) for c in range(N_CTX)])]
    reduce_sum x4 -> x3, other arithmetic: 11.1 us -> 10.6 us  [squares(): jnp.sum(jnp.square(part.astype(jnp.float32) / g[None, :]), axis=1, keepdi...]
  transfers between devices with their start and end apart: 41 -> 44, of which waited for: 16 -> 20; matrix products, arithmetic and copies ran while one was open for 8% -> 9% of each run, Pallas kernels for 24% -> 21%
where the time goes in v2:
time: 386 us; the launch traced here: 384 us
  waiting for transfers between devices  155 us (40%)
  Pallas kernels  104 us (27%)
  starting transfers between devices  69.7 us (18%)
  other arithmetic  30.9 us (8%)
  local copies, waits for them, and re-layouts  22.7 us (6%)
    ppermute x7, waiting for transfers between devices, hop_down(): return lax.ppermute(v, 'tp', [(N_TP - 1 - i, N_TP - 2 - i) for i in pairs])  59.3 us
    ppermute x7, waiting for transfers between devices, hop_up(): return lax.ppermute(v, 'tp', [(i, i + 1) for i in pairs])  46.6 us
    ppermute x26, waiting for transfers between devices, swap(): return lax.ppermute(x, 'ctx', [(c, c ^ bit) for c in range(N_CTX)])  40.6 us
    pallas_call x9, Pallas kernels, move(): pl.pallas_call(kernel, out_shape=tuple((jax.ShapeDtypeStruct(shape, jnp.b...  34.7 us
    ppermute x7, starting transfers between devices, hop_up(): return lax.ppermute(v, 'tp', [(i, i + 1) for i in pairs])  26.2 us
    ppermute x26, starting transfers between devices, swap(): return lax.ppermute(x, 'ctx', [(c, c ^ bit) for c in range(N_CTX)])  25.7 us
    pallas_call x1, Pallas kernels, project(): pl.pallas_call(functools.partial(project_kernel, scale, at_kv), out_shape...  21.5 us
    pallas_call x1, Pallas kernels, attend(): pl.pallas_call(functools.partial(attend_kernel, halo, at_old), out_shape=...  21.2 us
  transfers between devices with their start and end apart: 44, of which 20 were waited for; matrix products, arithmetic and copies ran while one was open for 9% of the time, Pallas kernels for 21%

profile of v2, /device:TPU:0, one launch (start us, length us, event | category | flops | bytes accessed | tf_op | source)
XLA Modules:
  0.0 384.1 jit_solution(10563484240356785564)
XLA Ops:
  4.4 5.0 %first_plan.1 = (bf16[1936,512]{1,0:T(8,128)(2,1)}, bf16[1936,512]{1,0:T(8,128)(2,1)}) custom-call(s32[3]{0:T(128)} %pad_add_fusion.1.ids_ref, bf16[1024,1024]{1,0:T(8,128)(2,1)} %refs_0_.2, bf16[1024,1024]{1,0:T(8,128)(2,1)} %refs_1_.1, bf16[1024,1024]{1,0:T(8,128)(2,1)} %refs_2_.1, bf16[8,768,128]{2,1,0:T(8,128)(2,1)} %refs_3_.1, ...), custom_call_target="tpu_custom_call" | custom-call | bytes 1024 | tf_op jit(solution)/shard_map/first_plan/pallas_call | solution.py:218
  17.9 4.6 %collective-permute-start.4 = (bf16[384,2048]{1,0:T(8,128)(2,1)}, bf16[384,2048]{1,0:T(8,128)(2,1)}, u32[]{:S(2)}, u32[]{:S(2)}) collective-permute-start(bf16[384,2048]{1,0:T(8,128)(2,1)} %gate.16.refs_0_), channel_id=1, source_target_pairs={{0,1},{1,2},{2,3},{4,5},{5,6},{6,7},{8,9},{9,10},{10,11},{12,13},{... | collective-permute-start | bytes 4718600 | tf_op jit(solution)/shard_map/ppermute | solution.py:179
  33.0 22.8 %collective-permute-done.4.up_ref.refs_1_ = bf16[384,2048]{1,0:T(8,128)(2,1)} collective-permute-done((bf16[384,2048]{1,0:T(8,128)(2,1)}, bf16[384,2048]{1,0:T(8,128)(2,1)}, u32[]{:S(2)}, u32[]{:S(2)}) %collective-permute-start.4) | collective-permute-done | bytes 1572896 | tf_op jit(solution)/shard_map/ppermute | solution.py:179
  55.8 5.2 %collective-permute-done.5.down_ref.refs_2_ = bf16[384,2048]{1,0:T(8,128)(2,1)} collective-permute-done((bf16[384,2048]{1,0:T(8,128)(2,1)}, bf16[384,2048]{1,0:T(8,128)(2,1)}, u32[]{:S(2)}, u32[]{:S(2)}) %collective-permute-start.5) | collective-permute-done | bytes 1572896 | tf_op jit(solution)/shard_map/ppermute | solution.py:183
  62.4 4.3 %hops.3 = (bf16[384,2048]{1,0:T(8,128)(2,1)}, bf16[384,2048]{1,0:T(8,128)(2,1)}) custom-call(s32[3]{0:T(128)} %pad_add_fusion.1.ids_ref, bf16[1,384,8192]{2,1,0:T(8,128)(2,1)} %pending_ref.5, bf16[384,2048]{1,0:T(8,128)(2,1)} %collective-permute-done.4.up_ref.refs_1_, bf16[384,2048]{1,0:T(8,128)(2,1)} %collective-permute-done.5.down_ref.refs_2_, ...), custom_call_target="tpu_custom_call" | custom-call | bytes 1024 | tf_op jit(solution)/shard_map/hops/pallas_call | solution.py:286
  68.0 5.8 %collective-permute-start.12 = (bf16[384,2048]{1,0:T(8,128)(2,1)}, bf16[384,2048]{1,0:T(8,128)(2,1)}, u32[]{:S(2)}, u32[]{:S(2)}) collective-permute-start(bf16[384,2048]{1,0:T(8,128)(2,1)} %get-tuple-element.30.refs_3_), channel_id=1, source_target_pairs={{0,1},{1,2},{2,3},{4,5},{5,6},{6,7},{8,9},{9,10},{10,11},{12,13},{... | collective-permute-start | bytes 4718600 | tf_op jit(solution)/shard_map/ppermute | solution.py:179
  73.8 5.5 %near_plan.1.refs_3_.refs_0_ = bf16[1152,2048]{1,0:T(8,128)(2,1)} custom-call(s32[3]{0:T(128)} %pad_add_fusion.1.ids_ref, bf16[384,2048]{1,0:T(8,128)(2,1)} %gate.16.refs_0_, bf16[384,2048]{1,0:T(8,128)(2,1)} %collective-permute-done.4.up_ref.refs_1_, bf16[384,2048]{1,0:T(8,128)(2,1)} %collective-permute-done.5.down_ref.refs_2_, ...), custom_call_target="tpu_custom_call" | custom-call | bytes 1024 | tf_op jit(solution)/shard_map/near_plan/pallas_call | solution.py:218
  80.5 24.0 %collective-permute-done.11.down_ref.refs_0_ = bf16[384,2048]{1,0:T(8,128)(2,1)} collective-permute-done((bf16[384,2048]{1,0:T(8,128)(2,1)}, bf16[384,2048]{1,0:T(8,128)(2,1)}, u32[]{:S(2)}, u32[]{:S(2)}) %collective-permute-start.11) | collective-permute-done | bytes 1572896 | tf_op jit(solution)/shard_map/ppermute | solution.py:183
  113.6 6.1 %collective-permute-start.14 = (bf16[384,2048]{1,0:T(8,128)(2,1)}, bf16[384,2048]{1,0:T(8,128)(2,1)}, u32[]{:S(2)}, u32[]{:S(2)}) collective-permute-start(bf16[384,2048]{1,0:T(8,128)(2,1)} %gate.20), channel_id=1, source_target_pairs={{0,1},{1,2},{2,3},{4,5},{5,6},{6,7},{8,9},{9,10},{10,11},{12,13},{... | collective-permute-start | bytes 4718600 | tf_op jit(solution)/shard_map/ppermute | solution.py:179
  130.5 22.6 %collective-permute-done.14.refs_4_.up_ref = bf16[384,2048]{1,0:T(8,128)(2,1)} collective-permute-done((bf16[384,2048]{1,0:T(8,128)(2,1)}, bf16[384,2048]{1,0:T(8,128)(2,1)}, u32[]{:S(2)}, u32[]{:S(2)}) %collective-permute-start.14) | collective-permute-done | bytes 1572896 | tf_op jit(solution)/shard_map/ppermute | solution.py:179
  153.1 6.6 %collective-permute-done.16.refs_6_.down_ref = bf16[384,2048]{1,0:T(8,128)(2,1)} collective-permute-done((bf16[384,2048]{1,0:T(8,128)(2,1)}, bf16[384,2048]{1,0:T(8,128)(2,1)}, u32[]{:S(2)}, u32[]{:S(2)}) %collective-permute-start.16) | collective-permute-done | bytes 1572896 | tf_op jit(solution)/shard_map/ppermute | solution.py:183
  163.9 8.2 %collective-permute-done.8.refs_14_.refs_1_.refs_6_ = bf16[1936,512]{1,0:T(8,128)(2,1)S(1)} collective-permute-done((bf16[1936,512]{1,0:T(8,128)(2,1)}, bf16[1936,512]{1,0:T(8,128)(2,1)S(1)}, u32[]{:S(2)}, u32[]{:S(2)}) %collective-permute-start.8) | collective-permute-done | bytes 1982496 | tf_op jit(solution)/shard_map/ppermute | solution.py:175
  177.8 7.2 %multiply_reduce_fusion.7 = (f32[384]{0:T(512)S(1)}, f32[384]{0:T(512)S(1)}, f32[384]{0:T(512)S(1)}, f32[384]{0:T(512)S(1)}, f32[384]{0:T(512)S(1)}, /*index=5*/...) fusion(bf16[384,2048]{1,0:T(8,128)(2,1)} %collective-permute-done.14.refs_4_.up_ref, ...), kind=kLoop, calls=%fused_computation.14 | loop fusion | flops 28308096 | bytes 14194176 | tf_op jit(solution)/shard_map/reduce_sum | solution.py:646
  186.8 5.0 %hops.5 = (bf16[384,2048]{1,0:T(8,128)(2,1)}, bf16[384,2048]{1,0:T(8,128)(2,1)}) custom-call(s32[3]{0:T(128)} %pad_add_fusion.1.ids_ref, bf16[1,384,8192]{2,1,0:T(8,128)(2,1)} %pending_ref.5, bf16[384,2048]{1,0:T(8,128)(2,1)} %collective-permute-done.14.refs_4_.up_ref, bf16[384,2048]{1,0:T(8,128)(2,1)} %collective-permute-done.16.refs_6_.down_ref, ...), custom_call_target="tpu_custom_call" | custom-call | bytes 1024 | tf_op jit(solution)/shard_map/hops/pallas_call | solution.py:286
  197.8 21.5 %project.1 = (bf16[4,768,128]{2,1,0:T(8,128)(2,1)}, bf16[2,768,128]{2,1,0:T(8,128)(2,1)}) custom-call(s32[7]{0:T(128)} %concatenate.59.ids_ref, bf16[1152,2048]{1,0:T(8,128)(2,1)} %near_plan.1.refs_3_.refs_0_, bf16[1152,2048]{1,0:T(8,128)(2,1)} %collective-permute-done.10.refs_1_, bf16[384,2048]{1,0:T(8,128)(2,1)} %pick_plan.4.refs_1_.refs_2_, ...), custom_call_target="tpu_custom_call" | custom-call | bytes 1024 | tf_op jit(solution)/shard_map/project/pallas_call | solution.py:384
  246.3 21.2 %attend.1.refs_0_.refs_4_ = bf16[768,512]{1,0:T(8,128)(2,1)} custom-call(s32[2,3]{1,0:T(2,128)} %pad_add_fusion.bound_ref, s32[3]{0:T(128)} %pad_add_fusion.1.ids_ref, bf16[4,768,128]{2,1,0:T(8,128)(2,1)} %get-tuple-element.34.refs_4_.q_ref, s32[768,128]{1,0:T(8,128)} %broadcast_in_dim.14.n_ref, s32[768,128]{1,0:T(8,128)} %broadcast_in_dim.15.lo_ref, ...), custom_call_target="tpu_custom_call" | custom-call | bytes 1024 | tf_op jit(solution)/shard_map/attend/pallas_call | solution.py:505
  267.6 8.6 %collective-permute-done.25.refs_2_ = bf16[512,512]{1,0:T(8,128)(2,1)S(1)} collective-permute-done((bf16[512,512]{1,0:T(8,128)(2,1)}, bf16[512,512]{1,0:T(8,128)(2,1)S(1)}, u32[]{:S(2)}, u32[]{:S(2)}) %collective-permute-start.25) | collective-permute-done | bytes 524320 | tf_op jit(solution)/shard_map/ppermute | solution.py:772
  283.2 8.9 %collective-permute-start.32 = (bf16[512,1024]{1,0:T(8,128)(2,1)}, bf16[512,1024]{1,0:T(8,128)(2,1)S(1)}, u32[]{:S(2)}, u32[]{:S(2)}) collective-permute-start(bf16[512,1024]{1,0:T(8,128)(2,1)} %get-tuple-element.46.refs_9_), channel_id=1, source_target_pairs={{0,16},{4,20},{8,24},{12,28},{16,0},{20,4},{24,8},{28,12},{1,17},{... | collective-permute-start | bytes 3145736 | tf_op jit(solution)/shard_map/ppermute | solution.py:175
  293.4 4.6 %collective-permute-start.29 = (bf16[768,512]{1,0:T(8,128)(2,1)}, bf16[768,512]{1,0:T(8,128)(2,1)S(1)}, u32[]{:S(2)}, u32[]{:S(2)}) collective-permute-start(bf16[768,512]{1,0:T(8,128)(2,1)} %gate.25.refs_0_), channel_id=1, source_target_pairs={{0,1},{1,2},{2,3},{4,5},{5,6},{6,7},{8,9},{9,10},{10,11},{12,13},{... | collective-permute-start | bytes 2359304 | tf_op jit(solution)/shard_map/ppermute | solution.py:179
  298.2 11.4 %collective-permute-done.28.refs_0_.refs_2_ = bf16[768,512]{1,0:T(8,128)(2,1)S(1)} collective-permute-done((bf16[768,512]{1,0:T(8,128)(2,1)}, bf16[768,512]{1,0:T(8,128)(2,1)S(1)}, u32[]{:S(2)}, u32[]{:S(2)}) %collective-permute-start.28) | collective-permute-done | bytes 786464 | tf_op jit(solution)/shard_map/ppermute | solution.py:183
  310.8 5.5 %collective-permute-done.32.refs_2_.refs_13_ = bf16[512,1024]{1,0:T(8,128)(2,1)S(1)} collective-permute-done((bf16[512,1024]{1,0:T(8,128)(2,1)}, bf16[512,1024]{1,0:T(8,128)(2,1)S(1)}, u32[]{:S(2)}, u32[]{:S(2)}) %collective-permute-start.32) | collective-permute-done | bytes 1048608 | tf_op jit(solution)/shard_map/ppermute | solution.py:175
  323.6 7.9 %collective-permute-done.33.refs_0_ = bf16[768,512]{1,0:T(8,128)(2,1)} collective-permute-done((bf16[768,512]{1,0:T(8,128)(2,1)}, bf16[768,512]{1,0:T(8,128)(2,1)}, u32[]{:S(2)}, u32[]{:S(2)}) %collective-permute-start.33) | collective-permute-done | bytes 786464 | tf_op jit(solution)/shard_map/ppermute | solution.py:183
  344.9 12.0 %collective-permute-done.40.refs_4_.refs_14_ = bf16[512,1024]{1,0:T(8,128)(2,1)} collective-permute-done((bf16[512,1024]{1,0:T(8,128)(2,1)S(1)}, bf16[512,1024]{1,0:T(8,128)(2,1)}, u32[]{:S(2)}, u32[]{:S(2)}) %collective-permute-start.40) | collective-permute-done | bytes 1048608 | tf_op jit(solution)/shard_map/ppermute | solution.py:175
  364.1 13.2 %out_project.1 = (bf16[384,1024]{1,0:T(8,128)(2,1)}, bf16[384,1024]{1,0:T(8,128)(2,1)}) custom-call(s32[7]{0:T(128)} %concatenate.59.ids_ref, bf16[768,512]{1,0:T(8,128)(2,1)} %gate.25.refs_0_, bf16[768,512]{1,0:T(8,128)(2,1)} %collective-permute-done.27.refs_1_, bf16[768,512]{1,0:T(8,128)(2,1)} %pick_plan.5.refs_2_, ...), custom_call_target="tpu_custom_call" | custom-call | bytes 1024 | tf_op jit(solution)/shard_map/out_project/pallas_call | solution.py:576
  (221 shorter events, 134.9 us)
Async XLA Ops:
  9.4 70.0 %collective-permute-start.1 = (bf16[1936,512]{1,0:T(8,128)(2,1)}, bf16[1936,512]{1,0:T(8,128)(2,1)}, u32[]{:S(2)}, u32[]{:S(2)}) collective-permute-start(bf16[1936,512]{1,0:T(8,128)(2,1)} %get-tuple-element.27.refs_1_.refs_8_.refs_0_), channel_id=1, source_target_pairs={{0,8},{4,12},{8,0},{12,4},{16,24},{20,28},{24,16},{28,20},{1,9},{5... | collective-permute-start | bytes 5947400 | tf_op jit(solution)/shard_map/ppermute | solution.py:175
  12.4 67.0 %collective-permute-start.2 = (bf16[1936,512]{1,0:T(8,128)(2,1)}, bf16[1936,512]{1,0:T(8,128)(2,1)}, u32[]{:S(2)}, u32[]{:S(2)}) collective-permute-start(bf16[1936,512]{1,0:T(8,128)(2,1)} %get-tuple-element.27.refs_1_.refs_8_.refs_0_), channel_id=1, source_target_pairs={{0,16},{4,20},{8,24},{12,28},{16,0},{20,4},{24,8},{28,12},{1,17},{... | collective-permute-start | bytes 5947400 | tf_op jit(solution)/shard_map/ppermute | solution.py:175
  13.9 47.2 %collective-permute-start = (bf16[1936,512]{1,0:T(8,128)(2,1)}, bf16[1936,512]{1,0:T(8,128)(2,1)S(1)}, u32[]{:S(2)}, u32[]{:S(2)}) collective-permute-start(bf16[1936,512]{1,0:T(8,128)(2,1)} %get-tuple-element.28), channel_id=1, source_target_pairs={{0,4},{4,0},{8,12},{12,8},{16,20},{20,16},{24,28},{28,24},{1,5},{5... | collective-permute-start | bytes 5947400 | tf_op jit(solution)/shard_map/ppermute | solution.py:175
  17.9 38.0 %collective-permute-start.4 = (bf16[384,2048]{1,0:T(8,128)(2,1)}, bf16[384,2048]{1,0:T(8,128)(2,1)}, u32[]{:S(2)}, u32[]{:S(2)}) collective-permute-start(bf16[384,2048]{1,0:T(8,128)(2,1)} %gate.16.refs_0_), channel_id=1, source_target_pairs={{0,1},{1,2},{2,3},{4,5},{5,6},{6,7},{8,9},{9,10},{10,11},{12,13},{... | collective-permute-start | bytes 4718600 | tf_op jit(solution)/shard_map/ppermute | solution.py:179
  22.5 38.6 %collective-permute-start.5 = (bf16[384,2048]{1,0:T(8,128)(2,1)}, bf16[384,2048]{1,0:T(8,128)(2,1)}, u32[]{:S(2)}, u32[]{:S(2)}) collective-permute-start(bf16[384,2048]{1,0:T(8,128)(2,1)} %gate.16.refs_0_), channel_id=1, source_target_pairs={{3,2},{2,1},{1,0},{7,6},{6,5},{5,4},{11,10},{10,9},{9,8},{15,14},{... | collective-permute-start | bytes 4718600 | tf_op jit(solution)/shard_map/ppermute | solution.py:183
  66.7 37.7 %collective-permute-start.11 = (bf16[384,2048]{1,0:T(8,128)(2,1)}, bf16[384,2048]{1,0:T(8,128)(2,1)}, u32[]{:S(2)}, u32[]{:S(2)}) collective-permute-start(bf16[384,2048]{1,0:T(8,128)(2,1)} %get-tuple-element.31), channel_id=1, source_target_pairs={{3,2},{2,1},{1,0},{7,6},{6,5},{5,4},{11,10},{10,9},{9,8},{15,14},{... | collective-permute-start | bytes 4718600 | tf_op jit(solution)/shard_map/ppermute | solution.py:183
  68.0 37.6 %collective-permute-start.12 = (bf16[384,2048]{1,0:T(8,128)(2,1)}, bf16[384,2048]{1,0:T(8,128)(2,1)}, u32[]{:S(2)}, u32[]{:S(2)}) collective-permute-start(bf16[384,2048]{1,0:T(8,128)(2,1)} %get-tuple-element.30.refs_3_), channel_id=1, source_target_pairs={{0,1},{1,2},{2,3},{4,5},{5,6},{6,7},{8,9},{9,10},{10,11},{12,13},{... | collective-permute-start | bytes 4718600 | tf_op jit(solution)/shard_map/ppermute | solution.py:179
  79.3 44.0 %collective-permute-start.6 = (bf16[1936,512]{1,0:T(8,128)(2,1)}, bf16[1936,512]{1,0:T(8,128)(2,1)S(1)}, u32[]{:S(2)}, u32[]{:S(2)}) collective-permute-start(bf16[1936,512]{1,0:T(8,128)(2,1)} %gate.17.refs_9_.refs_1_), channel_id=1, source_target_pairs={{0,8},{4,12},{8,0},{12,4},{16,24},{20,28},{24,16},{28,20},{1,9},{5... | collective-permute-start | bytes 5947400 | tf_op jit(solution)/shard_map/ppermute | solution.py:175
  80.0 97.8 %collective-permute-start.10 = (bf16[1152,2048]{1,0:T(8,128)(2,1)}, bf16[1152,2048]{1,0:T(8,128)(2,1)}, u32[]{:S(2)}, u32[]{:S(2)}) collective-permute-start(bf16[1152,2048]{1,0:T(8,128)(2,1)} %near_plan.1.refs_3_.refs_0_), channel_id=1, source_target_pairs={{0,4},{4,0},{8,12},{12,8},{16,20},{20,16},{24,28},{28,24},{1,5},{5... | collective-permute-start | bytes 14155784 | tf_op jit(solution)/shard_map/ppermute | solution.py:175
  80.0 45.8 %collective-permute-start.7 = (bf16[1936,512]{1,0:T(8,128)(2,1)}, bf16[1936,512]{1,0:T(8,128)(2,1)S(1)}, u32[]{:S(2)}, u32[]{:S(2)}) collective-permute-start(bf16[1936,512]{1,0:T(8,128)(2,1)} %gate.17.refs_9_.refs_1_), channel_id=1, source_target_pairs={{0,16},{4,20},{8,24},{12,28},{16,0},{20,4},{24,8},{28,12},{1,17},{... | collective-permute-start | bytes 5947400 | tf_op jit(solution)/shard_map/ppermute | solution.py:175
  113.6 39.5 %collective-permute-start.14 = (bf16[384,2048]{1,0:T(8,128)(2,1)}, bf16[384,2048]{1,0:T(8,128)(2,1)}, u32[]{:S(2)}, u32[]{:S(2)}) collective-permute-start(bf16[384,2048]{1,0:T(8,128)(2,1)} %gate.20), channel_id=1, source_target_pairs={{0,1},{1,2},{2,3},{4,5},{5,6},{6,7},{8,9},{9,10},{10,11},{12,13},{... | collective-permute-start | bytes 4718600 | tf_op jit(solution)/shard_map/ppermute | solution.py:179
  123.4 36.3 %collective-permute-start.16 = (bf16[384,2048]{1,0:T(8,128)(2,1)}, bf16[384,2048]{1,0:T(8,128)(2,1)}, u32[]{:S(2)}, u32[]{:S(2)}) collective-permute-start(bf16[384,2048]{1,0:T(8,128)(2,1)} %gate.21), channel_id=1, source_target_pairs={{3,2},{2,1},{1,0},{7,6},{6,5},{5,4},{11,10},{10,9},{9,8},{15,14},{... | collective-permute-start | bytes 4718600 | tf_op jit(solution)/shard_map/ppermute | solution.py:183
  127.1 45.0 %collective-permute-start.8 = (bf16[1936,512]{1,0:T(8,128)(2,1)}, bf16[1936,512]{1,0:T(8,128)(2,1)S(1)}, u32[]{:S(2)}, u32[]{:S(2)}) collective-permute-start(bf16[1936,512]{1,0:T(8,128)(2,1)} %gate.18.refs_10_.refs_2_), channel_id=1, source_target_pairs={{0,16},{4,20},{8,24},{12,28},{16,0},{20,4},{24,8},{28,12},{1,17},{... | collective-permute-start | bytes 5947400 | tf_op jit(solution)/shard_map/ppermute | solution.py:175
  127.6 44.8 %collective-permute-start.9 = (bf16[1936,512]{1,0:T(8,128)(2,1)}, bf16[1936,512]{1,0:T(8,128)(2,1)}, u32[]{:S(2)}, u32[]{:S(2)}) collective-permute-start(bf16[1936,512]{1,0:T(8,128)(2,1)} %gate.19.refs_13_.refs_5_), channel_id=1, source_target_pairs={{0,8},{4,12},{8,0},{12,4},{16,24},{20,28},{24,16},{28,20},{1,9},{5... | collective-permute-start | bytes 5947400 | tf_op jit(solution)/shard_map/ppermute | solution.py:175
  173.4 47.5 %collective-permute-start.19 = (bf16[512,512]{1,0:T(8,128)(2,1)}, bf16[512,512]{1,0:T(8,128)(2,1)}, u32[]{:S(2)}, u32[]{:S(2)}) collective-permute-start(bf16[512,512]{1,0:T(8,128)(2,1)} %gate.22), channel_id=1, source_target_pairs={{0,8},{4,12},{8,0},{12,4},{16,24},{20,28},{24,16},{28,20},{1,9},{5... | collective-permute-start | bytes 1572872 | tf_op jit(solution)/shard_map/ppermute | solution.py:175
  174.9 51.8 %collective-permute-start.20 = (bf16[512,512]{1,0:T(8,128)(2,1)}, bf16[512,512]{1,0:T(8,128)(2,1)}, u32[]{:S(2)}, u32[]{:S(2)}) collective-permute-start(bf16[512,512]{1,0:T(8,128)(2,1)} %gate.23), channel_id=1, source_target_pairs={{0,16},{4,20},{8,24},{12,28},{16,0},{20,4},{24,8},{28,12},{1,17},{... | collective-permute-start | bytes 1572872 | tf_op jit(solution)/shard_map/ppermute | solution.py:175
  176.3 50.5 %collective-permute-start.21 = (bf16[512,512]{1,0:T(8,128)(2,1)}, bf16[512,512]{1,0:T(8,128)(2,1)}, u32[]{:S(2)}, u32[]{:S(2)}) collective-permute-start(bf16[512,512]{1,0:T(8,128)(2,1)} %gate.24), channel_id=1, source_target_pairs={{0,24},{4,28},{8,16},{12,20},{16,8},{20,12},{24,0},{28,4},{1,25},{... | collective-permute-start | bytes 1572872 | tf_op jit(solution)/shard_map/ppermute | solution.py:175
  191.9 34.9 %collective-permute-start.22 = (bf16[384,2048]{1,0:T(8,128)(2,1)}, bf16[384,2048]{1,0:T(8,128)(2,1)S(1)}, u32[]{:S(2)}, u32[]{:S(2)}) collective-permute-start(bf16[384,2048]{1,0:T(8,128)(2,1)} %get-tuple-element.39), channel_id=1, source_target_pairs={{0,1},{1,2},{2,3},{4,5},{5,6},{6,7},{8,9},{9,10},{10,11},{12,13},{... | collective-permute-start | bytes 4718600 | tf_op jit(solution)/shard_map/ppermute | solution.py:179
  193.7 37.2 %collective-permute-start.23 = (bf16[384,2048]{1,0:T(8,128)(2,1)}, bf16[384,2048]{1,0:T(8,128)(2,1)S(1)}, u32[]{:S(2)}, u32[]{:S(2)}) collective-permute-start(bf16[384,2048]{1,0:T(8,128)(2,1)} %get-tuple-element.40), channel_id=1, source_target_pairs={{3,2},{2,1},{1,0},{7,6},{6,5},{5,4},{11,10},{10,9},{9,8},{15,14},{... | collective-permute-start | bytes 4718600 | tf_op jit(solution)/shard_map/ppermute | solution.py:183
  237.8 38.4 %collective-permute-start.25 = (bf16[512,512]{1,0:T(8,128)(2,1)}, bf16[512,512]{1,0:T(8,128)(2,1)S(1)}, u32[]{:S(2)}, u32[]{:S(2)}) collective-permute-start(bf16[512,512]{1,0:T(8,128)(2,1)} %get-tuple-element.43), channel_id=1, source_target_pairs={{0,2},{1,3},{2,0},{3,1},{4,6},{5,7},{6,4},{7,5},{8,10},{9,11},{10,... | collective-permute-start | bytes 1572872 | tf_op jit(solution)/shard_map/ppermute | solution.py:772
  237.8 38.4 %collective-permute-start.26 = (bf16[512,512]{1,0:T(8,128)(2,1)}, bf16[512,512]{1,0:T(8,128)(2,1)S(1)}, u32[]{:S(2)}, u32[]{:S(2)}) collective-permute-start(bf16[512,512]{1,0:T(8,128)(2,1)} %get-tuple-element.44), channel_id=1, source_target_pairs={{0,3},{1,2},{2,1},{3,0},{4,7},{5,6},{6,5},{7,4},{8,11},{9,10},{10,... | collective-permute-start | bytes 1572872 | tf_op jit(solution)/shard_map/ppermute | solution.py:772
  283.2 33.0 %collective-permute-start.32 = (bf16[512,1024]{1,0:T(8,128)(2,1)}, bf16[512,1024]{1,0:T(8,128)(2,1)S(1)}, u32[]{:S(2)}, u32[]{:S(2)}) collective-permute-start(bf16[512,1024]{1,0:T(8,128)(2,1)} %get-tuple-element.46.refs_9_), channel_id=1, source_target_pairs={{0,16},{4,20},{8,24},{12,28},{16,0},{20,4},{24,8},{28,12},{1,17},{... | collective-permute-start | bytes 3145736 | tf_op jit(solution)/shard_map/ppermute | solution.py:175
  298.0 36.6 %collective-permute-start.36 = (bf16[512,1024]{1,0:T(8,128)(2,1)}, bf16[512,1024]{1,0:T(8,128)(2,1)S(1)}, u32[]{:S(2)}, u32[]{:S(2)}) collective-permute-start(bf16[512,1024]{1,0:T(8,128)(2,1)} %get-tuple-element.46.refs_9_), channel_id=1, source_target_pairs={{0,8},{4,12},{8,0},{12,4},{16,24},{20,28},{24,16},{28,20},{1,9},{5... | collective-permute-start | bytes 3145736 | tf_op jit(solution)/shard_map/ppermute | solution.py:175
  321.4 35.5 %collective-permute-start.40 = (bf16[512,1024]{1,0:T(8,128)(2,1)S(1)}, bf16[512,1024]{1,0:T(8,128)(2,1)}, u32[]{:S(2)}, u32[]{:S(2)}) collective-permute-start(bf16[512,1024]{1,0:T(8,128)(2,1)S(1)} %copy-done.8), channel_id=1, source_target_pairs={{0,16},{4,20},{8,24},{12,28},{16,0},{20,4},{24,8},{28,12},{1,17},{... | collective-permute-start | bytes 3145736 | tf_op jit(solution)/shard_map/ppermute | solution.py:175
  (55 other events, 543.4 us)

commit v3 on v2

--- a/solution.py
+++ b/solution.py
@@ -252,8 +252,8 @@
     return move(pick_plan, (options[0].shape,), ids, distinct, arrived)[0]
 
 
-def hops(ids, pending, up, down, offset, relay, both, arrived=()):
-    tok, feat = up.shape
+def hops(ids, pending, up, down, offset, relay, both, rows, arrived=()):
+    tok, feat = pending.shape[1], up.shape[1]
 
     def kernel(ids_ref, pending_ref, up_ref, down_ref, *refs):
         out_up, out_down, buf, sems = refs[len(arrived) :]
@@ -266,23 +266,32 @@
             is_both = functools.reduce(jnp.logical_or, [at == p for p in both], at < 0)
             place = jnp.clip(z + step, 0, N_TP - 1)
             share = pltpu.make_async_copy(
-                pending_ref.at[0, :, pl.ds(multiple(place, feat), feat)], out, sems.at[i]
+                pending_ref.at[0, :, pl.ds(multiple(place, feat), feat)],
+                out.at[pl.ds(0, tok)],
+                sems.at[i],
             )
-            passed = pltpu.make_async_copy(src, out, sems.at[i])
-            added = pltpu.make_async_copy(src, buf.at[i], sems.at[2 + i])
+            passed = pltpu.make_async_copy(src.at[pl.ds(0, rows)], out, sems.at[i])
+            added = pltpu.make_async_copy(src.at[pl.ds(0, tok)], buf.at[i], sems.at[2 + i])
             pl.when(is_relay)(passed.start)
-            pl.when(jnp.logical_not(is_relay))(share.start)
+
+            @pl.when(jnp.logical_not(is_relay))
+            def _():
+                if rows > tok:
+                    out[tok:] = jnp.zeros((rows - tok, feat), jnp.bfloat16)
+                share.start()
+
             pl.when(is_both)(added.start)
-            todo.append((passed, added, is_both, out, i))
-        for passed, added, is_both, out, i in todo:
-            passed.wait()
+            todo.append((passed, share, added, is_relay, is_both, out, i))
+        for passed, share, added, is_relay, is_both, out, i in todo:
+            pl.when(is_relay)(passed.wait)
+            pl.when(jnp.logical_not(is_relay))(share.wait)
 
             @pl.when(is_both)
             def _():
                 added.wait()
-                out[...] += buf[i]
-
-    shape = jax.ShapeDtypeStruct((tok, feat), jnp.bfloat16)
+                out[:tok] += buf[i]
+
+    shape = jax.ShapeDtypeStruct((rows, feat), jnp.bfloat16)
     return pl.pallas_call(
         kernel,
         out_shape=(shape, shape),
@@ -307,32 +316,25 @@
 
 
 AHEAD = 3
-
-
-def part_choices(r, z):
-    return (
-        [(None, 0, 0)],
-        [(None, 0, 1)],
-        [(None, 1, 0)],
-        [(z == 0, 3, 0), (z == 3, 2, 0), ((z == 1) | (z == 2), 0, 2)],
-    )[r]
-
-
-def project_kernel(scale, at_kv, ids_ref, *refs):
-    xs, ws = refs[:8], refs[8:16]
-    factor_ref, cos_ref, sin_ref, q_ref, kv_ref, x_buf, w_buf, x_sem, w_sem = refs[16:]
-    chip, core, z = ids_ref[0], ids_ref[1], ids_ref[2]
-    tok, half, cols = xs[7].shape[0], x_buf.shape[-1], ws[0].shape[1]
+PARTS = ((0, 0), (0, 1), (1, 0), (2, 0))
+
+
+def project_kernel(slots, x_count, w_count, tok, rows, scale, at_kv, ids_ref, *refs):
+    last = scale is not None
+    xs, ws, refs = refs[:x_count], refs[x_count : x_count + w_count], refs[x_count + w_count :]
+    x_buf, w_buf, x_sem, w_sem = refs[-4:]
+    chip, core = ids_ref[0], ids_ref[1]
+    half, cols = x_buf.shape[-1], ws[0].shape[1]
     fold = half // 2
     mine = pl.multiple_of(core * tok, 128)
     theirs = pl.multiple_of((1 - core) * tok, 128)
 
     def fetch(at):
-        r, h = at // 2, at % 2
-        place = ids_ref[3 + r]
+        part, h = ids_ref[7 + slots[at // 2]], at % 2
+        place = ids_ref[3 + part]
         waits = []
         for i in range(3):
-            for m in range(4):
+            for m in range(w_count // 2):
                 src, dst = ws[2 * m + h], w_buf.at[at]
                 if i == 0:
                     src, dst = src.at[pl.ds(0, half)], dst.at[:, pl.ds(0, cols)]
@@ -344,27 +346,28 @@
                 pl.when((place ^ chip) == m)(copy.start)
             waits.append(copy)
         features = pl.ds(pl.multiple_of((core ^ h) * half, 128), half)
-        for s, rows in ((0, mine), (1, theirs)):
-            for cond, index, group in part_choices(r, z):
-                src = xs[2 * index + s].at[pl.ds(group * tok, tok), features]
-                copy = pltpu.make_async_copy(
-                    src, x_buf.at[at, pl.ds(rows, tok)], x_sem.at[2 * at + s]
-                )
-                if cond is None:
-                    copy.start()
-                else:
-                    pl.when(cond)(copy.start)
+        for s, to in ((0, mine), (1, theirs)):
+            for r, (index, group) in enumerate(PARTS):
+                if 2 * index < x_count:
+                    src = xs[2 * index + s].at[pl.ds(group * rows, tok), features]
+                    dst = x_buf.at[at, pl.ds(to, tok)]
+                    copy = pltpu.make_async_copy(src, dst, x_sem.at[2 * at + s])
+                    pl.when(part == r)(copy.start)
             waits.append(copy)
         return waits
 
     ahead = [fetch(at) for at in range(AHEAD)]
-    acc = 0.0
-    for at in range(8):
+    acc = refs[0][...] if last else 0.0
+    for at in range(4):
         for copy in ahead[at]:
             copy.wait()
-        if at + AHEAD < 8:
+        if at + AHEAD < 4:
             ahead.append(fetch(at + AHEAD))
         acc = acc + jnp.dot(x_buf[at], w_buf[at], preferred_element_type=jnp.float32)
+    if not last:
+        refs[0][...] = acc
+        return
+    factor_ref, cos_ref, sin_ref, q_ref, kv_ref, tail_ref = refs[1:7]
     factor = factor_ref[...]
     heads = q_ref.shape[0]
     for h in range(heads + 2):
@@ -375,30 +378,37 @@
             q_ref[h] = (v * scale).astype(jnp.bfloat16)
         else:
             kv_ref[h - heads] = v.astype(jnp.bfloat16)
-
-
-def project(ids, xs, weights, at_kv, factor, cosine, sinus, scale):
-    tok, feat = xs[7].shape
+            tail_ref[h - heads] = v[tok:].astype(jnp.bfloat16)
+
+
+def project(ids, slots, xs, weights, tok, at_kv, tables=(), scale=None):
+    rows = xs[0].shape[0] // 2
+    feat = xs[0].shape[1]
     cols = weights[0].shape[1]
     half = feat // 2
+    sums = jax.ShapeDtypeStruct((2 * tok, cols + 2 * HD), jnp.float32)
+    results = (
+        jax.ShapeDtypeStruct((cols // HD, 2 * tok, HD), jnp.bfloat16),
+        jax.ShapeDtypeStruct((2, 2 * tok, HD), jnp.bfloat16),
+        jax.ShapeDtypeStruct((2, tok, HD), jnp.bfloat16),
+    )
     return pl.pallas_call(
-        functools.partial(project_kernel, scale, at_kv),
-        out_shape=(
-            jax.ShapeDtypeStruct((cols // HD, 2 * tok, HD), jnp.bfloat16),
-            jax.ShapeDtypeStruct((2, 2 * tok, HD), jnp.bfloat16),
+        functools.partial(
+            project_kernel, slots, len(xs), len(weights), tok, rows, scale, at_kv
         ),
-        in_specs=[SMEM] + [HBM] * 16 + [VMEM] * 3,
-        out_specs=(VMEM, VMEM),
+        out_shape=results if tables else sums,
+        in_specs=[SMEM] + [HBM] * (len(xs) + len(weights)) + [VMEM] * len(tables),
+        out_specs=(VMEM,) * 3 if tables else VMEM,
         scratch_shapes=[
-            pltpu.VMEM((8, 2 * tok, half), jnp.bfloat16),
-            pltpu.VMEM((8, half, cols + 2 * HD), jnp.bfloat16),
-            pltpu.SemaphoreType.DMA((16,)),
-            pltpu.SemaphoreType.DMA((24,)),
+            pltpu.VMEM((4, 2 * tok, half), jnp.bfloat16),
+            pltpu.VMEM((4, half, cols + 2 * HD), jnp.bfloat16),
+            pltpu.SemaphoreType.DMA((8,)),
+            pltpu.SemaphoreType.DMA((12,)),
         ],
         compiler_params=pltpu.CompilerParams(vmem_limit_bytes=GRANT),
         cost_estimate=LITTLE,
         name="project",
-    )(ids, *xs, *weights, factor, cosine, sinus)
+    )(ids, *xs, *weights, *tables)
 
 
 BT = 256
@@ -417,8 +427,9 @@
     return new, acc
 
 
-def attend_kernel(halo, at_old, bound_ref, ids_ref, q_ref, n_ref, lo_ref, k_ref, v_ref, *refs):
-    bundles, (out_ref, k_old, v_ext, s_ref, m_ref, acc_ref, sems) = refs[:8], refs[-7:]
+def attend_kernel(at_old, bound_ref, ids_ref, q_ref, n_ref, lo_ref, before_ref, new_ref, *refs):
+    bundles, (out_ref, k_old, v_ext, kv_near, s_ref, m_ref, acc_ref, sems) = refs[:8], refs[-8:]
+    halo = before_ref.shape[1]
     b = pl.program_id(0)
     heads, bt = q_ref.shape[0], q_ref.shape[1]
     rows, chains = CHAIN * bt, heads // CHAIN
@@ -443,6 +454,8 @@
         for copy in copies:
             copy.start()
         v_ext[:, HD:] = jnp.ones((v_ext.shape[0], HD), jnp.bfloat16)
+        kv_near[:, :halo] = before_ref[...]
+        kv_near[:, halo:] = new_ref[...]
         for copy in copies:
             copy.wait()
 
@@ -482,8 +495,8 @@
 
     span = halo + bt
     start = pl.multiple_of(b * bt, bt)
-    k = k_ref[pl.ds(start, span), :]
-    v = v_ref[pl.ds(start, span), :]
+    k = kv_near[0, pl.ds(start, span), :]
+    v = kv_near[1, pl.ds(start, span), :]
     v = jnp.concatenate([v, jnp.ones_like(v)], axis=1)
     lo = jnp.concatenate([lo_ref[:, :1]] * CHAIN, axis=0)
     col = lax.broadcasted_iota(jnp.int32, (rows, span), 1)
@@ -498,12 +511,12 @@
             out_ref[:, at : at + HD] = mixed[h * bt : (h + 1) * bt]
 
 
-def attend(bounds, ids, q, n_tok, lo_tok, k, v, bundles, at_old, keys, arrived=()):
+def attend(bounds, ids, q, n_tok, lo_tok, before, new, bundles, at_old, keys, arrived=()):
     heads, tokens = q.shape[:2]
     chains, rows = heads // CHAIN, CHAIN * BT
-    halo = k.shape[0] - tokens
+    halo = before.shape[1]
     return pl.pallas_call(
-        functools.partial(attend_kernel, halo, at_old),
+        functools.partial(attend_kernel, at_old),
         out_shape=jax.ShapeDtypeStruct((tokens, heads * HD), jnp.bfloat16),
         grid_spec=pltpu.PrefetchScalarGridSpec(
             num_scalar_prefetch=2,
@@ -512,8 +525,8 @@
                 pl.BlockSpec((heads, BT, HD), lambda b, *_: (0, b, 0)),
                 pl.BlockSpec((BT, 128), lambda b, *_: (b, 0)),
                 pl.BlockSpec((BT, 128), lambda b, *_: (b, 0)),
-                pl.BlockSpec(k.shape, lambda b, *_: (0, 0)),
-                pl.BlockSpec(v.shape, lambda b, *_: (0, 0)),
+                pl.BlockSpec(before.shape, lambda b, *_: (0, 0, 0)),
+                pl.BlockSpec(new.shape, lambda b, *_: (0, 0, 0)),
             ]
             + [HBM] * 8
             + specs_of(arrived),
@@ -521,6 +534,7 @@
             scratch_shapes=[
                 pltpu.VMEM((keys, HD), jnp.bfloat16),
                 pltpu.VMEM((keys, 2 * HD), jnp.bfloat16),
+                pltpu.VMEM((2, halo + tokens, HD), jnp.bfloat16),
                 pltpu.VMEM((rows, BK), jnp.float32),
                 pltpu.VMEM((chains, rows, 128), jnp.float32),
                 pltpu.VMEM((chains, rows, 2 * HD), jnp.float32),
@@ -530,7 +544,7 @@
         compiler_params=pltpu.CompilerParams(vmem_limit_bytes=GRANT),
         cost_estimate=LITTLE,
         name="attend",
-    )(bounds, ids, q, n_tok, lo_tok, k, v, *bundles, *arrived)
+    )(bounds, ids, q, n_tok, lo_tok, before, new, *bundles, *arrived)
 
 
 def out_kernel(ids_ref, *refs):
@@ -620,6 +634,20 @@
     gain = lax.dynamic_slice_in_dim(norm_gain, z * feat, feat, 0).astype(jnp.float32)
     scaled = (wide * gain[None, :]).astype(jnp.bfloat16)
 
+    left = jnp.sum(wide * wide, axis=1)
+    sums = []
+    for _ in range(3):
+        sums.append(lax.reduce_precision(left, 8, 7))
+        left = left - sums[-1]
+    sums = jnp.pad(jnp.stack(sums), ((0, 13), (0, feat - tok))).astype(jnp.bfloat16)
+    scaled = jnp.concatenate([scaled, sums], axis=0)
+    n_rows = scaled.shape[0]
+
+    def squares(part, group=0):
+        at = group * n_rows + tok
+        return jnp.sum(part[at : at + 3, :tok].astype(jnp.float32), axis=0)
+
+
     labels = jnp.arange(NTRAJ, dtype=jnp.int32)
     counts = jnp.concatenate(
         [
@@ -640,10 +668,6 @@
     cosine, sinus = jnp.cos(angles), jnp.sin(angles)
     cosine = jnp.concatenate([cosine, cosine], axis=1)
     sinus = jnp.concatenate([-sinus, sinus], axis=1)
-
-    def squares(part, place):
-        g = lax.dynamic_slice_in_dim(norm_gain, place * feat, feat, 0).astype(jnp.float32)
-        return jnp.sum(jnp.square(part.astype(jnp.float32) / g[None, :]), axis=1, keepdims=True)
 
     q_heads = w_query.shape[1] // HD // 2
     q_cols = q_heads * HD
@@ -675,13 +699,21 @@
     places = jnp.stack(
         [z, jnp.where(z < 2, z + 1, z - 1), jnp.where(z < 2, z + 2, z - 2), jnp.where(z % 2 == 1, 0, 3)]
     ).astype(jnp.int32)
-    ids = jnp.concatenate([here, places])
+    skip = jnp.sum(jnp.where(places == (chip ^ 3), jnp.arange(N_TP), 0))
+    order = jnp.stack(
+        [
+            jnp.where(skip == 0, 1, 0),
+            jnp.where(skip < 2, 2, 1),
+            jnp.minimum(skip, 2),
+            jnp.full((), 3),
+        ]
+    )
+    ids = jnp.concatenate([here, places, order]).astype(jnp.int32)
 
     x1, y1, given = swap(own, 2), swap(own, 4), swap(give, 1)
     turn = swap(gate(notes, own), 1)
     scaled = gate(scaled, turn)
     u1, d1 = hop_up(scaled, every), hop_down(scaled, every)
-    mine = squares(scaled, z)
 
     def piece_plan(at, src, out):
         for r, dst in enumerate(out):
@@ -697,50 +729,43 @@
         (w_out,),
         (own,),
     )
-    up, down = hops(here, pending, u1, d1, 3, (1, 2, 3), (), (cosine, sinus, mine, given, by_chip[0]))
+    given = gate(given, x1, y1)
+    up, down = hops(here, pending, u1, d1, 3, (1, 2, 3), (), n_rows, (cosine, sinus, given))
     u2, d2 = hop_up(up, every), hop_down(down, every)
+    x2, y2 = swap(given, 2), swap(given, 4)
 
     def near_plan(at, src, out):
         own_part, up_part, down_part = src
-        low = at[2] < 2
-        high = at[2] >= 2
-        yield one(own_part, out[0].at[pl.ds(0, tok)])
-        yield ([(low, down_part), (high, up_part)], out[0].at[pl.ds(tok, tok)])
-        yield ([(low, up_part), (high, down_part)], out[0].at[pl.ds(2 * tok, tok)])
-
-    (near,) = move(near_plan, ((3 * tok, feat),), here, (scaled, u1, d1), (up,))
-    given = gate(given, x1, y1, near)
-    x2, y2 = swap(given, 2), swap(given, 4)
+        yield one(own_part, out[0].at[pl.ds(0, n_rows)])
+        near = [(at[2] < 2, down_part), (at[2] >= 2, up_part)]
+        yield (near, out[0].at[pl.ds(n_rows, n_rows)])
+
+    (near,) = move(near_plan, ((2 * n_rows, feat),), here, (scaled, u1, d1), (by_chip[0],))
+    near = gate(near, x1, y1)
     over1 = swap(near, 1)
-    mine = mine + squares(near[tok : 2 * tok], places[1])
-    theirs = squares(over1[:tok], z) + squares(over1[tok : 2 * tok], places[1])
-    mine_near = squares(near[2 * tok :], places[3])
-    theirs_near = squares(over1[2 * tok :], places[3])
-
-    up, down = hops(here, pending, u2, d2, 2, (2,), (1,))
-    second = pick(z, (d2, d2, u2, u2), here, (up,))
-    u3, d3 = hop_up(gate(up, second), every), hop_down(gate(down, second), every)
+
+    up, down = hops(here, pending, u2, d2, 2, (2,), (1,), n_rows)
+    u3, d3 = hop_up(gate(up, x2), every), hop_down(gate(down, y2), every)
     x1, y2 = gate(x1, x2, y2), gate(y2, x2)
     far_own, far_other = swap(x1, 4), swap(y2, 2)
-
+    second = pick(z, (d2, d2, u2, u2), here)
     over2 = swap(second, 1)
-    mine = mine + squares(second, places[2])
-    theirs = theirs + squares(over2, places[2])
-
-    su3, sd3 = swap(u3, 1), swap(d3, 1)
-    up, down = hops(here, pending, u3, d3, 1, (), (1, 2, 3), (over2, mine, theirs))
+    own_rows = (own, given, x1, x2, y1, y2, far_own, far_other)
+    xs = [near, over1, second, over2]
+    sums = project(ids, (0, 1), xs, own_rows[:6], tok, n_both)
+
+    third = pick(z, (d3, u1, d1, u3), here, (sums, far_own, far_other))
+    over3 = swap(third, 1)
+    up, down = hops(here, pending, u3, d3, 1, (), (1, 2, 3), tok, (third,))
     u4, d4 = hop_up(up, every), hop_down(down, every)
-    mine = mine + jnp.where(
-        z == 0, squares(d3, places[3]), jnp.where(z == 3, squares(u3, places[3]), mine_near)
-    )
-    theirs = theirs + jnp.where(
-        z == 0, squares(sd3, places[3]), jnp.where(z == 3, squares(su3, places[3]), theirs_near)
+    mine, theirs = (
+        squares(a) + squares(a, 1) + squares(b) + squares(c)
+        for a, b, c in ((near, second, third), (over1, over2, over3))
     )
     total = jnp.where(first, jnp.concatenate([mine, theirs]), jnp.concatenate([theirs, mine]))
     factor = lax.rsqrt(total * (1.0 / depth) + NORM_EPSILON)
-    factor = jnp.broadcast_to(factor, (chip_tok, 128))
-    xs = [near, over1, second, over2, u3, su3, d3, sd3]
-    own_rows = (own, given, x1, x2, y1, y2, far_own, far_other)
+    factor = jnp.broadcast_to(factor[:, None], (chip_tok, 128))
+    xs += [third, over3]
 
     said = [rows[n_both + n_kv : n_both + n_kv + 2].astype(jnp.float32) for rows in own_rows]
     total = sum(v[1, : 4 * NTRAJ] for v in said).astype(jnp.int32)
@@ -759,27 +784,27 @@
         swap(gate(by_chip[r], far_own, far_other), 2 * r) for r in (1, 2, 3)
     )
     scale = math.log2(math.e) / math.sqrt(HD)
-    q, kv_new = project(ids, xs, own_rows, n_both, factor, cosine, sinus, scale)
-    before = lax.ppermute(kv_new[:, tok:], "ctx", [(i, i + 2) for i in range(N_CTX - 2)])
+    q, kv_new, tail = project(
+        ids, (2, 3), xs, own_rows, tok, n_both, (sums, factor, cosine, sinus), scale
+    )
+    before = lax.ppermute(tail, "ctx", [(i, i + 2) for i in range(N_CTX - 2)])
 
     def pieces_plan(at, src, out):
         for r, dst in enumerate(out):
             near = (at[2] ^ r) ^ at[0]
             yield ([(near == m, src[m]) for m in range(4)], dst)
 
-    pieces = list(move(pieces_plan, ((2 * n_piece, q_cols),) * 4, here, by_chip, (q, u4, d4)))
+    pieces = list(move(pieces_plan, ((2 * n_piece, q_cols),) * 4, here, by_chip, (q,)))
     for r in (1, 2, 3):
         pieces[r] = lax.ppermute(pieces[r], "tp", [(i, i ^ r) for i in range(N_TP)])
-    k_near = jnp.concatenate([before[0], kv_new[0]], axis=0)
-    v_near = jnp.concatenate([before[1], kv_new[1]], axis=0)
     attended = attend(
         bounds,
         here,
         q,
         n_wide,
         lo_wide,
-        k_near,
-        v_near,
+        before,
+        kv_new,
         own_rows,
         n_q,
         N_CTX * prefix_keys.shape[1],
@@ -796,7 +821,7 @@
     wo_xa, wo_yb = swap(wo_a, 2), swap(wo_b, 4)
     wo_xb, wo_ya = swap(wo_b, 2), swap(wo_a, 4)
 
-    attended = gate(attended, *pieces[1:])
+    attended = gate(attended, u4, d4, *pieces[1:])
     u1, d1 = hop_up(attended, every), hop_down(attended, every)
     near = pick(z, (d1, d1, u1, u1), here)
 

time: 386 us -> 378 us (0.979)
  other arithmetic: 30.9 us -> 19.8 us
  Pallas kernels: 104 us -> 111 us
  local copies, waits for them, and re-layouts: 22.7 us -> 17.7 us
  waiting for transfers between devices: 155 us -> 151 us
    ppermute x26 -> x25, waiting for transfers between devices: 40.6 us -> 15.9 us  [swap(): return lax.ppermute(x, 'ctx', [(c, c ^ bit) for c in range(N_CTX)])]
    ppermute x7, waiting for transfers between devices: 46.6 us -> 63.6 us  [hop_up(): return lax.ppermute(v, 'tp', [(i, i + 1) for i in pairs])]
    ppermute x7, starting transfers between devices: 26.2 us -> 35.5 us  [hop_up(): return lax.ppermute(v, 'tp', [(i, i + 1) for i in pairs])]
    ppermute x3, waiting for transfers between devices: 8.6 us -> 16.3 us  [per_device(): pieces[r] = lax.ppermute(pieces[r], 'tp', [(i, i ^ r) for i in range(N_TP)])]
    reduce_sum x3 -> x7, other arithmetic: 10.6 us -> 4.37 us  [the longest x6 3.6 us: squares(): return jnp.sum(part[at:at + 3, :tok].astype(jnp.float32), axis=0)]
    ppermute x26 -> x25, starting transfers between devices: 25.7 us -> 20.7 us  [swap(): return lax.ppermute(x, 'ctx', [(c, c ^ bit) for c in range(N_CTX)])]
    ppermute x7, waiting for transfers between devices: 59.3 us -> 55.2 us  [hop_down(): return lax.ppermute(v, 'tp', [(N_TP - 1 - i, N_TP - 2 - i) for i in pairs])]
    pallas_call x2 -> x3, Pallas kernels: 42.7 us -> 46.2 us  [the longest x2 25.1 us: project(): pl.pallas_call(functools.partial(project_kernel, slots, len(xs), len(weig...]
  transfers between devices with their start and end apart: 44 -> 43, of which waited for: 20 -> 13; matrix products, arithmetic and copies ran while one was open for 9% -> 5% of each run, Pallas kernels for 21% -> 24%
where the time goes in v3:
time: 378 us; the launch traced here: 375 us
  waiting for transfers between devices  151 us (40%)
  Pallas kernels  111 us (29%)
  starting transfers between devices  73.1 us (19%)
  other arithmetic  19.8 us (5%)
  local copies, waits for them, and re-layouts  17.7 us (5%)
    ppermute x7, waiting for transfers between devices, hop_up(): return lax.ppermute(v, 'tp', [(i, i + 1) for i in pairs])  63.6 us
    ppermute x7, waiting for transfers between devices, hop_down(): return lax.ppermute(v, 'tp', [(N_TP - 1 - i, N_TP - 2 - i) for i in pairs])  55.2 us
    pallas_call x10, Pallas kernels, move(): pl.pallas_call(kernel, out_shape=tuple((jax.ShapeDtypeStruct(shape, jnp.b...  37.8 us
    ppermute x7, starting transfers between devices, hop_up(): return lax.ppermute(v, 'tp', [(i, i + 1) for i in pairs])  35.5 us
    pallas_call x2, Pallas kernels, project(): pl.pallas_call(functools.partial(project_kernel, slots, len(xs), len(weig...  25.1 us
    pallas_call x1, Pallas kernels, attend(): pl.pallas_call(functools.partial(attend_kernel, at_old), out_shape=jax.Sh...  21 us
    ppermute x25, starting transfers between devices, swap(): return lax.ppermute(x, 'ctx', [(c, c ^ bit) for c in range(N_CTX)])  20.7 us
    ppermute x3, waiting for transfers between devices, per_device(): pieces[r] = lax.ppermute(pieces[r], 'tp', [(i, i ^ r) for i in range(N_TP)])  16.3 us
  transfers between devices with their start and end apart: 43, of which 13 were waited for; matrix products, arithmetic and copies ran while one was open for 5% of the time, Pallas kernels for 24%

profile of v3, /device:TPU:0, one launch (start us, length us, event | category | flops | bytes accessed | tf_op | source)
XLA Modules:
  0.0 375.5 jit_solution(17772063222476563785)
XLA Ops:
  4.4 5.0 %first_plan.1 = (bf16[1936,512]{1,0:T(8,128)(2,1)}, bf16[1936,512]{1,0:T(8,128)(2,1)}) custom-call(s32[3]{0:T(128)} %pad_add_fusion.1.ids_ref, bf16[1024,1024]{1,0:T(8,128)(2,1)} %refs_0_.2, bf16[1024,1024]{1,0:T(8,128)(2,1)} %refs_1_.1, bf16[1024,1024]{1,0:T(8,128)(2,1)} %refs_2_.1, bf16[8,768,128]{2,1,0:T(8,128)(2,1)} %refs_3_.1, ...), custom_call_target="tpu_custom_call" | custom-call | bytes 1024 | tf_op jit(solution)/shard_map/first_plan/pallas_call | solution.py:218
  16.5 4.7 %collective-permute-start.8 = (bf16[400,2048]{1,0:T(8,128)(2,1)}, bf16[400,2048]{1,0:T(8,128)(2,1)}, u32[]{:S(2)}, u32[]{:S(2)}) collective-permute-start(bf16[400,2048]{1,0:T(8,128)(2,1)} %gate.20.refs_0_), channel_id=1, source_target_pairs={{0,1},{1,2},{2,3},{4,5},{5,6},{6,7},{8,9},{9,10},{10,11},{12,13},{... | collective-permute-start | bytes 4915208 | tf_op jit(solution)/shard_map/ppermute | solution.py:179
  26.6 29.4 %collective-permute-done.8.refs_1_.up_ref = bf16[400,2048]{1,0:T(8,128)(2,1)} collective-permute-done((bf16[400,2048]{1,0:T(8,128)(2,1)}, bf16[400,2048]{1,0:T(8,128)(2,1)}, u32[]{:S(2)}, u32[]{:S(2)}) %collective-permute-start.8) | collective-permute-done | bytes 1638432 | tf_op jit(solution)/shard_map/ppermute | solution.py:179
  56.0 5.3 %collective-permute-done.9.refs_2_.down_ref = bf16[400,2048]{1,0:T(8,128)(2,1)} collective-permute-done((bf16[400,2048]{1,0:T(8,128)(2,1)}, bf16[400,2048]{1,0:T(8,128)(2,1)}, u32[]{:S(2)}, u32[]{:S(2)}) %collective-permute-start.9) | collective-permute-done | bytes 1638432 | tf_op jit(solution)/shard_map/ppermute | solution.py:183
  61.3 4.7 %near_plan.1.refs_0_ = bf16[800,2048]{1,0:T(8,128)(2,1)} custom-call(s32[3]{0:T(128)} %pad_add_fusion.1.ids_ref, bf16[400,2048]{1,0:T(8,128)(2,1)} %gate.20.refs_0_, bf16[400,2048]{1,0:T(8,128)(2,1)} %collective-permute-done.8.refs_1_.up_ref, bf16[400,2048]{1,0:T(8,128)(2,1)} %collective-permute-done.9.refs_2_.down_ref, ...), custom_call_target="tpu_custom_call" | custom-call | bytes 1024 | tf_op jit(solution)/shard_map/near_plan/pallas_call | solution.py:218
  71.7 4.3 %hops.3 = (bf16[400,2048]{1,0:T(8,128)(2,1)}, bf16[400,2048]{1,0:T(8,128)(2,1)}) custom-call(s32[3]{0:T(128)} %pad_add_fusion.1.ids_ref, bf16[1,384,8192]{2,1,0:T(8,128)(2,1)} %pending_ref.5, bf16[400,2048]{1,0:T(8,128)(2,1)} %collective-permute-done.8.refs_1_.up_ref, bf16[400,2048]{1,0:T(8,128)(2,1)} %collective-permute-done.9.refs_2_.down_ref, ...), custom_call_target="tpu_custom_call" | custom-call | bytes 1024 | tf_op jit(solution)/shard_map/hops/pallas_call | solution.py:295
  80.8 33.0 %collective-permute-done.12.refs_1_.up_ref = bf16[400,2048]{1,0:T(8,128)(2,1)} collective-permute-done((bf16[400,2048]{1,0:T(8,128)(2,1)}, bf16[400,2048]{1,0:T(8,128)(2,1)}, u32[]{:S(2)}, u32[]{:S(2)}) %collective-permute-start.12) | collective-permute-done | bytes 1638432 | tf_op jit(solution)/shard_map/ppermute | solution.py:179
  113.8 5.3 %collective-permute-done.11.refs_0_.down_ref = bf16[400,2048]{1,0:T(8,128)(2,1)} collective-permute-done((bf16[400,2048]{1,0:T(8,128)(2,1)}, bf16[400,2048]{1,0:T(8,128)(2,1)}, u32[]{:S(2)}, u32[]{:S(2)}) %collective-permute-start.11) | collective-permute-done | bytes 1638432 | tf_op jit(solution)/shard_map/ppermute | solution.py:183
  119.1 4.3 %hops.4 = (bf16[400,2048]{1,0:T(8,128)(2,1)}, bf16[400,2048]{1,0:T(8,128)(2,1)}) custom-call(s32[3]{0:T(128)} %pad_add_fusion.1.ids_ref, bf16[1,384,8192]{2,1,0:T(8,128)(2,1)} %pending_ref.5, bf16[400,2048]{1,0:T(8,128)(2,1)} %collective-permute-done.12.refs_1_.up_ref, bf16[400,2048]{1,0:T(8,128)(2,1)} %collective-permute-done.11.refs_0_.down_ref), custom_call_target="tpu_custom_call" | custom-call | bytes 1024 | tf_op jit(solution)/shard_map/hops/pallas_call | solution.py:295
  134.2 5.7 %collective-permute-start.15 = (bf16[400,2048]{1,0:T(8,128)(2,1)}, bf16[400,2048]{1,0:T(8,128)(2,1)}, u32[]{:S(2)}, u32[]{:S(2)}) collective-permute-start(bf16[400,2048]{1,0:T(8,128)(2,1)} %gate.23), channel_id=1, source_target_pairs={{0,1},{1,2},{2,3},{4,5},{5,6},{6,7},{8,9},{9,10},{10,11},{12,13},{... | collective-permute-start | bytes 4915208 | tf_op jit(solution)/shard_map/ppermute | solution.py:179
  144.0 11.9 %project.2.refs_4_.refs_14_ = f32[768,768]{1,0:T(8,128)} custom-call(s32[11]{0:T(128)} %concatenate.54.ids_ref, bf16[800,2048]{1,0:T(8,128)(2,1)} %gate.21.refs_0_, bf16[800,2048]{1,0:T(8,128)(2,1)} %collective-permute-done.10.refs_1_, bf16[400,2048]{1,0:T(8,128)(2,1)} %pick_plan.5.refs_2_, bf16[400,2048]{1,0:T(8,128)(2,1)} %collective-permute-done.13.refs_3_, ...), custom_call_target="tpu_custom_call" | custom-call | bytes 1024 | tf_op jit(solution)/shard_map/project/pallas_call | solution.py:395
  155.9 17.3 %collective-permute-done.14.refs_0_.down_ref = bf16[400,2048]{1,0:T(8,128)(2,1)} collective-permute-done((bf16[400,2048]{1,0:T(8,128)(2,1)}, bf16[400,2048]{1,0:T(8,128)(2,1)}, u32[]{:S(2)}, u32[]{:S(2)}) %collective-permute-start.14) | collective-permute-done | bytes 1638432 | tf_op jit(solution)/shard_map/ppermute | solution.py:183
  184.2 4.9 %hops.5 = (bf16[384,2048]{1,0:T(8,128)(2,1)}, bf16[384,2048]{1,0:T(8,128)(2,1)}) custom-call(s32[3]{0:T(128)} %pad_add_fusion.1.ids_ref, bf16[1,384,8192]{2,1,0:T(8,128)(2,1)} %pending_ref.5, bf16[400,2048]{1,0:T(8,128)(2,1)} %collective-permute-done.15.refs_3_.up_ref, bf16[400,2048]{1,0:T(8,128)(2,1)} %collective-permute-done.14.refs_0_.down_ref, ...), custom_call_target="tpu_custom_call" | custom-call | bytes 1024 | tf_op jit(solution)/shard_map/hops/pallas_call | solution.py:295
  189.1 6.0 %collective-permute-start.21 = (bf16[384,2048]{1,0:T(8,128)(2,1)}, bf16[384,2048]{1,0:T(8,128)(2,1)}, u32[]{:S(2)}, u32[]{:S(2)}) collective-permute-start(bf16[384,2048]{1,0:T(8,128)(2,1)} %get-tuple-element.42), channel_id=1, source_target_pairs={{0,1},{1,2},{2,3},{4,5},{5,6},{6,7},{8,9},{9,10},{10,11},{12,13},{... | collective-permute-start | bytes 4718600 | tf_op jit(solution)/shard_map/ppermute | solution.py:179
  201.7 13.2 %project.3 = (bf16[4,768,128]{2,1,0:T(8,128)(2,1)}, bf16[2,768,128]{2,1,0:T(8,128)(2,1)}, bf16[2,384,128]{2,1,0:T(8,128)(2,1)}) custom-call(s32[11]{0:T(128)} %concatenate.54.ids_ref, bf16[800,2048]{1,0:T(8,128)(2,1)} %gate.21.refs_0_, bf16[800,2048]{1,0:T(8,128)(2,1)} %collective-permute-done.10.refs_1_, bf16[400,2048]{1,0:T(8,128)(2,1)} %pick_plan.5.refs_2_, ...), custom_call_target="tpu_custom_call" | custom-call | bytes 1024 | tf_op jit(solution)/shard_map/project/pallas_call | solution.py:395
  230.1 21.0 %attend.1.refs_0_.refs_4_ = bf16[768,512]{1,0:T(8,128)(2,1)} custom-call(s32[2,3]{1,0:T(2,128)} %pad_add_fusion.bound_ref, s32[3]{0:T(128)} %pad_add_fusion.1.ids_ref, bf16[4,768,128]{2,1,0:T(8,128)(2,1)} %get-tuple-element.35.refs_4_.q_ref, s32[768,128]{1,0:T(8,128)} %broadcast_in_dim.16.n_ref, s32[768,128]{1,0:T(8,128)} %broadcast_in_dim.17.lo_ref, ...), custom_call_target="tpu_custom_call" | custom-call | bytes 1024 | tf_op jit(solution)/shard_map/attend/pallas_call | solution.py:518
  251.2 5.2 %collective-permute-done.23.refs_3_.refs_1_ = bf16[512,512]{1,0:T(8,128)(2,1)S(1)} collective-permute-done((bf16[512,512]{1,0:T(8,128)(2,1)}, bf16[512,512]{1,0:T(8,128)(2,1)S(1)}, u32[]{:S(2)}, u32[]{:S(2)}) %collective-permute-start.23) | collective-permute-done | bytes 524320 | tf_op jit(solution)/shard_map/ppermute | solution.py:799
  256.4 11.1 %collective-permute-done.24.refs_4_.refs_2_ = bf16[512,512]{1,0:T(8,128)(2,1)S(1)} collective-permute-done((bf16[512,512]{1,0:T(8,128)(2,1)}, bf16[512,512]{1,0:T(8,128)(2,1)S(1)}, u32[]{:S(2)}, u32[]{:S(2)}) %collective-permute-start.24) | collective-permute-done | bytes 524320 | tf_op jit(solution)/shard_map/ppermute | solution.py:799
  277.4 12.2 %collective-permute-start.28 = (bf16[768,512]{1,0:T(8,128)(2,1)}, bf16[768,512]{1,0:T(8,128)(2,1)S(1)}, u32[]{:S(2)}, u32[]{:S(2)}) collective-permute-start(bf16[768,512]{1,0:T(8,128)(2,1)} %gate.27.refs_0_), channel_id=1, source_target_pairs={{0,1},{1,2},{2,3},{4,5},{5,6},{6,7},{8,9},{9,10},{10,11},{12,13},{... | collective-permute-start | bytes 2359304 | tf_op jit(solution)/shard_map/ppermute | solution.py:179
  290.3 13.5 %collective-permute-done.27.refs_0_.refs_2_ = bf16[768,512]{1,0:T(8,128)(2,1)S(1)} collective-permute-done((bf16[768,512]{1,0:T(8,128)(2,1)}, bf16[768,512]{1,0:T(8,128)(2,1)S(1)}, u32[]{:S(2)}, u32[]{:S(2)}) %collective-permute-start.27) | collective-permute-done | bytes 786464 | tf_op jit(solution)/shard_map/ppermute | solution.py:183
  312.9 13.6 %collective-permute-done.32.refs_0_ = bf16[768,512]{1,0:T(8,128)(2,1)} collective-permute-done((bf16[768,512]{1,0:T(8,128)(2,1)}, bf16[768,512]{1,0:T(8,128)(2,1)}, u32[]{:S(2)}, u32[]{:S(2)}) %collective-permute-start.32) | collective-permute-done | bytes 786464 | tf_op jit(solution)/shard_map/ppermute | solution.py:183
  338.3 10.9 %collective-permute-done.39.refs_4_.refs_14_ = bf16[512,1024]{1,0:T(8,128)(2,1)} collective-permute-done((bf16[512,1024]{1,0:T(8,128)(2,1)S(1)}, bf16[512,1024]{1,0:T(8,128)(2,1)}, u32[]{:S(2)}, u32[]{:S(2)}) %collective-permute-start.39) | collective-permute-done | bytes 1048608 | tf_op jit(solution)/shard_map/ppermute | solution.py:175
  355.5 13.2 %out_project.1 = (bf16[384,1024]{1,0:T(8,128)(2,1)}, bf16[384,1024]{1,0:T(8,128)(2,1)}) custom-call(s32[11]{0:T(128)} %concatenate.54.ids_ref, bf16[768,512]{1,0:T(8,128)(2,1)} %gate.27.refs_0_, bf16[768,512]{1,0:T(8,128)(2,1)} %collective-permute-done.26.refs_1_, bf16[768,512]{1,0:T(8,128)(2,1)} %pick_plan.7.refs_2_, ...), custom_call_target="tpu_custom_call" | custom-call | bytes 1024 | tf_op jit(solution)/shard_map/out_project/pallas_call | solution.py:590
  371.2 4.2 %fusion.2 = bf16[384,2048]{1,0:T(8,128)(2,1)} fusion(bf16[384,2048]{1,0:T(8,128)(2,1)S(1)} %copy-done.13, bf16[384,1024]{1,0:T(8,128)(2,1)S(1)} %collective-permute-done.42, bf16[384,1024]{1,0:T(8,128)(2,1)} %get-tuple-element.49, bf16[384,2048]{1,0:T(8,128)(2,1)} %collective-permute-done.22.refs_2_, bf16[384,2048]{1,0:T(8,128)(2,1)} %collective-permute-done.21.refs_1_, ...), kind=kLoop, calls=%fused_computation.5 | loop fusion | flops 16515072 | bytes 9437191 | tf_op jit(solution)/shard_map/convert_element_type | solution.py:848
  (194 shorter events, 112.1 us)
Async XLA Ops:
  9.4 56.6 %collective-permute-start.1 = (bf16[1936,512]{1,0:T(8,128)(2,1)}, bf16[1936,512]{1,0:T(8,128)(2,1)S(1)}, u32[]{:S(2)}, u32[]{:S(2)}) collective-permute-start(bf16[1936,512]{1,0:T(8,128)(2,1)} %get-tuple-element.28.refs_1_.refs_4_.refs_6_.refs_0_), channel_id=1, source_target_pairs={{0,8},{4,12},{8,0},{12,4},{16,24},{20,28},{24,16},{28,20},{1,9},{5... | collective-permute-start | bytes 5947400 | tf_op jit(solution)/shard_map/ppermute | solution.py:175
  12.4 53.6 %collective-permute-start.2 = (bf16[1936,512]{1,0:T(8,128)(2,1)}, bf16[1936,512]{1,0:T(8,128)(2,1)}, u32[]{:S(2)}, u32[]{:S(2)}) collective-permute-start(bf16[1936,512]{1,0:T(8,128)(2,1)} %get-tuple-element.28.refs_1_.refs_4_.refs_6_.refs_0_), channel_id=1, source_target_pairs={{0,16},{4,20},{8,24},{12,28},{16,0},{20,4},{24,8},{28,12},{1,17},{... | collective-permute-start | bytes 5947400 | tf_op jit(solution)/shard_map/ppermute | solution.py:175
  16.5 39.5 %collective-permute-start.8 = (bf16[400,2048]{1,0:T(8,128)(2,1)}, bf16[400,2048]{1,0:T(8,128)(2,1)}, u32[]{:S(2)}, u32[]{:S(2)}) collective-permute-start(bf16[400,2048]{1,0:T(8,128)(2,1)} %gate.20.refs_0_), channel_id=1, source_target_pairs={{0,1},{1,2},{2,3},{4,5},{5,6},{6,7},{8,9},{9,10},{10,11},{12,13},{... | collective-permute-start | bytes 4915208 | tf_op jit(solution)/shard_map/ppermute | solution.py:179
  21.2 40.1 %collective-permute-start.9 = (bf16[400,2048]{1,0:T(8,128)(2,1)}, bf16[400,2048]{1,0:T(8,128)(2,1)}, u32[]{:S(2)}, u32[]{:S(2)}) collective-permute-start(bf16[400,2048]{1,0:T(8,128)(2,1)} %gate.20.refs_0_), channel_id=1, source_target_pairs={{3,2},{2,1},{1,0},{7,6},{6,5},{5,4},{11,10},{10,9},{9,8},{15,14},{... | collective-permute-start | bytes 4915208 | tf_op jit(solution)/shard_map/ppermute | solution.py:183
  22.5 45.5 %collective-permute-start = (bf16[1936,512]{1,0:T(8,128)(2,1)}, bf16[1936,512]{1,0:T(8,128)(2,1)}, u32[]{:S(2)}, u32[]{:S(2)}) collective-permute-start(bf16[1936,512]{1,0:T(8,128)(2,1)} %get-tuple-element.29), channel_id=1, source_target_pairs={{0,4},{4,0},{8,12},{12,8},{16,20},{20,16},{24,28},{28,24},{1,5},{5... | collective-permute-start | bytes 5947400 | tf_op jit(solution)/shard_map/ppermute | solution.py:175
  67.3 66.9 %collective-permute-start.10 = (bf16[800,2048]{1,0:T(8,128)(2,1)}, bf16[800,2048]{1,0:T(8,128)(2,1)}, u32[]{:S(2)}, u32[]{:S(2)}) collective-permute-start(bf16[800,2048]{1,0:T(8,128)(2,1)} %gate.21.refs_0_), channel_id=1, source_target_pairs={{0,4},{4,0},{8,12},{12,8},{16,20},{20,16},{24,28},{28,24},{1,5},{5... | collective-permute-start | bytes 9830408 | tf_op jit(solution)/shard_map/ppermute | solution.py:175
  68.0 55.5 %collective-permute-start.3 = (bf16[1936,512]{1,0:T(8,128)(2,1)}, bf16[1936,512]{1,0:T(8,128)(2,1)S(1)}, u32[]{:S(2)}, u32[]{:S(2)}) collective-permute-start(bf16[1936,512]{1,0:T(8,128)(2,1)} %gate.16.refs_2_.refs_5_.refs_7_.refs_1_), channel_id=1, source_target_pairs={{0,8},{4,12},{8,0},{12,4},{16,24},{20,28},{24,16},{28,20},{1,9},{5... | collective-permute-start | bytes 5947400 | tf_op jit(solution)/shard_map/ppermute | solution.py:175
  68.6 54.9 %collective-permute-start.4 = (bf16[1936,512]{1,0:T(8,128)(2,1)}, bf16[1936,512]{1,0:T(8,128)(2,1)S(1)}, u32[]{:S(2)}, u32[]{:S(2)}) collective-permute-start(bf16[1936,512]{1,0:T(8,128)(2,1)} %gate.16.refs_2_.refs_5_.refs_7_.refs_1_), channel_id=1, source_target_pairs={{0,16},{4,20},{8,24},{12,28},{16,0},{20,4},{24,8},{28,12},{1,17},{... | collective-permute-start | bytes 5947400 | tf_op jit(solution)/shard_map/ppermute | solution.py:175
  76.0 37.8 %collective-permute-start.12 = (bf16[400,2048]{1,0:T(8,128)(2,1)}, bf16[400,2048]{1,0:T(8,128)(2,1)}, u32[]{:S(2)}, u32[]{:S(2)}) collective-permute-start(bf16[400,2048]{1,0:T(8,128)(2,1)} %get-tuple-element.32), channel_id=1, source_target_pairs={{0,1},{1,2},{2,3},{4,5},{5,6},{6,7},{8,9},{9,10},{10,11},{12,13},{... | collective-permute-start | bytes 4915208 | tf_op jit(solution)/shard_map/ppermute | solution.py:179
  79.5 39.6 %collective-permute-start.11 = (bf16[400,2048]{1,0:T(8,128)(2,1)}, bf16[400,2048]{1,0:T(8,128)(2,1)}, u32[]{:S(2)}, u32[]{:S(2)}) collective-permute-start(bf16[400,2048]{1,0:T(8,128)(2,1)} %get-tuple-element.31), channel_id=1, source_target_pairs={{3,2},{2,1},{1,0},{7,6},{6,5},{5,4},{11,10},{10,9},{9,8},{15,14},{... | collective-permute-start | bytes 4915208 | tf_op jit(solution)/shard_map/ppermute | solution.py:183
  126.0 48.4 %collective-permute-start.5 = (bf16[1936,512]{1,0:T(8,128)(2,1)}, bf16[1936,512]{1,0:T(8,128)(2,1)S(1)}, u32[]{:S(2)}, u32[]{:S(2)}) collective-permute-start(bf16[1936,512]{1,0:T(8,128)(2,1)} %gate.17.refs_6_.refs_8_.refs_2_), channel_id=1, source_target_pairs={{0,16},{4,20},{8,24},{12,28},{16,0},{20,4},{24,8},{28,12},{1,17},{... | collective-permute-start | bytes 5947400 | tf_op jit(solution)/shard_map/ppermute | solution.py:175
  127.6 46.9 %collective-permute-start.6 = (bf16[1936,512]{1,0:T(8,128)(2,1)}, bf16[1936,512]{1,0:T(8,128)(2,1)}, u32[]{:S(2)}, u32[]{:S(2)}) collective-permute-start(bf16[1936,512]{1,0:T(8,128)(2,1)} %gate.18.refs_9_.refs_11_.refs_5_), channel_id=1, source_target_pairs={{0,8},{4,12},{8,0},{12,4},{16,24},{20,28},{24,16},{28,20},{1,9},{5... | collective-permute-start | bytes 5947400 | tf_op jit(solution)/shard_map/ppermute | solution.py:175
  132.9 40.4 %collective-permute-start.14 = (bf16[400,2048]{1,0:T(8,128)(2,1)}, bf16[400,2048]{1,0:T(8,128)(2,1)}, u32[]{:S(2)}, u32[]{:S(2)}) collective-permute-start(bf16[400,2048]{1,0:T(8,128)(2,1)} %gate.22), channel_id=1, source_target_pairs={{3,2},{2,1},{1,0},{7,6},{6,5},{5,4},{11,10},{10,9},{9,8},{15,14},{... | collective-permute-start | bytes 4915208 | tf_op jit(solution)/shard_map/ppermute | solution.py:183
  134.2 40.3 %collective-permute-start.15 = (bf16[400,2048]{1,0:T(8,128)(2,1)}, bf16[400,2048]{1,0:T(8,128)(2,1)}, u32[]{:S(2)}, u32[]{:S(2)}) collective-permute-start(bf16[400,2048]{1,0:T(8,128)(2,1)} %gate.23), channel_id=1, source_target_pairs={{0,1},{1,2},{2,3},{4,5},{5,6},{6,7},{8,9},{9,10},{10,11},{12,13},{... | collective-permute-start | bytes 4915208 | tf_op jit(solution)/shard_map/ppermute | solution.py:179
  183.1 31.8 %collective-permute-start.18 = (bf16[512,512]{1,0:T(8,128)(2,1)}, bf16[512,512]{1,0:T(8,128)(2,1)S(1)}, u32[]{:S(2)}, u32[]{:S(2)}) collective-permute-start(bf16[512,512]{1,0:T(8,128)(2,1)} %gate.24), channel_id=1, source_target_pairs={{0,8},{4,12},{8,0},{12,4},{16,24},{20,28},{24,16},{28,20},{1,9},{5... | collective-permute-start | bytes 1572872 | tf_op jit(solution)/shard_map/ppermute | solution.py:175
  183.7 33.7 %collective-permute-start.19 = (bf16[512,512]{1,0:T(8,128)(2,1)}, bf16[512,512]{1,0:T(8,128)(2,1)S(1)}, u32[]{:S(2)}, u32[]{:S(2)}) collective-permute-start(bf16[512,512]{1,0:T(8,128)(2,1)} %gate.25), channel_id=1, source_target_pairs={{0,16},{4,20},{8,24},{12,28},{16,0},{20,4},{24,8},{28,12},{1,17},{... | collective-permute-start | bytes 1572872 | tf_op jit(solution)/shard_map/ppermute | solution.py:175
  189.1 87.0 %collective-permute-start.21 = (bf16[384,2048]{1,0:T(8,128)(2,1)}, bf16[384,2048]{1,0:T(8,128)(2,1)}, u32[]{:S(2)}, u32[]{:S(2)}) collective-permute-start(bf16[384,2048]{1,0:T(8,128)(2,1)} %get-tuple-element.42), channel_id=1, source_target_pairs={{0,1},{1,2},{2,3},{4,5},{5,6},{6,7},{8,9},{9,10},{10,11},{12,13},{... | collective-permute-start | bytes 4718600 | tf_op jit(solution)/shard_map/ppermute | solution.py:179
  195.1 81.0 %collective-permute-start.22 = (bf16[384,2048]{1,0:T(8,128)(2,1)}, bf16[384,2048]{1,0:T(8,128)(2,1)}, u32[]{:S(2)}, u32[]{:S(2)}) collective-permute-start(bf16[384,2048]{1,0:T(8,128)(2,1)} %get-tuple-element.43), channel_id=1, source_target_pairs={{3,2},{2,1},{1,0},{7,6},{6,5},{5,4},{11,10},{10,9},{9,8},{15,14},{... | collective-permute-start | bytes 4718600 | tf_op jit(solution)/shard_map/ppermute | solution.py:183
  222.3 34.1 %collective-permute-start.23 = (bf16[512,512]{1,0:T(8,128)(2,1)}, bf16[512,512]{1,0:T(8,128)(2,1)S(1)}, u32[]{:S(2)}, u32[]{:S(2)}) collective-permute-start(bf16[512,512]{1,0:T(8,128)(2,1)} %get-tuple-element.44), channel_id=1, source_target_pairs={{0,1},{1,0},{2,3},{3,2},{4,5},{5,4},{6,7},{7,6},{8,9},{9,8},{10,11... | collective-permute-start | bytes 1572872 | tf_op jit(solution)/shard_map/ppermute | solution.py:799
  225.0 42.5 %collective-permute-start.24 = (bf16[512,512]{1,0:T(8,128)(2,1)}, bf16[512,512]{1,0:T(8,128)(2,1)S(1)}, u32[]{:S(2)}, u32[]{:S(2)}) collective-permute-start(bf16[512,512]{1,0:T(8,128)(2,1)} %get-tuple-element.45), channel_id=1, source_target_pairs={{0,2},{1,3},{2,0},{3,1},{4,6},{5,7},{6,4},{7,5},{8,10},{9,11},{10,... | collective-permute-start | bytes 1572872 | tf_op jit(solution)/shard_map/ppermute | solution.py:799
  226.1 41.4 %collective-permute-start.25 = (bf16[512,512]{1,0:T(8,128)(2,1)}, bf16[512,512]{1,0:T(8,128)(2,1)S(1)}, u32[]{:S(2)}, u32[]{:S(2)}) collective-permute-start(bf16[512,512]{1,0:T(8,128)(2,1)} %get-tuple-element.46), channel_id=1, source_target_pairs={{0,3},{1,2},{2,1},{3,0},{4,7},{5,6},{6,5},{7,4},{8,11},{9,10},{10,... | collective-permute-start | bytes 1572872 | tf_op jit(solution)/shard_map/ppermute | solution.py:799
  273.1 32.2 %collective-permute-start.30 = (bf16[512,1024]{1,0:T(8,128)(2,1)}, bf16[512,1024]{1,0:T(8,128)(2,1)S(1)}, u32[]{:S(2)}, u32[]{:S(2)}) collective-permute-start(bf16[512,1024]{1,0:T(8,128)(2,1)} %get-tuple-element.47.refs_8_), channel_id=1, source_target_pairs={{0,8},{4,12},{8,0},{12,4},{16,24},{20,28},{24,16},{28,20},{1,9},{5... | collective-permute-start | bytes 3145736 | tf_op jit(solution)/shard_map/ppermute | solution.py:175
  289.7 41.4 %collective-permute-start.35 = (bf16[512,1024]{1,0:T(8,128)(2,1)}, bf16[512,1024]{1,0:T(8,128)(2,1)S(1)}, u32[]{:S(2)}, u32[]{:S(2)}) collective-permute-start(bf16[512,1024]{1,0:T(8,128)(2,1)} %get-tuple-element.48.refs_9_), channel_id=1, source_target_pairs={{0,8},{4,12},{8,0},{12,4},{16,24},{20,28},{24,16},{28,20},{1,9},{5... | collective-permute-start | bytes 3145736 | tf_op jit(solution)/shard_map/ppermute | solution.py:175
  311.3 37.9 %collective-permute-start.39 = (bf16[512,1024]{1,0:T(8,128)(2,1)S(1)}, bf16[512,1024]{1,0:T(8,128)(2,1)}, u32[]{:S(2)}, u32[]{:S(2)}) collective-permute-start(bf16[512,1024]{1,0:T(8,128)(2,1)S(1)} %copy-done.6), channel_id=1, source_target_pairs={{0,16},{4,20},{8,24},{12,28},{16,0},{20,4},{24,8},{28,12},{1,17},{... | collective-permute-start | bytes 3145736 | tf_op jit(solution)/shard_map/ppermute | solution.py:175
  (42 other events, 400.9 us)

commit v4 on v3

--- a/solution.py
+++ b/solution.py
@@ -411,7 +411,7 @@
     )(ids, *xs, *weights, *tables)
 
 
-BT = 256
+BT = 384
 BK = 1024
 CHAIN = 2
 
@@ -756,8 +756,7 @@
 
     third = pick(z, (d3, u1, d1, u3), here, (sums, far_own, far_other))
     over3 = swap(third, 1)
-    up, down = hops(here, pending, u3, d3, 1, (), (1, 2, 3), tok, (third,))
-    u4, d4 = hop_up(up, every), hop_down(down, every)
+    last_up, last_down = u3, d3
     mine, theirs = (
         squares(a) + squares(a, 1) + squares(b) + squares(c)
         for a, b, c in ((near, second, third), (over1, over2, over3))
@@ -796,7 +795,9 @@
 
     pieces = list(move(pieces_plan, ((2 * n_piece, q_cols),) * 4, here, by_chip, (q,)))
     for r in (1, 2, 3):
-        pieces[r] = lax.ppermute(pieces[r], "tp", [(i, i ^ r) for i in range(N_TP)])
+        pieces[r] = lax.ppermute(
+            gate(pieces[r], before), "tp", [(i, i ^ r) for i in range(N_TP)]
+        )
     attended = attend(
         bounds,
         here,
@@ -821,7 +822,7 @@
     wo_xa, wo_yb = swap(wo_a, 2), swap(wo_b, 4)
     wo_xb, wo_ya = swap(wo_b, 2), swap(wo_a, 4)
 
-    attended = gate(attended, u4, d4, *pieces[1:])
+    attended = gate(attended, *pieces[1:])
     u1, d1 = hop_up(attended, every), hop_down(attended, every)
     near = pick(z, (d1, d1, u1, u1), here)
 
@@ -830,6 +831,9 @@
     second = pick(z, (d2, d2, u2, u2), here)
     u3, d3 = hop_up(gate(u2, wo_xb, wo_ya), (2,)), hop_down(gate(d2, wo_xb, wo_ya), (2,))
     third = pick(z, (d3, u1, d1, u3), here, wo_parts[6:])
+
+    up, down = hops(here, pending, last_up, last_down, 1, (), (1, 2, 3), tok, (second,))
+    u4, d4 = hop_up(up, every), hop_down(down, every)
     hs = []
     for part in (attended, near, second, third):
         hs += [part, swap(part, 1)]

time: 378 us -> 393 us (1.040)
  waiting for transfers between devices: 151 us -> 163 us
    ppermute x7, waiting for transfers between devices: 55.2 us -> 67.8 us  [hop_down(): return lax.ppermute(v, 'tp', [(N_TP - 1 - i, N_TP - 2 - i) for i in pairs])]
    ppermute x25, starting transfers between devices: 20.7 us -> 28.7 us  [swap(): return lax.ppermute(x, 'ctx', [(c, c ^ bit) for c in range(N_CTX)])]
    ppermute x7, starting transfers between devices: 35.5 us -> 28.8 us  [hop_up(): return lax.ppermute(v, 'tp', [(i, i + 1) for i in pairs])]
    ppermute x3, waiting for transfers between devices: 16.3 us -> 10.9 us  [per_device(): lax.ppermute(gate(pieces[r], before), 'tp', [(i, i ^ r) for i in range(N_...]
    ppermute x7, waiting for transfers between devices: 63.6 us -> 68.4 us  [hop_up(): return lax.ppermute(v, 'tp', [(i, i + 1) for i in pairs])]
  transfers between devices with their start and end apart: 43 -> 43, of which waited for: 13 -> 15; matrix products, arithmetic and copies ran while one was open for 5% -> 5% of each run, Pallas kernels for 24% -> 26%
where the time goes in v4:
time: 393 us; the launch traced here: 390 us
  waiting for transfers between devices  163 us (41%)
  Pallas kernels  112 us (28%)
  starting transfers between devices  74.1 us (19%)
  other arithmetic  19.9 us (5%)
  local copies, waits for them, and re-layouts  17.2 us (4%)
    ppermute x7, waiting for transfers between devices, hop_up(): return lax.ppermute(v, 'tp', [(i, i + 1) for i in pairs])  68.4 us
    ppermute x7, waiting for transfers between devices, hop_down(): return lax.ppermute(v, 'tp', [(N_TP - 1 - i, N_TP - 2 - i) for i in pairs])  67.8 us
    pallas_call x10, Pallas kernels, move(): pl.pallas_call(kernel, out_shape=tuple((jax.ShapeDtypeStruct(shape, jnp.b...  37.7 us
    ppermute x7, starting transfers between devices, hop_up(): return lax.ppermute(v, 'tp', [(i, i + 1) for i in pairs])  28.8 us
    ppermute x25, starting transfers between devices, swap(): return lax.ppermute(x, 'ctx', [(c, c ^ bit) for c in range(N_CTX)])  28.7 us
    pallas_call x2, Pallas kernels, project(): pl.pallas_call(functools.partial(project_kernel, slots, len(xs), len(weig...  25.1 us
    pallas_call x1, Pallas kernels, attend(): pl.pallas_call(functools.partial(attend_kernel, at_old), out_shape=jax.Sh...  22.4 us
    ppermute x25, waiting for transfers between devices, swap(): return lax.ppermute(x, 'ctx', [(c, c ^ bit) for c in range(N_CTX)])  16 us
  transfers between devices with their start and end apart: 43, of which 15 were waited for; matrix products, arithmetic and copies ran while one was open for 5% of the time, Pallas kernels for 26%

profile of v4, /device:TPU:0, one launch (start us, length us, event | category | flops | bytes accessed | tf_op | source)
XLA Modules:
  0.0 389.6 jit_solution(8762482034363890773)
XLA Ops:
  4.4 5.0 %first_plan.1 = (bf16[1936,512]{1,0:T(8,128)(2,1)}, bf16[1936,512]{1,0:T(8,128)(2,1)}) custom-call(s32[3]{0:T(128)} %pad_add_fusion.1.ids_ref, bf16[1024,1024]{1,0:T(8,128)(2,1)} %refs_0_.2, bf16[1024,1024]{1,0:T(8,128)(2,1)} %refs_1_.1, bf16[1024,1024]{1,0:T(8,128)(2,1)} %refs_2_.1, bf16[8,768,128]{2,1,0:T(8,128)(2,1)} %refs_3_.1, ...), custom_call_target="tpu_custom_call" | custom-call | bytes 1024 | tf_op jit(solution)/shard_map/first_plan/pallas_call | solution.py:218
  16.6 4.8 %collective-permute-start.8 = (bf16[400,2048]{1,0:T(8,128)(2,1)}, bf16[400,2048]{1,0:T(8,128)(2,1)}, u32[]{:S(2)}, u32[]{:S(2)}) collective-permute-start(bf16[400,2048]{1,0:T(8,128)(2,1)} %gate.23.refs_0_), channel_id=1, source_target_pairs={{0,1},{1,2},{2,3},{4,5},{5,6},{6,7},{8,9},{9,10},{10,11},{12,13},{... | collective-permute-start | bytes 4915208 | tf_op jit(solution)/shard_map/ppermute | solution.py:179
  26.7 29.3 %collective-permute-done.8.refs_1_.up_ref = bf16[400,2048]{1,0:T(8,128)(2,1)} collective-permute-done((bf16[400,2048]{1,0:T(8,128)(2,1)}, bf16[400,2048]{1,0:T(8,128)(2,1)}, u32[]{:S(2)}, u32[]{:S(2)}) %collective-permute-start.8) | collective-permute-done | bytes 1638432 | tf_op jit(solution)/shard_map/ppermute | solution.py:179
  56.1 5.4 %collective-permute-done.9.refs_2_.down_ref = bf16[400,2048]{1,0:T(8,128)(2,1)} collective-permute-done((bf16[400,2048]{1,0:T(8,128)(2,1)}, bf16[400,2048]{1,0:T(8,128)(2,1)}, u32[]{:S(2)}, u32[]{:S(2)}) %collective-permute-start.9) | collective-permute-done | bytes 1638432 | tf_op jit(solution)/shard_map/ppermute | solution.py:183
  61.5 4.7 %near_plan.1.refs_0_ = bf16[800,2048]{1,0:T(8,128)(2,1)} custom-call(s32[3]{0:T(128)} %pad_add_fusion.1.ids_ref, bf16[400,2048]{1,0:T(8,128)(2,1)} %gate.23.refs_0_, bf16[400,2048]{1,0:T(8,128)(2,1)} %collective-permute-done.8.refs_1_.up_ref, bf16[400,2048]{1,0:T(8,128)(2,1)} %collective-permute-done.9.refs_2_.down_ref, ...), custom_call_target="tpu_custom_call" | custom-call | bytes 1024 | tf_op jit(solution)/shard_map/near_plan/pallas_call | solution.py:218
  80.9 33.0 %collective-permute-done.12.refs_1_.up_ref = bf16[400,2048]{1,0:T(8,128)(2,1)} collective-permute-done((bf16[400,2048]{1,0:T(8,128)(2,1)}, bf16[400,2048]{1,0:T(8,128)(2,1)}, u32[]{:S(2)}, u32[]{:S(2)}) %collective-permute-start.12) | collective-permute-done | bytes 1638432 | tf_op jit(solution)/shard_map/ppermute | solution.py:179
  113.8 5.3 %collective-permute-done.11.refs_0_.down_ref = bf16[400,2048]{1,0:T(8,128)(2,1)} collective-permute-done((bf16[400,2048]{1,0:T(8,128)(2,1)}, bf16[400,2048]{1,0:T(8,128)(2,1)}, u32[]{:S(2)}, u32[]{:S(2)}) %collective-permute-start.11) | collective-permute-done | bytes 1638432 | tf_op jit(solution)/shard_map/ppermute | solution.py:183
  134.2 5.7 %collective-permute-start.15 = (bf16[400,2048]{1,0:T(8,128)(2,1)}, bf16[400,2048]{1,0:T(8,128)(2,1)}, u32[]{:S(2)}, u32[]{:S(2)}) collective-permute-start(bf16[400,2048]{1,0:T(8,128)(2,1)} %gate.26), channel_id=1, source_target_pairs={{0,1},{1,2},{2,3},{4,5},{5,6},{6,7},{8,9},{9,10},{10,11},{12,13},{... | collective-permute-start | bytes 4915208 | tf_op jit(solution)/shard_map/ppermute | solution.py:179
  143.9 11.9 %project.2.refs_4_.refs_14_ = f32[768,768]{1,0:T(8,128)} custom-call(s32[11]{0:T(128)} %concatenate.54.ids_ref, bf16[800,2048]{1,0:T(8,128)(2,1)} %gate.24.refs_0_, bf16[800,2048]{1,0:T(8,128)(2,1)} %collective-permute-done.10.refs_1_, bf16[400,2048]{1,0:T(8,128)(2,1)} %pick_plan.5.refs_2_, bf16[400,2048]{1,0:T(8,128)(2,1)} %collective-permute-done.13.refs_3_, ...), custom_call_target="tpu_custom_call" | custom-call | bytes 1024 | tf_op jit(solution)/shard_map/project/pallas_call | solution.py:395
  155.8 17.4 %collective-permute-done.14.refs_0_.down_ref = bf16[400,2048]{1,0:T(8,128)(2,1)} collective-permute-done((bf16[400,2048]{1,0:T(8,128)(2,1)}, bf16[400,2048]{1,0:T(8,128)(2,1)}, u32[]{:S(2)}, u32[]{:S(2)}) %collective-permute-start.14) | collective-permute-done | bytes 1638432 | tf_op jit(solution)/shard_map/ppermute | solution.py:183
  189.6 13.2 %project.3 = (bf16[4,768,128]{2,1,0:T(8,128)(2,1)}, bf16[2,768,128]{2,1,0:T(8,128)(2,1)}, bf16[2,384,128]{2,1,0:T(8,128)(2,1)}) custom-call(s32[11]{0:T(128)} %concatenate.54.ids_ref, bf16[800,2048]{1,0:T(8,128)(2,1)} %gate.24.refs_0_, bf16[800,2048]{1,0:T(8,128)(2,1)} %collective-permute-done.10.refs_1_, bf16[400,2048]{1,0:T(8,128)(2,1)} %pick_plan.5.refs_2_, ...), custom_call_target="tpu_custom_call" | custom-call | bytes 1024 | tf_op jit(solution)/shard_map/project/pallas_call | solution.py:395
  222.4 22.4 %attend.1.refs_0_.refs_4_ = bf16[768,512]{1,0:T(8,128)(2,1)} custom-call(s32[2,2]{1,0:T(2,128)} %pad_add_fusion.bound_ref, s32[3]{0:T(128)} %pad_add_fusion.1.ids_ref, bf16[4,768,128]{2,1,0:T(8,128)(2,1)} %get-tuple-element.35.refs_4_.q_ref, s32[768,128]{1,0:T(8,128)} %broadcast_in_dim.16.n_ref, s32[768,128]{1,0:T(8,128)} %broadcast_in_dim.17.lo_ref, ...), custom_call_target="tpu_custom_call" | custom-call | bytes 1024 | tf_op jit(solution)/shard_map/attend/pallas_call | solution.py:518
  244.9 10.8 %collective-permute-done.22.refs_2_ = bf16[512,512]{1,0:T(8,128)(2,1)S(1)} collective-permute-done((bf16[512,512]{1,0:T(8,128)(2,1)}, bf16[512,512]{1,0:T(8,128)(2,1)S(1)}, u32[]{:S(2)}, u32[]{:S(2)}) %collective-permute-start.22) | collective-permute-done | bytes 524320 | tf_op jit(solution)/shard_map/ppermute | solution.py:798
  262.8 7.3 %collective-permute-start.29 = (bf16[512,1024]{1,0:T(8,128)(2,1)}, bf16[512,1024]{1,0:T(8,128)(2,1)S(1)}, u32[]{:S(2)}, u32[]{:S(2)}) collective-permute-start(bf16[512,1024]{1,0:T(8,128)(2,1)} %get-tuple-element.46.refs_9_), channel_id=1, source_target_pairs={{0,16},{4,20},{8,24},{12,28},{16,0},{20,4},{24,8},{28,12},{1,17},{... | collective-permute-start | bytes 3145736 | tf_op jit(solution)/shard_map/ppermute | solution.py:175
  271.4 4.8 %collective-permute-start.26 = (bf16[768,512]{1,0:T(8,128)(2,1)}, bf16[768,512]{1,0:T(8,128)(2,1)S(1)}, u32[]{:S(2)}, u32[]{:S(2)}) collective-permute-start(bf16[768,512]{1,0:T(8,128)(2,1)} %gate.33.refs_0_), channel_id=1, source_target_pairs={{0,1},{1,2},{2,3},{4,5},{5,6},{6,7},{8,9},{9,10},{10,11},{12,13},{... | collective-permute-start | bytes 2359304 | tf_op jit(solution)/shard_map/ppermute | solution.py:179
  277.7 12.1 %collective-permute-done.25.refs_0_.refs_2_ = bf16[768,512]{1,0:T(8,128)(2,1)S(1)} collective-permute-done((bf16[768,512]{1,0:T(8,128)(2,1)}, bf16[768,512]{1,0:T(8,128)(2,1)S(1)}, u32[]{:S(2)}, u32[]{:S(2)}) %collective-permute-start.25) | collective-permute-done | bytes 786464 | tf_op jit(solution)/shard_map/ppermute | solution.py:183
  300.6 12.6 %collective-permute-done.30.refs_0_ = bf16[768,512]{1,0:T(8,128)(2,1)} collective-permute-done((bf16[768,512]{1,0:T(8,128)(2,1)}, bf16[768,512]{1,0:T(8,128)(2,1)}, u32[]{:S(2)}, u32[]{:S(2)}) %collective-permute-start.30) | collective-permute-done | bytes 786464 | tf_op jit(solution)/shard_map/ppermute | solution.py:183
  317.8 4.4 %collective-permute-done.34.refs_2_.refs_12_ = bf16[512,1024]{1,0:T(8,128)(2,1)} collective-permute-done((bf16[512,1024]{1,0:T(8,128)(2,1)}, bf16[512,1024]{1,0:T(8,128)(2,1)}, u32[]{:S(2)}, u32[]{:S(2)}) %collective-permute-start.34) | collective-permute-done | bytes 1048608 | tf_op jit(solution)/shard_map/ppermute | solution.py:175
  328.3 5.1 %hops.5 = (bf16[384,2048]{1,0:T(8,128)(2,1)}, bf16[384,2048]{1,0:T(8,128)(2,1)}) custom-call(s32[3]{0:T(128)} %pad_add_fusion.1.ids_ref, bf16[1,384,8192]{2,1,0:T(8,128)(2,1)} %pending_ref.5, bf16[400,2048]{1,0:T(8,128)(2,1)} %collective-permute-done.15.refs_3_.up_ref, bf16[400,2048]{1,0:T(8,128)(2,1)} %collective-permute-done.14.refs_0_.down_ref, ...), custom_call_target="tpu_custom_call" | custom-call | bytes 1024 | tf_op jit(solution)/shard_map/hops/pallas_call | solution.py:295
  333.3 6.9 %collective-permute-done.37.refs_4_.refs_14_ = bf16[512,1024]{1,0:T(8,128)(2,1)} collective-permute-done((bf16[512,1024]{1,0:T(8,128)(2,1)S(1)}, bf16[512,1024]{1,0:T(8,128)(2,1)}, u32[]{:S(2)}, u32[]{:S(2)}) %collective-permute-start.37) | collective-permute-done | bytes 1048608 | tf_op jit(solution)/shard_map/ppermute | solution.py:175
  345.3 6.7 %collective-permute-start.41 = (bf16[384,2048]{1,0:T(8,128)(2,1)}, bf16[384,2048]{1,0:T(8,128)(2,1)}, u32[]{:S(2)}, u32[]{:S(2)}) collective-permute-start(bf16[384,2048]{1,0:T(8,128)(2,1)} %get-tuple-element.49), channel_id=1, source_target_pairs={{0,1},{1,2},{2,3},{4,5},{5,6},{6,7},{8,9},{9,10},{10,11},{12,13},{... | collective-permute-start | bytes 4718600 | tf_op jit(solution)/shard_map/ppermute | solution.py:179
  352.0 13.2 %out_project.1 = (bf16[384,1024]{1,0:T(8,128)(2,1)}, bf16[384,1024]{1,0:T(8,128)(2,1)}) custom-call(s32[11]{0:T(128)} %concatenate.54.ids_ref, bf16[768,512]{1,0:T(8,128)(2,1)} %gate.33.refs_0_, bf16[768,512]{1,0:T(8,128)(2,1)} %collective-permute-done.24.refs_1_, bf16[768,512]{1,0:T(8,128)(2,1)} %pick_plan.7.refs_2_, ...), custom_call_target="tpu_custom_call" | custom-call | bytes 1024 | tf_op jit(solution)/shard_map/out_project/pallas_call | solution.py:590
  365.4 15.0 %collective-permute-done.42 = bf16[384,2048]{1,0:T(8,128)(2,1)} collective-permute-done((bf16[384,2048]{1,0:T(8,128)(2,1)}, bf16[384,2048]{1,0:T(8,128)(2,1)}, u32[]{:S(2)}, u32[]{:S(2)}) %collective-permute-start.42) | collective-permute-done | bytes 1572896 | tf_op jit(solution)/shard_map/ppermute | solution.py:183
  380.5 4.9 %collective-permute-done.41 = bf16[384,2048]{1,0:T(8,128)(2,1)} collective-permute-done((bf16[384,2048]{1,0:T(8,128)(2,1)}, bf16[384,2048]{1,0:T(8,128)(2,1)}, u32[]{:S(2)}, u32[]{:S(2)}) %collective-permute-start.41) | collective-permute-done | bytes 1572896 | tf_op jit(solution)/shard_map/ppermute | solution.py:179
  (197 shorter events, 124.5 us)
Async XLA Ops:
  9.5 56.7 %collective-permute-start.1 = (bf16[1936,512]{1,0:T(8,128)(2,1)}, bf16[1936,512]{1,0:T(8,128)(2,1)S(1)}, u32[]{:S(2)}, u32[]{:S(2)}) collective-permute-start(bf16[1936,512]{1,0:T(8,128)(2,1)} %get-tuple-element.28.refs_1_.refs_4_.refs_6_.refs_0_), channel_id=1, source_target_pairs={{0,8},{4,12},{8,0},{12,4},{16,24},{20,28},{24,16},{28,20},{1,9},{5... | collective-permute-start | bytes 5947400 | tf_op jit(solution)/shard_map/ppermute | solution.py:175
  12.5 53.7 %collective-permute-start.2 = (bf16[1936,512]{1,0:T(8,128)(2,1)}, bf16[1936,512]{1,0:T(8,128)(2,1)}, u32[]{:S(2)}, u32[]{:S(2)}) collective-permute-start(bf16[1936,512]{1,0:T(8,128)(2,1)} %get-tuple-element.28.refs_1_.refs_4_.refs_6_.refs_0_), channel_id=1, source_target_pairs={{0,16},{4,20},{8,24},{12,28},{16,0},{20,4},{24,8},{28,12},{1,17},{... | collective-permute-start | bytes 5947400 | tf_op jit(solution)/shard_map/ppermute | solution.py:175
  16.6 39.5 %collective-permute-start.8 = (bf16[400,2048]{1,0:T(8,128)(2,1)}, bf16[400,2048]{1,0:T(8,128)(2,1)}, u32[]{:S(2)}, u32[]{:S(2)}) collective-permute-start(bf16[400,2048]{1,0:T(8,128)(2,1)} %gate.23.refs_0_), channel_id=1, source_target_pairs={{0,1},{1,2},{2,3},{4,5},{5,6},{6,7},{8,9},{9,10},{10,11},{12,13},{... | collective-permute-start | bytes 4915208 | tf_op jit(solution)/shard_map/ppermute | solution.py:179
  21.3 40.1 %collective-permute-start.9 = (bf16[400,2048]{1,0:T(8,128)(2,1)}, bf16[400,2048]{1,0:T(8,128)(2,1)}, u32[]{:S(2)}, u32[]{:S(2)}) collective-permute-start(bf16[400,2048]{1,0:T(8,128)(2,1)} %gate.23.refs_0_), channel_id=1, source_target_pairs={{3,2},{2,1},{1,0},{7,6},{6,5},{5,4},{11,10},{10,9},{9,8},{15,14},{... | collective-permute-start | bytes 4915208 | tf_op jit(solution)/shard_map/ppermute | solution.py:183
  22.6 45.5 %collective-permute-start = (bf16[1936,512]{1,0:T(8,128)(2,1)}, bf16[1936,512]{1,0:T(8,128)(2,1)}, u32[]{:S(2)}, u32[]{:S(2)}) collective-permute-start(bf16[1936,512]{1,0:T(8,128)(2,1)} %get-tuple-element.29), channel_id=1, source_target_pairs={{0,4},{4,0},{8,12},{12,8},{16,20},{20,16},{24,28},{28,24},{1,5},{5... | collective-permute-start | bytes 5947400 | tf_op jit(solution)/shard_map/ppermute | solution.py:175
  67.4 66.7 %collective-permute-start.10 = (bf16[800,2048]{1,0:T(8,128)(2,1)}, bf16[800,2048]{1,0:T(8,128)(2,1)}, u32[]{:S(2)}, u32[]{:S(2)}) collective-permute-start(bf16[800,2048]{1,0:T(8,128)(2,1)} %gate.24.refs_0_), channel_id=1, source_target_pairs={{0,4},{4,0},{8,12},{12,8},{16,20},{20,16},{24,28},{28,24},{1,5},{5... | collective-permute-start | bytes 9830408 | tf_op jit(solution)/shard_map/ppermute | solution.py:175
  68.1 55.4 %collective-permute-start.3 = (bf16[1936,512]{1,0:T(8,128)(2,1)}, bf16[1936,512]{1,0:T(8,128)(2,1)S(1)}, u32[]{:S(2)}, u32[]{:S(2)}) collective-permute-start(bf16[1936,512]{1,0:T(8,128)(2,1)} %gate.19.refs_2_.refs_5_.refs_7_.refs_1_), channel_id=1, source_target_pairs={{0,8},{4,12},{8,0},{12,4},{16,24},{20,28},{24,16},{28,20},{1,9},{5... | collective-permute-start | bytes 5947400 | tf_op jit(solution)/shard_map/ppermute | solution.py:175
  68.7 54.8 %collective-permute-start.4 = (bf16[1936,512]{1,0:T(8,128)(2,1)}, bf16[1936,512]{1,0:T(8,128)(2,1)S(1)}, u32[]{:S(2)}, u32[]{:S(2)}) collective-permute-start(bf16[1936,512]{1,0:T(8,128)(2,1)} %gate.19.refs_2_.refs_5_.refs_7_.refs_1_), channel_id=1, source_target_pairs={{0,16},{4,20},{8,24},{12,28},{16,0},{20,4},{24,8},{28,12},{1,17},{... | collective-permute-start | bytes 5947400 | tf_op jit(solution)/shard_map/ppermute | solution.py:175
  76.1 37.7 %collective-permute-start.12 = (bf16[400,2048]{1,0:T(8,128)(2,1)}, bf16[400,2048]{1,0:T(8,128)(2,1)}, u32[]{:S(2)}, u32[]{:S(2)}) collective-permute-start(bf16[400,2048]{1,0:T(8,128)(2,1)} %get-tuple-element.32), channel_id=1, source_target_pairs={{0,1},{1,2},{2,3},{4,5},{5,6},{6,7},{8,9},{9,10},{10,11},{12,13},{... | collective-permute-start | bytes 4915208 | tf_op jit(solution)/shard_map/ppermute | solution.py:179
  79.6 39.6 %collective-permute-start.11 = (bf16[400,2048]{1,0:T(8,128)(2,1)}, bf16[400,2048]{1,0:T(8,128)(2,1)}, u32[]{:S(2)}, u32[]{:S(2)}) collective-permute-start(bf16[400,2048]{1,0:T(8,128)(2,1)} %get-tuple-element.31), channel_id=1, source_target_pairs={{3,2},{2,1},{1,0},{7,6},{6,5},{5,4},{11,10},{10,9},{9,8},{15,14},{... | collective-permute-start | bytes 4915208 | tf_op jit(solution)/shard_map/ppermute | solution.py:183
  126.1 48.3 %collective-permute-start.5 = (bf16[1936,512]{1,0:T(8,128)(2,1)}, bf16[1936,512]{1,0:T(8,128)(2,1)S(1)}, u32[]{:S(2)}, u32[]{:S(2)}) collective-permute-start(bf16[1936,512]{1,0:T(8,128)(2,1)} %gate.20.refs_6_.refs_8_.refs_2_), channel_id=1, source_target_pairs={{0,16},{4,20},{8,24},{12,28},{16,0},{20,4},{24,8},{28,12},{1,17},{... | collective-permute-start | bytes 5947400 | tf_op jit(solution)/shard_map/ppermute | solution.py:175
  127.6 46.8 %collective-permute-start.6 = (bf16[1936,512]{1,0:T(8,128)(2,1)}, bf16[1936,512]{1,0:T(8,128)(2,1)}, u32[]{:S(2)}, u32[]{:S(2)}) collective-permute-start(bf16[1936,512]{1,0:T(8,128)(2,1)} %gate.21.refs_9_.refs_11_.refs_5_), channel_id=1, source_target_pairs={{0,8},{4,12},{8,0},{12,4},{16,24},{20,28},{24,16},{28,20},{1,9},{5... | collective-permute-start | bytes 5947400 | tf_op jit(solution)/shard_map/ppermute | solution.py:175
  132.8 40.4 %collective-permute-start.14 = (bf16[400,2048]{1,0:T(8,128)(2,1)}, bf16[400,2048]{1,0:T(8,128)(2,1)}, u32[]{:S(2)}, u32[]{:S(2)}) collective-permute-start(bf16[400,2048]{1,0:T(8,128)(2,1)} %gate.25), channel_id=1, source_target_pairs={{3,2},{2,1},{1,0},{7,6},{6,5},{5,4},{11,10},{10,9},{9,8},{15,14},{... | collective-permute-start | bytes 4915208 | tf_op jit(solution)/shard_map/ppermute | solution.py:183
  134.2 40.3 %collective-permute-start.15 = (bf16[400,2048]{1,0:T(8,128)(2,1)}, bf16[400,2048]{1,0:T(8,128)(2,1)}, u32[]{:S(2)}, u32[]{:S(2)}) collective-permute-start(bf16[400,2048]{1,0:T(8,128)(2,1)} %gate.26), channel_id=1, source_target_pairs={{0,1},{1,2},{2,3},{4,5},{5,6},{6,7},{8,9},{9,10},{10,11},{12,13},{... | collective-permute-start | bytes 4915208 | tf_op jit(solution)/shard_map/ppermute | solution.py:179
  214.8 30.1 %collective-permute-start.21 = (bf16[512,512]{1,0:T(8,128)(2,1)}, bf16[512,512]{1,0:T(8,128)(2,1)S(1)}, u32[]{:S(2)}, u32[]{:S(2)}) collective-permute-start(bf16[512,512]{1,0:T(8,128)(2,1)} %gate.30), channel_id=1, source_target_pairs={{0,1},{1,0},{2,3},{3,2},{4,5},{5,4},{6,7},{7,6},{8,9},{9,8},{10,11... | collective-permute-start | bytes 1572872 | tf_op jit(solution)/shard_map/ppermute | solution.py:798
  217.3 38.4 %collective-permute-start.22 = (bf16[512,512]{1,0:T(8,128)(2,1)}, bf16[512,512]{1,0:T(8,128)(2,1)S(1)}, u32[]{:S(2)}, u32[]{:S(2)}) collective-permute-start(bf16[512,512]{1,0:T(8,128)(2,1)} %gate.31), channel_id=1, source_target_pairs={{0,2},{1,3},{2,0},{3,1},{4,6},{5,7},{6,4},{7,5},{8,10},{9,11},{10,... | collective-permute-start | bytes 1572872 | tf_op jit(solution)/shard_map/ppermute | solution.py:798
  219.2 36.5 %collective-permute-start.23 = (bf16[512,512]{1,0:T(8,128)(2,1)}, bf16[512,512]{1,0:T(8,128)(2,1)S(1)}, u32[]{:S(2)}, u32[]{:S(2)}) collective-permute-start(bf16[512,512]{1,0:T(8,128)(2,1)} %gate.32), channel_id=1, source_target_pairs={{0,3},{1,2},{2,1},{3,0},{4,7},{5,6},{6,5},{7,4},{8,11},{9,10},{10,... | collective-permute-start | bytes 1572872 | tf_op jit(solution)/shard_map/ppermute | solution.py:798
  261.3 29.5 %collective-permute-start.28 = (bf16[512,1024]{1,0:T(8,128)(2,1)}, bf16[512,1024]{1,0:T(8,128)(2,1)S(1)}, u32[]{:S(2)}, u32[]{:S(2)}) collective-permute-start(bf16[512,1024]{1,0:T(8,128)(2,1)} %get-tuple-element.45.refs_8_), channel_id=1, source_target_pairs={{0,8},{4,12},{8,0},{12,4},{16,24},{20,28},{24,16},{28,20},{1,9},{5... | collective-permute-start | bytes 3145736 | tf_op jit(solution)/shard_map/ppermute | solution.py:175
  262.8 29.3 %collective-permute-start.29 = (bf16[512,1024]{1,0:T(8,128)(2,1)}, bf16[512,1024]{1,0:T(8,128)(2,1)S(1)}, u32[]{:S(2)}, u32[]{:S(2)}) collective-permute-start(bf16[512,1024]{1,0:T(8,128)(2,1)} %get-tuple-element.46.refs_9_), channel_id=1, source_target_pairs={{0,16},{4,20},{8,24},{12,28},{16,0},{20,4},{24,8},{28,12},{1,17},{... | collective-permute-start | bytes 3145736 | tf_op jit(solution)/shard_map/ppermute | solution.py:175
  276.2 41.6 %collective-permute-start.33 = (bf16[512,1024]{1,0:T(8,128)(2,1)}, bf16[512,1024]{1,0:T(8,128)(2,1)S(1)}, u32[]{:S(2)}, u32[]{:S(2)}) collective-permute-start(bf16[512,1024]{1,0:T(8,128)(2,1)} %get-tuple-element.46.refs_9_), channel_id=1, source_target_pairs={{0,8},{4,12},{8,0},{12,4},{16,24},{20,28},{24,16},{28,20},{1,9},{5... | collective-permute-start | bytes 3145736 | tf_op jit(solution)/shard_map/ppermute | solution.py:175
  294.5 27.7 %collective-permute-start.34 = (bf16[512,1024]{1,0:T(8,128)(2,1)}, bf16[512,1024]{1,0:T(8,128)(2,1)}, u32[]{:S(2)}, u32[]{:S(2)}) collective-permute-start(bf16[512,1024]{1,0:T(8,128)(2,1)} %get-tuple-element.45.refs_8_), channel_id=1, source_target_pairs={{0,16},{4,20},{8,24},{12,28},{16,0},{20,4},{24,8},{28,12},{1,17},{... | collective-permute-start | bytes 3145736 | tf_op jit(solution)/shard_map/ppermute | solution.py:175
  300.6 39.6 %collective-permute-start.37 = (bf16[512,1024]{1,0:T(8,128)(2,1)S(1)}, bf16[512,1024]{1,0:T(8,128)(2,1)}, u32[]{:S(2)}, u32[]{:S(2)}) collective-permute-start(bf16[512,1024]{1,0:T(8,128)(2,1)S(1)} %copy-done.6), channel_id=1, source_target_pairs={{0,16},{4,20},{8,24},{12,28},{16,0},{20,4},{24,8},{28,12},{1,17},{... | collective-permute-start | bytes 3145736 | tf_op jit(solution)/shard_map/ppermute | solution.py:175
  340.8 39.7 %collective-permute-start.42 = (bf16[384,2048]{1,0:T(8,128)(2,1)}, bf16[384,2048]{1,0:T(8,128)(2,1)}, u32[]{:S(2)}, u32[]{:S(2)}) collective-permute-start(bf16[384,2048]{1,0:T(8,128)(2,1)} %get-tuple-element.50), channel_id=1, source_target_pairs={{3,2},{2,1},{1,0},{7,6},{6,5},{5,4},{11,10},{10,9},{9,8},{15,14},{... | collective-permute-start | bytes 4718600 | tf_op jit(solution)/shard_map/ppermute | solution.py:183
  345.3 40.1 %collective-permute-start.41 = (bf16[384,2048]{1,0:T(8,128)(2,1)}, bf16[384,2048]{1,0:T(8,128)(2,1)}, u32[]{:S(2)}, u32[]{:S(2)}) collective-permute-start(bf16[384,2048]{1,0:T(8,128)(2,1)} %get-tuple-element.49), channel_id=1, source_target_pairs={{0,1},{1,2},{2,3},{4,5},{5,6},{6,7},{8,9},{9,10},{10,11},{12,13},{... | collective-permute-start | bytes 4718600 | tf_op jit(solution)/shard_map/ppermute | solution.py:179
  (42 other events, 434.4 us)

commit v5 on v3

--- a/solution.py
+++ b/solution.py
@@ -730,7 +730,7 @@
         (own,),
     )
     given = gate(given, x1, y1)
-    up, down = hops(here, pending, u1, d1, 3, (1, 2, 3), (), n_rows, (cosine, sinus, given))
+    up, down = hops(here, pending, u1, d1, 3, (1, 2, 3), (), n_rows, (cosine, sinus, given, by_chip[0]))
     u2, d2 = hop_up(up, every), hop_down(down, every)
     x2, y2 = swap(given, 2), swap(given, 4)
 
@@ -740,15 +740,15 @@
         near = [(at[2] < 2, down_part), (at[2] >= 2, up_part)]
         yield (near, out[0].at[pl.ds(n_rows, n_rows)])
 
-    (near,) = move(near_plan, ((2 * n_rows, feat),), here, (scaled, u1, d1), (by_chip[0],))
-    near = gate(near, x1, y1)
+    (near,) = move(near_plan, ((2 * n_rows, feat),), here, (scaled, u1, d1), (up,))
+
+    x1, y2 = gate(x1, x2, y2, u2, d2), gate(y2, x2, u2, d2)
+    up, down = hops(here, pending, u2, d2, 2, (2,), (1,), n_rows, (x1, y2, near))
+    u3, d3 = hop_up(up, every), hop_down(down, every)
+    far_own, far_other = swap(x1, 4), swap(y2, 2)
+    near = gate(near, up)
     over1 = swap(near, 1)
-
-    up, down = hops(here, pending, u2, d2, 2, (2,), (1,), n_rows)
-    u3, d3 = hop_up(gate(up, x2), every), hop_down(gate(down, y2), every)
-    x1, y2 = gate(x1, x2, y2), gate(y2, x2)
-    far_own, far_other = swap(x1, 4), swap(y2, 2)
-    second = pick(z, (d2, d2, u2, u2), here)
+    second = pick(z, (d2, d2, u2, u2), here, (up,))
     over2 = swap(second, 1)
     own_rows = (own, given, x1, x2, y1, y2, far_own, far_other)
     xs = [near, over1, second, over2]
@@ -796,7 +796,9 @@
 
     pieces = list(move(pieces_plan, ((2 * n_piece, q_cols),) * 4, here, by_chip, (q,)))
     for r in (1, 2, 3):
-        pieces[r] = lax.ppermute(pieces[r], "tp", [(i, i ^ r) for i in range(N_TP)])
+        pieces[r] = lax.ppermute(
+            gate(pieces[r], before), "tp", [(i, i ^ r) for i in range(N_TP)]
+        )
     attended = attend(
         bounds,
         here,
@@ -828,8 +830,8 @@
     wo_parts = (wo_a, wo_b, wo_xa, wo_xb, wo_ya, wo_yb, swap(wo_xa, 4), swap(wo_yb, 2))
     u2, d2 = hop_up(gate(u1, wo_xa, wo_yb), (1, 2)), hop_down(gate(d1, wo_xa, wo_yb), (1, 2))
     second = pick(z, (d2, d2, u2, u2), here)
-    u3, d3 = hop_up(gate(u2, wo_xb, wo_ya), (2,)), hop_down(gate(d2, wo_xb, wo_ya), (2,))
-    third = pick(z, (d3, u1, d1, u3), here, wo_parts[6:])
+    u3, d3 = hop_up(gate(u2, wo_ya), (2,)), hop_down(gate(d2, wo_ya), (2,))
+    third = pick(z, (d3, u1, d1, u3), here, wo_parts[6:] + (wo_xb,))
     hs = []
     for part in (attended, near, second, third):
         hs += [part, swap(part, 1)]

time: 378 us -> 380 us (level)
  waiting for transfers between devices: 151 us -> 156 us
    ppermute x25, waiting for transfers between devices: 15.9 us -> 57.3 us  [swap(): return lax.ppermute(x, 'ctx', [(c, c ^ bit) for c in range(N_CTX)])]
    ppermute x7, waiting for transfers between devices: 63.6 us -> 29.2 us  [hop_up(): return lax.ppermute(v, 'tp', [(i, i + 1) for i in pairs])]
    ppermute x7, waiting for transfers between devices: 55.2 us -> 49.5 us  [hop_down(): return lax.ppermute(v, 'tp', [(N_TP - 1 - i, N_TP - 2 - i) for i in pairs])]
    unnamed x48 -> x50, local copies, waits for them, and re-layouts: 12.7 us -> 12.1 us
  transfers between devices with their start and end apart: 43 -> 43, of which waited for: 13 -> 18; matrix products, arithmetic and copies ran while one was open for 5% -> 5% of each run, Pallas kernels for 24% -> 22%
where the time goes in v5:
time: 380 us; the launch traced here: 374 us
  waiting for transfers between devices  156 us (41%)
  Pallas kernels  108 us (28%)
  starting transfers between devices  70.7 us (19%)
  other arithmetic  19.7 us (5%)
  local copies, waits for them, and re-layouts  17 us (4%)
    ppermute x25, waiting for transfers between devices, swap(): return lax.ppermute(x, 'ctx', [(c, c ^ bit) for c in range(N_CTX)])  57.3 us
    ppermute x7, waiting for transfers between devices, hop_down(): return lax.ppermute(v, 'tp', [(N_TP - 1 - i, N_TP - 2 - i) for i in pairs])  49.5 us
    pallas_call x10, Pallas kernels, move(): pl.pallas_call(kernel, out_shape=tuple((jax.ShapeDtypeStruct(shape, jnp.b...  37.8 us
    ppermute x7, starting transfers between devices, hop_up(): return lax.ppermute(v, 'tp', [(i, i + 1) for i in pairs])  32.1 us
    ppermute x7, waiting for transfers between devices, hop_up(): return lax.ppermute(v, 'tp', [(i, i + 1) for i in pairs])  29.2 us
    pallas_call x2, Pallas kernels, project(): pl.pallas_call(functools.partial(project_kernel, slots, len(xs), len(weig...  25.2 us
    ppermute x25, starting transfers between devices, swap(): return lax.ppermute(x, 'ctx', [(c, c ^ bit) for c in range(N_CTX)])  21.9 us
    ppermute x3, waiting for transfers between devices, per_device(): lax.ppermute(gate(pieces[r], before), 'tp', [(i, i ^ r) for i in range(N_...  19.8 us
  transfers between devices with their start and end apart: 43, of which 18 were waited for; matrix products, arithmetic and copies ran while one was open for 5% of the time, Pallas kernels for 22%

profile of v5, /device:TPU:0, one launch (start us, length us, event | category | flops | bytes accessed | tf_op | source)
XLA Modules:
  0.0 373.9 jit_solution(4429915714972140037)
XLA Ops:
  4.3 5.0 %first_plan.1 = (bf16[1936,512]{1,0:T(8,128)(2,1)}, bf16[1936,512]{1,0:T(8,128)(2,1)}) custom-call(s32[3]{0:T(128)} %pad_add_fusion.1.ids_ref, bf16[1024,1024]{1,0:T(8,128)(2,1)} %refs_0_.2, bf16[1024,1024]{1,0:T(8,128)(2,1)} %refs_1_.1, bf16[1024,1024]{1,0:T(8,128)(2,1)} %refs_2_.1, bf16[8,768,128]{2,1,0:T(8,128)(2,1)} %refs_3_.1, ...), custom_call_target="tpu_custom_call" | custom-call | bytes 1024 | tf_op jit(solution)/shard_map/first_plan/pallas_call | solution.py:218
  18.2 4.7 %collective-permute-start.6 = (bf16[400,2048]{1,0:T(8,128)(2,1)}, bf16[400,2048]{1,0:T(8,128)(2,1)}, u32[]{:S(2)}, u32[]{:S(2)}) collective-permute-start(bf16[400,2048]{1,0:T(8,128)(2,1)} %gate.19.refs_0_), channel_id=1, source_target_pairs={{0,1},{1,2},{2,3},{4,5},{5,6},{6,7},{8,9},{9,10},{10,11},{12,13},{... | collective-permute-start | bytes 4915208 | tf_op jit(solution)/shard_map/ppermute | solution.py:179
  28.7 27.0 %collective-permute-done.1.refs_1_.refs_0_ = bf16[1936,512]{1,0:T(8,128)(2,1)S(1)} collective-permute-done((bf16[1936,512]{1,0:T(8,128)(2,1)}, bf16[1936,512]{1,0:T(8,128)(2,1)S(1)}, u32[]{:S(2)}, u32[]{:S(2)}) %collective-permute-start.1) | collective-permute-done | bytes 1982496 | tf_op jit(solution)/shard_map/ppermute | solution.py:175
  62.8 4.3 %hops.3 = (bf16[400,2048]{1,0:T(8,128)(2,1)}, bf16[400,2048]{1,0:T(8,128)(2,1)}) custom-call(s32[3]{0:T(128)} %pad_add_fusion.1.ids_ref, bf16[1,384,8192]{2,1,0:T(8,128)(2,1)} %pending_ref.5, bf16[400,2048]{1,0:T(8,128)(2,1)} %collective-permute-done.6.up_ref.refs_1_, bf16[400,2048]{1,0:T(8,128)(2,1)} %collective-permute-done.7.down_ref.refs_2_, ...), custom_call_target="tpu_custom_call" | custom-call | bytes 1024 | tf_op jit(solution)/shard_map/hops/pallas_call | solution.py:295
  67.1 4.7 %collective-permute-start.8 = (bf16[400,2048]{1,0:T(8,128)(2,1)}, bf16[400,2048]{1,0:T(8,128)(2,1)}, u32[]{:S(2)}, u32[]{:S(2)}) collective-permute-start(bf16[400,2048]{1,0:T(8,128)(2,1)} %get-tuple-element.31.refs_3_), channel_id=1, source_target_pairs={{0,1},{1,2},{2,3},{4,5},{5,6},{6,7},{8,9},{9,10},{10,11},{12,13},{... | collective-permute-start | bytes 4915208 | tf_op jit(solution)/shard_map/ppermute | solution.py:179
  73.1 4.7 %near_plan.1.refs_2_.refs_0_ = bf16[800,2048]{1,0:T(8,128)(2,1)} custom-call(s32[3]{0:T(128)} %pad_add_fusion.1.ids_ref, bf16[400,2048]{1,0:T(8,128)(2,1)} %gate.19.refs_0_, bf16[400,2048]{1,0:T(8,128)(2,1)} %collective-permute-done.6.up_ref.refs_1_, bf16[400,2048]{1,0:T(8,128)(2,1)} %collective-permute-done.7.down_ref.refs_2_, ...), custom_call_target="tpu_custom_call" | custom-call | bytes 1024 | tf_op jit(solution)/shard_map/near_plan/pallas_call | solution.py:218
  77.8 26.9 %collective-permute-done.8.refs_3_.refs_2_.up_ref.refs_1_ = bf16[400,2048]{1,0:T(8,128)(2,1)} collective-permute-done((bf16[400,2048]{1,0:T(8,128)(2,1)}, bf16[400,2048]{1,0:T(8,128)(2,1)}, u32[]{:S(2)}, u32[]{:S(2)}) %collective-permute-start.8) | collective-permute-done | bytes 1638432 | tf_op jit(solution)/shard_map/ppermute | solution.py:179
  104.7 5.3 %collective-permute-done.9.refs_4_.refs_3_.down_ref.refs_0_ = bf16[400,2048]{1,0:T(8,128)(2,1)} collective-permute-done((bf16[400,2048]{1,0:T(8,128)(2,1)}, bf16[400,2048]{1,0:T(8,128)(2,1)}, u32[]{:S(2)}, u32[]{:S(2)}) %collective-permute-start.9) | collective-permute-done | bytes 1638432 | tf_op jit(solution)/shard_map/ppermute | solution.py:183
  112.5 4.3 %hops.4 = (bf16[400,2048]{1,0:T(8,128)(2,1)}, bf16[400,2048]{1,0:T(8,128)(2,1)}) custom-call(s32[3]{0:T(128)} %pad_add_fusion.1.ids_ref, bf16[1,384,8192]{2,1,0:T(8,128)(2,1)} %pending_ref.5, bf16[400,2048]{1,0:T(8,128)(2,1)} %collective-permute-done.8.refs_3_.refs_2_.up_ref.refs_1_, ...), custom_call_target="tpu_custom_call" | custom-call | bytes 1024 | tf_op jit(solution)/shard_map/hops/pallas_call | solution.py:295
  133.4 11.9 %project.2.refs_4_.refs_14_ = f32[768,768]{1,0:T(8,128)} custom-call(s32[11]{0:T(128)} %concatenate.54.ids_ref, bf16[800,2048]{1,0:T(8,128)(2,1)} %gate.22.refs_0_, bf16[800,2048]{1,0:T(8,128)(2,1)} %collective-permute-done.12.refs_1_, bf16[400,2048]{1,0:T(8,128)(2,1)} %pick_plan.5.refs_2_, bf16[400,2048]{1,0:T(8,128)(2,1)} %collective-permute-done.13.refs_3_, ...), custom_call_target="tpu_custom_call" | custom-call | bytes 1024 | tf_op jit(solution)/shard_map/project/pallas_call | solution.py:395
  145.3 16.3 %collective-permute-done.14.refs_0_.down_ref = bf16[400,2048]{1,0:T(8,128)(2,1)} collective-permute-done((bf16[400,2048]{1,0:T(8,128)(2,1)}, bf16[400,2048]{1,0:T(8,128)(2,1)}, u32[]{:S(2)}, u32[]{:S(2)}) %collective-permute-start.14) | collective-permute-done | bytes 1638432 | tf_op jit(solution)/shard_map/ppermute | solution.py:183
  176.4 5.0 %hops.5 = (bf16[384,2048]{1,0:T(8,128)(2,1)}, bf16[384,2048]{1,0:T(8,128)(2,1)}) custom-call(s32[3]{0:T(128)} %pad_add_fusion.1.ids_ref, bf16[1,384,8192]{2,1,0:T(8,128)(2,1)} %pending_ref.5, bf16[400,2048]{1,0:T(8,128)(2,1)} %collective-permute-done.15.refs_3_.up_ref, bf16[400,2048]{1,0:T(8,128)(2,1)} %collective-permute-done.14.refs_0_.down_ref, ...), custom_call_target="tpu_custom_call" | custom-call | bytes 1024 | tf_op jit(solution)/shard_map/hops/pallas_call | solution.py:295
  181.5 4.5 %collective-permute-start.21 = (bf16[384,2048]{1,0:T(8,128)(2,1)}, bf16[384,2048]{1,0:T(8,128)(2,1)}, u32[]{:S(2)}, u32[]{:S(2)}) collective-permute-start(bf16[384,2048]{1,0:T(8,128)(2,1)} %get-tuple-element.42), channel_id=1, source_target_pairs={{0,1},{1,2},{2,3},{4,5},{5,6},{6,7},{8,9},{9,10},{10,11},{12,13},{... | collective-permute-start | bytes 4718600 | tf_op jit(solution)/shard_map/ppermute | solution.py:179
  192.3 13.2 %project.3 = (bf16[4,768,128]{2,1,0:T(8,128)(2,1)}, bf16[2,768,128]{2,1,0:T(8,128)(2,1)}, bf16[2,384,128]{2,1,0:T(8,128)(2,1)}) custom-call(s32[11]{0:T(128)} %concatenate.54.ids_ref, bf16[800,2048]{1,0:T(8,128)(2,1)} %gate.22.refs_0_, bf16[800,2048]{1,0:T(8,128)(2,1)} %collective-permute-done.12.refs_1_, bf16[400,2048]{1,0:T(8,128)(2,1)} %pick_plan.5.refs_2_, ...), custom_call_target="tpu_custom_call" | custom-call | bytes 1024 | tf_op jit(solution)/shard_map/project/pallas_call | solution.py:395
  221.4 17.9 %attend.1.refs_0_.refs_4_ = bf16[768,512]{1,0:T(8,128)(2,1)} custom-call(s32[2,3]{1,0:T(2,128)} %pad_add_fusion.bound_ref, s32[3]{0:T(128)} %pad_add_fusion.1.ids_ref, bf16[4,768,128]{2,1,0:T(8,128)(2,1)} %get-tuple-element.35.refs_4_.q_ref, s32[768,128]{1,0:T(8,128)} %broadcast_in_dim.16.n_ref, s32[768,128]{1,0:T(8,128)} %broadcast_in_dim.17.lo_ref, ...), custom_call_target="tpu_custom_call" | custom-call | bytes 1024 | tf_op jit(solution)/shard_map/attend/pallas_call | solution.py:518
  239.3 7.1 %collective-permute-done.23.refs_3_.refs_1_ = bf16[512,512]{1,0:T(8,128)(2,1)S(1)} collective-permute-done((bf16[512,512]{1,0:T(8,128)(2,1)}, bf16[512,512]{1,0:T(8,128)(2,1)S(1)}, u32[]{:S(2)}, u32[]{:S(2)}) %collective-permute-start.23) | collective-permute-done | bytes 524320 | tf_op jit(solution)/shard_map/ppermute | solution.py:799
  246.4 12.7 %collective-permute-done.24.refs_4_.refs_2_ = bf16[512,512]{1,0:T(8,128)(2,1)S(1)} collective-permute-done((bf16[512,512]{1,0:T(8,128)(2,1)}, bf16[512,512]{1,0:T(8,128)(2,1)S(1)}, u32[]{:S(2)}, u32[]{:S(2)}) %collective-permute-start.24) | collective-permute-done | bytes 524320 | tf_op jit(solution)/shard_map/ppermute | solution.py:799
  270.2 11.0 %collective-permute-start.28 = (bf16[768,512]{1,0:T(8,128)(2,1)}, bf16[768,512]{1,0:T(8,128)(2,1)S(1)}, u32[]{:S(2)}, u32[]{:S(2)}) collective-permute-start(bf16[768,512]{1,0:T(8,128)(2,1)} %gate.29.refs_0_), channel_id=1, source_target_pairs={{0,1},{1,2},{2,3},{4,5},{5,6},{6,7},{8,9},{9,10},{10,11},{12,13},{... | collective-permute-start | bytes 2359304 | tf_op jit(solution)/shard_map/ppermute | solution.py:179
  281.9 13.5 %collective-permute-done.27.refs_0_.refs_2_ = bf16[768,512]{1,0:T(8,128)(2,1)S(1)} collective-permute-done((bf16[768,512]{1,0:T(8,128)(2,1)}, bf16[768,512]{1,0:T(8,128)(2,1)S(1)}, u32[]{:S(2)}, u32[]{:S(2)}) %collective-permute-start.27) | collective-permute-done | bytes 786464 | tf_op jit(solution)/shard_map/ppermute | solution.py:183
  303.7 14.4 %collective-permute-done.32.refs_0_ = bf16[768,512]{1,0:T(8,128)(2,1)} collective-permute-done((bf16[768,512]{1,0:T(8,128)(2,1)}, bf16[768,512]{1,0:T(8,128)(2,1)}, u32[]{:S(2)}, u32[]{:S(2)}) %collective-permute-start.32) | collective-permute-done | bytes 786464 | tf_op jit(solution)/shard_map/ppermute | solution.py:183
  329.8 5.1 %collective-permute-done.38.refs_4_.refs_14_ = bf16[512,1024]{1,0:T(8,128)(2,1)} collective-permute-done((bf16[512,1024]{1,0:T(8,128)(2,1)S(1)}, bf16[512,1024]{1,0:T(8,128)(2,1)}, u32[]{:S(2)}, u32[]{:S(2)}) %collective-permute-start.38) | collective-permute-done | bytes 1048608 | tf_op jit(solution)/shard_map/ppermute | solution.py:175
  335.0 13.1 %collective-permute-done.39.refs_5_.refs_15_ = bf16[512,1024]{1,0:T(8,128)(2,1)} collective-permute-done((bf16[512,1024]{1,0:T(8,128)(2,1)S(1)}, bf16[512,1024]{1,0:T(8,128)(2,1)}, u32[]{:S(2)}, u32[]{:S(2)}) %collective-permute-start.39) | collective-permute-done | bytes 1048608 | tf_op jit(solution)/shard_map/ppermute | solution.py:175
  353.9 13.2 %out_project.1 = (bf16[384,1024]{1,0:T(8,128)(2,1)}, bf16[384,1024]{1,0:T(8,128)(2,1)}) custom-call(s32[11]{0:T(128)} %concatenate.54.ids_ref, bf16[768,512]{1,0:T(8,128)(2,1)} %gate.29.refs_0_, bf16[768,512]{1,0:T(8,128)(2,1)} %collective-permute-done.26.refs_1_, bf16[768,512]{1,0:T(8,128)(2,1)} %pick_plan.7.refs_2_, ...), custom_call_target="tpu_custom_call" | custom-call | bytes 1024 | tf_op jit(solution)/shard_map/out_project/pallas_call | solution.py:590
  369.7 4.2 %fusion.2 = bf16[384,2048]{1,0:T(8,128)(2,1)} fusion(bf16[384,2048]{1,0:T(8,128)(2,1)S(1)} %copy-done.13, bf16[384,1024]{1,0:T(8,128)(2,1)S(1)} %collective-permute-done.42, bf16[384,1024]{1,0:T(8,128)(2,1)} %get-tuple-element.49, bf16[384,2048]{1,0:T(8,128)(2,1)} %collective-permute-done.22.refs_2_, bf16[384,2048]{1,0:T(8,128)(2,1)} %collective-permute-done.21.refs_1_, ...), kind=kLoop, calls=%fused_computation.5 | loop fusion | flops 16515072 | bytes 9437191 | tf_op jit(solution)/shard_map/convert_element_type | solution.py:850
  (197 shorter events, 120.8 us)
Async XLA Ops:
  9.3 46.4 %collective-permute-start.1 = (bf16[1936,512]{1,0:T(8,128)(2,1)}, bf16[1936,512]{1,0:T(8,128)(2,1)S(1)}, u32[]{:S(2)}, u32[]{:S(2)}) collective-permute-start(bf16[1936,512]{1,0:T(8,128)(2,1)} %get-tuple-element.28.refs_1_.refs_4_.refs_6_.refs_0_), channel_id=1, source_target_pairs={{0,8},{4,12},{8,0},{12,4},{16,24},{20,28},{24,16},{28,20},{1,9},{5... | collective-permute-start | bytes 5947400 | tf_op jit(solution)/shard_map/ppermute | solution.py:175
  12.3 44.9 %collective-permute-start.2 = (bf16[1936,512]{1,0:T(8,128)(2,1)}, bf16[1936,512]{1,0:T(8,128)(2,1)}, u32[]{:S(2)}, u32[]{:S(2)}) collective-permute-start(bf16[1936,512]{1,0:T(8,128)(2,1)} %get-tuple-element.28.refs_1_.refs_4_.refs_6_.refs_0_), channel_id=1, source_target_pairs={{0,16},{4,20},{8,24},{12,28},{16,0},{20,4},{24,8},{28,12},{1,17},{... | collective-permute-start | bytes 5947400 | tf_op jit(solution)/shard_map/ppermute | solution.py:175
  13.8 41.9 %collective-permute-start = (bf16[1936,512]{1,0:T(8,128)(2,1)}, bf16[1936,512]{1,0:T(8,128)(2,1)}, u32[]{:S(2)}, u32[]{:S(2)}) collective-permute-start(bf16[1936,512]{1,0:T(8,128)(2,1)} %get-tuple-element.29), channel_id=1, source_target_pairs={{0,4},{4,0},{8,12},{12,8},{16,20},{20,16},{24,28},{28,24},{1,5},{5... | collective-permute-start | bytes 5947400 | tf_op jit(solution)/shard_map/ppermute | solution.py:175
  18.2 44.6 %collective-permute-start.6 = (bf16[400,2048]{1,0:T(8,128)(2,1)}, bf16[400,2048]{1,0:T(8,128)(2,1)}, u32[]{:S(2)}, u32[]{:S(2)}) collective-permute-start(bf16[400,2048]{1,0:T(8,128)(2,1)} %gate.19.refs_0_), channel_id=1, source_target_pairs={{0,1},{1,2},{2,3},{4,5},{5,6},{6,7},{8,9},{9,10},{10,11},{12,13},{... | collective-permute-start | bytes 4915208 | tf_op jit(solution)/shard_map/ppermute | solution.py:179
  22.9 40.0 %collective-permute-start.7 = (bf16[400,2048]{1,0:T(8,128)(2,1)}, bf16[400,2048]{1,0:T(8,128)(2,1)}, u32[]{:S(2)}, u32[]{:S(2)}) collective-permute-start(bf16[400,2048]{1,0:T(8,128)(2,1)} %gate.19.refs_0_), channel_id=1, source_target_pairs={{3,2},{2,1},{1,0},{7,6},{6,5},{5,4},{11,10},{10,9},{9,8},{15,14},{... | collective-permute-start | bytes 4915208 | tf_op jit(solution)/shard_map/ppermute | solution.py:183
  57.3 52.7 %collective-permute-start.3 = (bf16[1936,512]{1,0:T(8,128)(2,1)}, bf16[1936,512]{1,0:T(8,128)(2,1)S(1)}, u32[]{:S(2)}, u32[]{:S(2)}) collective-permute-start(bf16[1936,512]{1,0:T(8,128)(2,1)} %gate.17.refs_2_.refs_5_.refs_7_.refs_1_), channel_id=1, source_target_pairs={{0,8},{4,12},{8,0},{12,4},{16,24},{20,28},{24,16},{28,20},{1,9},{5... | collective-permute-start | bytes 5947400 | tf_op jit(solution)/shard_map/ppermute | solution.py:175
  58.7 51.3 %collective-permute-start.4 = (bf16[1936,512]{1,0:T(8,128)(2,1)}, bf16[1936,512]{1,0:T(8,128)(2,1)S(1)}, u32[]{:S(2)}, u32[]{:S(2)}) collective-permute-start(bf16[1936,512]{1,0:T(8,128)(2,1)} %gate.17.refs_2_.refs_5_.refs_7_.refs_1_), channel_id=1, source_target_pairs={{0,16},{4,20},{8,24},{12,28},{16,0},{20,4},{24,8},{28,12},{1,17},{... | collective-permute-start | bytes 5947400 | tf_op jit(solution)/shard_map/ppermute | solution.py:175
  67.1 37.5 %collective-permute-start.8 = (bf16[400,2048]{1,0:T(8,128)(2,1)}, bf16[400,2048]{1,0:T(8,128)(2,1)}, u32[]{:S(2)}, u32[]{:S(2)}) collective-permute-start(bf16[400,2048]{1,0:T(8,128)(2,1)} %get-tuple-element.31.refs_3_), channel_id=1, source_target_pairs={{0,1},{1,2},{2,3},{4,5},{5,6},{6,7},{8,9},{9,10},{10,11},{12,13},{... | collective-permute-start | bytes 4915208 | tf_op jit(solution)/shard_map/ppermute | solution.py:179
  71.8 38.1 %collective-permute-start.9 = (bf16[400,2048]{1,0:T(8,128)(2,1)}, bf16[400,2048]{1,0:T(8,128)(2,1)}, u32[]{:S(2)}, u32[]{:S(2)}) collective-permute-start(bf16[400,2048]{1,0:T(8,128)(2,1)} %get-tuple-element.32), channel_id=1, source_target_pairs={{3,2},{2,1},{1,0},{7,6},{6,5},{5,4},{11,10},{10,9},{9,8},{15,14},{... | collective-permute-start | bytes 4915208 | tf_op jit(solution)/shard_map/ppermute | solution.py:183
  121.2 45.4 %collective-permute-start.10 = (bf16[1936,512]{1,0:T(8,128)(2,1)}, bf16[1936,512]{1,0:T(8,128)(2,1)S(1)}, u32[]{:S(2)}, u32[]{:S(2)}) collective-permute-start(bf16[1936,512]{1,0:T(8,128)(2,1)} %gate.20.refs_0_.refs_6_.refs_8_.refs_2_), channel_id=1, source_target_pairs={{0,16},{4,20},{8,24},{12,28},{16,0},{20,4},{24,8},{28,12},{1,17},{... | collective-permute-start | bytes 5947400 | tf_op jit(solution)/shard_map/ppermute | solution.py:175
  121.7 45.2 %collective-permute-start.11 = (bf16[1936,512]{1,0:T(8,128)(2,1)}, bf16[1936,512]{1,0:T(8,128)(2,1)}, u32[]{:S(2)}, u32[]{:S(2)}) collective-permute-start(bf16[1936,512]{1,0:T(8,128)(2,1)} %gate.21.refs_1_.refs_9_.refs_11_.refs_5_), channel_id=1, source_target_pairs={{0,8},{4,12},{8,0},{12,4},{16,24},{20,28},{24,16},{28,20},{1,9},{5... | collective-permute-start | bytes 5947400 | tf_op jit(solution)/shard_map/ppermute | solution.py:175
  122.2 39.4 %collective-permute-start.14 = (bf16[400,2048]{1,0:T(8,128)(2,1)}, bf16[400,2048]{1,0:T(8,128)(2,1)}, u32[]{:S(2)}, u32[]{:S(2)}) collective-permute-start(bf16[400,2048]{1,0:T(8,128)(2,1)} %get-tuple-element.34), channel_id=1, source_target_pairs={{3,2},{2,1},{1,0},{7,6},{6,5},{5,4},{11,10},{10,9},{9,8},{15,14},{... | collective-permute-start | bytes 4915208 | tf_op jit(solution)/shard_map/ppermute | solution.py:183
  125.4 38.5 %collective-permute-start.15 = (bf16[400,2048]{1,0:T(8,128)(2,1)}, bf16[400,2048]{1,0:T(8,128)(2,1)}, u32[]{:S(2)}, u32[]{:S(2)}) collective-permute-start(bf16[400,2048]{1,0:T(8,128)(2,1)} %get-tuple-element.33.refs_1_.refs_2_), channel_id=1, source_target_pairs={{0,1},{1,2},{2,3},{4,5},{5,6},{6,7},{8,9},{9,10},{10,11},{12,13},{... | collective-permute-start | bytes 4915208 | tf_op jit(solution)/shard_map/ppermute | solution.py:179
  174.4 31.1 %collective-permute-start.18 = (bf16[512,512]{1,0:T(8,128)(2,1)}, bf16[512,512]{1,0:T(8,128)(2,1)S(1)}, u32[]{:S(2)}, u32[]{:S(2)}) collective-permute-start(bf16[512,512]{1,0:T(8,128)(2,1)} %gate.23), channel_id=1, source_target_pairs={{0,8},{4,12},{8,0},{12,4},{16,24},{20,28},{24,16},{28,20},{1,9},{5... | collective-permute-start | bytes 1572872 | tf_op jit(solution)/shard_map/ppermute | solution.py:175
  175.0 33.0 %collective-permute-start.19 = (bf16[512,512]{1,0:T(8,128)(2,1)}, bf16[512,512]{1,0:T(8,128)(2,1)S(1)}, u32[]{:S(2)}, u32[]{:S(2)}) collective-permute-start(bf16[512,512]{1,0:T(8,128)(2,1)} %gate.24), channel_id=1, source_target_pairs={{0,16},{4,20},{8,24},{12,28},{16,0},{20,4},{24,8},{28,12},{1,17},{... | collective-permute-start | bytes 1572872 | tf_op jit(solution)/shard_map/ppermute | solution.py:175
  181.5 87.4 %collective-permute-start.21 = (bf16[384,2048]{1,0:T(8,128)(2,1)}, bf16[384,2048]{1,0:T(8,128)(2,1)}, u32[]{:S(2)}, u32[]{:S(2)}) collective-permute-start(bf16[384,2048]{1,0:T(8,128)(2,1)} %get-tuple-element.42), channel_id=1, source_target_pairs={{0,1},{1,2},{2,3},{4,5},{5,6},{6,7},{8,9},{9,10},{10,11},{12,13},{... | collective-permute-start | bytes 4718600 | tf_op jit(solution)/shard_map/ppermute | solution.py:179
  185.9 83.0 %collective-permute-start.22 = (bf16[384,2048]{1,0:T(8,128)(2,1)}, bf16[384,2048]{1,0:T(8,128)(2,1)}, u32[]{:S(2)}, u32[]{:S(2)}) collective-permute-start(bf16[384,2048]{1,0:T(8,128)(2,1)} %get-tuple-element.43), channel_id=1, source_target_pairs={{3,2},{2,1},{1,0},{7,6},{6,5},{5,4},{11,10},{10,9},{9,8},{15,14},{... | collective-permute-start | bytes 4718600 | tf_op jit(solution)/shard_map/ppermute | solution.py:183
  213.7 32.7 %collective-permute-start.23 = (bf16[512,512]{1,0:T(8,128)(2,1)}, bf16[512,512]{1,0:T(8,128)(2,1)S(1)}, u32[]{:S(2)}, u32[]{:S(2)}) collective-permute-start(bf16[512,512]{1,0:T(8,128)(2,1)} %gate.26), channel_id=1, source_target_pairs={{0,1},{1,0},{2,3},{3,2},{4,5},{5,4},{6,7},{7,6},{8,9},{9,8},{10,11... | collective-permute-start | bytes 1572872 | tf_op jit(solution)/shard_map/ppermute | solution.py:799
  216.3 42.8 %collective-permute-start.24 = (bf16[512,512]{1,0:T(8,128)(2,1)}, bf16[512,512]{1,0:T(8,128)(2,1)S(1)}, u32[]{:S(2)}, u32[]{:S(2)}) collective-permute-start(bf16[512,512]{1,0:T(8,128)(2,1)} %gate.27), channel_id=1, source_target_pairs={{0,2},{1,3},{2,0},{3,1},{4,6},{5,7},{6,4},{7,5},{8,10},{9,11},{10,... | collective-permute-start | bytes 1572872 | tf_op jit(solution)/shard_map/ppermute | solution.py:799
  217.6 41.5 %collective-permute-start.25 = (bf16[512,512]{1,0:T(8,128)(2,1)}, bf16[512,512]{1,0:T(8,128)(2,1)S(1)}, u32[]{:S(2)}, u32[]{:S(2)}) collective-permute-start(bf16[512,512]{1,0:T(8,128)(2,1)} %gate.28), channel_id=1, source_target_pairs={{0,3},{1,2},{2,1},{3,0},{4,7},{5,6},{6,5},{7,4},{8,11},{9,10},{10,... | collective-permute-start | bytes 1572872 | tf_op jit(solution)/shard_map/ppermute | solution.py:799
  264.7 31.6 %collective-permute-start.30 = (bf16[512,1024]{1,0:T(8,128)(2,1)}, bf16[512,1024]{1,0:T(8,128)(2,1)S(1)}, u32[]{:S(2)}, u32[]{:S(2)}) collective-permute-start(bf16[512,1024]{1,0:T(8,128)(2,1)} %get-tuple-element.47.refs_8_), channel_id=1, source_target_pairs={{0,8},{4,12},{8,0},{12,4},{16,24},{20,28},{24,16},{28,20},{1,9},{5... | collective-permute-start | bytes 3145736 | tf_op jit(solution)/shard_map/ppermute | solution.py:175
  266.2 30.3 %collective-permute-start.31 = (bf16[512,1024]{1,0:T(8,128)(2,1)}, bf16[512,1024]{1,0:T(8,128)(2,1)S(1)}, u32[]{:S(2)}, u32[]{:S(2)}) collective-permute-start(bf16[512,1024]{1,0:T(8,128)(2,1)} %get-tuple-element.48.refs_9_), channel_id=1, source_target_pairs={{0,16},{4,20},{8,24},{12,28},{16,0},{20,4},{24,8},{28,12},{1,17},{... | collective-permute-start | bytes 3145736 | tf_op jit(solution)/shard_map/ppermute | solution.py:175
  281.2 41.5 %collective-permute-start.35 = (bf16[512,1024]{1,0:T(8,128)(2,1)}, bf16[512,1024]{1,0:T(8,128)(2,1)S(1)}, u32[]{:S(2)}, u32[]{:S(2)}) collective-permute-start(bf16[512,1024]{1,0:T(8,128)(2,1)} %get-tuple-element.47.refs_8_), channel_id=1, source_target_pairs={{0,16},{4,20},{8,24},{12,28},{16,0},{20,4},{24,8},{28,12},{1,17},{... | collective-permute-start | bytes 3145736 | tf_op jit(solution)/shard_map/ppermute | solution.py:175
  303.2 31.8 %collective-permute-start.38 = (bf16[512,1024]{1,0:T(8,128)(2,1)S(1)}, bf16[512,1024]{1,0:T(8,128)(2,1)}, u32[]{:S(2)}, u32[]{:S(2)}) collective-permute-start(bf16[512,1024]{1,0:T(8,128)(2,1)S(1)} %copy-done.6), channel_id=1, source_target_pairs={{0,16},{4,20},{8,24},{12,28},{16,0},{20,4},{24,8},{28,12},{1,17},{... | collective-permute-start | bytes 3145736 | tf_op jit(solution)/shard_map/ppermute | solution.py:175
  (43 other events, 436.6 us)

commit v6 on v5

--- a/solution.py
+++ b/solution.py
@@ -422,7 +422,7 @@
 
 def absorb(s, v_ext, m, acc):
     new = jnp.maximum(m, jnp.max(s, axis=1, keepdims=True))
-    p = jnp.exp2(s - new).astype(jnp.bfloat16)
+    p = jnp.exp2((s - new).astype(jnp.bfloat16))
     acc = acc * jnp.exp2(m - new) + jnp.dot(p, v_ext, preferred_element_type=jnp.float32)
     return new, acc
 
@@ -830,8 +830,8 @@
     wo_parts = (wo_a, wo_b, wo_xa, wo_xb, wo_ya, wo_yb, swap(wo_xa, 4), swap(wo_yb, 2))
     u2, d2 = hop_up(gate(u1, wo_xa, wo_yb), (1, 2)), hop_down(gate(d1, wo_xa, wo_yb), (1, 2))
     second = pick(z, (d2, d2, u2, u2), here)
-    u3, d3 = hop_up(gate(u2, wo_ya), (2,)), hop_down(gate(d2, wo_ya), (2,))
-    third = pick(z, (d3, u1, d1, u3), here, wo_parts[6:] + (wo_xb,))
+    u3, d3 = hop_up(gate(u2, wo_xb, wo_ya), (2,)), hop_down(gate(d2, wo_xb, wo_ya), (2,))
+    third = pick(z, (d3, u1, d1, u3), here, wo_parts[6:])
     hs = []
     for part in (attended, near, second, third):
         hs += [part, swap(part, 1)]

time: 380 us -> 370 us (0.974)
  waiting for transfers between devices: 156 us -> 147 us
    ppermute x25, waiting for transfers between devices: 57.3 us -> 50.5 us  [swap(): return lax.ppermute(x, 'ctx', [(c, c ^ bit) for c in range(N_CTX)])]
  transfers between devices with their start and end apart: 43 -> 43, of which waited for: 18 -> 17; matrix products, arithmetic and copies ran while one was open for 5% -> 5% of each run, Pallas kernels for 22% -> 23%
where the time goes in v6:
time: 370 us; the launch traced here: 367 us
  waiting for transfers between devices  147 us (40%)
  Pallas kernels  109 us (29%)
  starting transfers between devices  71.5 us (19%)
  other arithmetic  19.7 us (5%)
  local copies, waits for them, and re-layouts  16.7 us (5%)
    ppermute x25, waiting for transfers between devices, swap(): return lax.ppermute(x, 'ctx', [(c, c ^ bit) for c in range(N_CTX)])  50.5 us
    ppermute x7, waiting for transfers between devices, hop_down(): return lax.ppermute(v, 'tp', [(N_TP - 1 - i, N_TP - 2 - i) for i in pairs])  48.8 us
    pallas_call x10, Pallas kernels, move(): pl.pallas_call(kernel, out_shape=tuple((jax.ShapeDtypeStruct(shape, jnp.b...  37.8 us
    ppermute x7, starting transfers between devices, hop_up(): return lax.ppermute(v, 'tp', [(i, i + 1) for i in pairs])  33.4 us
    ppermute x7, waiting for transfers between devices, hop_up(): return lax.ppermute(v, 'tp', [(i, i + 1) for i in pairs])  29.2 us
    pallas_call x2, Pallas kernels, project(): pl.pallas_call(functools.partial(project_kernel, slots, len(xs), len(weig...  25.2 us
    ppermute x25, starting transfers between devices, swap(): return lax.ppermute(x, 'ctx', [(c, c ^ bit) for c in range(N_CTX)])  21.4 us
    pallas_call x1, Pallas kernels, attend(): pl.pallas_call(functools.partial(attend_kernel, at_old), out_shape=jax.Sh...  19.4 us
  transfers between devices with their start and end apart: 43, of which 17 were waited for; matrix products, arithmetic and copies ran while one was open for 5% of the time, Pallas kernels for 23%

profile of v6, /device:TPU:0, one launch (start us, length us, event | category | flops | bytes accessed | tf_op | source)
XLA Modules:
  0.0 367.0 jit_solution(16962606272129877393)
XLA Ops:
  4.3 5.0 %first_plan.1 = (bf16[1936,512]{1,0:T(8,128)(2,1)}, bf16[1936,512]{1,0:T(8,128)(2,1)}) custom-call(s32[3]{0:T(128)} %pad_add_fusion.1.ids_ref, bf16[1024,1024]{1,0:T(8,128)(2,1)} %refs_0_.2, bf16[1024,1024]{1,0:T(8,128)(2,1)} %refs_1_.1, bf16[1024,1024]{1,0:T(8,128)(2,1)} %refs_2_.1, bf16[8,768,128]{2,1,0:T(8,128)(2,1)} %refs_3_.1, ...), custom_call_target="tpu_custom_call" | custom-call | bytes 1024 | tf_op jit(solution)/shard_map/first_plan/pallas_call | solution.py:218
  18.2 4.7 %collective-permute-start.6 = (bf16[400,2048]{1,0:T(8,128)(2,1)}, bf16[400,2048]{1,0:T(8,128)(2,1)}, u32[]{:S(2)}, u32[]{:S(2)}) collective-permute-start(bf16[400,2048]{1,0:T(8,128)(2,1)} %gate.19.refs_0_), channel_id=1, source_target_pairs={{0,1},{1,2},{2,3},{4,5},{5,6},{6,7},{8,9},{9,10},{10,11},{12,13},{... | collective-permute-start | bytes 4915208 | tf_op jit(solution)/shard_map/ppermute | solution.py:179
  28.7 27.0 %collective-permute-done.1.refs_1_.refs_0_ = bf16[1936,512]{1,0:T(8,128)(2,1)S(1)} collective-permute-done((bf16[1936,512]{1,0:T(8,128)(2,1)}, bf16[1936,512]{1,0:T(8,128)(2,1)S(1)}, u32[]{:S(2)}, u32[]{:S(2)}) %collective-permute-start.1) | collective-permute-done | bytes 1982496 | tf_op jit(solution)/shard_map/ppermute | solution.py:175
  62.8 4.3 %hops.3 = (bf16[400,2048]{1,0:T(8,128)(2,1)}, bf16[400,2048]{1,0:T(8,128)(2,1)}) custom-call(s32[3]{0:T(128)} %pad_add_fusion.1.ids_ref, bf16[1,384,8192]{2,1,0:T(8,128)(2,1)} %pending_ref.5, bf16[400,2048]{1,0:T(8,128)(2,1)} %collective-permute-done.6.up_ref.refs_1_, bf16[400,2048]{1,0:T(8,128)(2,1)} %collective-permute-done.7.down_ref.refs_2_, ...), custom_call_target="tpu_custom_call" | custom-call | bytes 1024 | tf_op jit(solution)/shard_map/hops/pallas_call | solution.py:295
  67.1 4.7 %collective-permute-start.8 = (bf16[400,2048]{1,0:T(8,128)(2,1)}, bf16[400,2048]{1,0:T(8,128)(2,1)}, u32[]{:S(2)}, u32[]{:S(2)}) collective-permute-start(bf16[400,2048]{1,0:T(8,128)(2,1)} %get-tuple-element.31.refs_3_), channel_id=1, source_target_pairs={{0,1},{1,2},{2,3},{4,5},{5,6},{6,7},{8,9},{9,10},{10,11},{12,13},{... | collective-permute-start | bytes 4915208 | tf_op jit(solution)/shard_map/ppermute | solution.py:179
  73.1 4.7 %near_plan.1.refs_2_.refs_0_ = bf16[800,2048]{1,0:T(8,128)(2,1)} custom-call(s32[3]{0:T(128)} %pad_add_fusion.1.ids_ref, bf16[400,2048]{1,0:T(8,128)(2,1)} %gate.19.refs_0_, bf16[400,2048]{1,0:T(8,128)(2,1)} %collective-permute-done.6.up_ref.refs_1_, bf16[400,2048]{1,0:T(8,128)(2,1)} %collective-permute-done.7.down_ref.refs_2_, ...), custom_call_target="tpu_custom_call" | custom-call | bytes 1024 | tf_op jit(solution)/shard_map/near_plan/pallas_call | solution.py:218
  77.8 26.9 %collective-permute-done.8.refs_3_.refs_2_.up_ref.refs_1_ = bf16[400,2048]{1,0:T(8,128)(2,1)} collective-permute-done((bf16[400,2048]{1,0:T(8,128)(2,1)}, bf16[400,2048]{1,0:T(8,128)(2,1)}, u32[]{:S(2)}, u32[]{:S(2)}) %collective-permute-start.8) | collective-permute-done | bytes 1638432 | tf_op jit(solution)/shard_map/ppermute | solution.py:179
  104.7 5.3 %collective-permute-done.9.refs_4_.refs_3_.down_ref.refs_0_ = bf16[400,2048]{1,0:T(8,128)(2,1)} collective-permute-done((bf16[400,2048]{1,0:T(8,128)(2,1)}, bf16[400,2048]{1,0:T(8,128)(2,1)}, u32[]{:S(2)}, u32[]{:S(2)}) %collective-permute-start.9) | collective-permute-done | bytes 1638432 | tf_op jit(solution)/shard_map/ppermute | solution.py:183
  112.5 4.3 %hops.4 = (bf16[400,2048]{1,0:T(8,128)(2,1)}, bf16[400,2048]{1,0:T(8,128)(2,1)}) custom-call(s32[3]{0:T(128)} %pad_add_fusion.1.ids_ref, bf16[1,384,8192]{2,1,0:T(8,128)(2,1)} %pending_ref.5, bf16[400,2048]{1,0:T(8,128)(2,1)} %collective-permute-done.8.refs_3_.refs_2_.up_ref.refs_1_, ...), custom_call_target="tpu_custom_call" | custom-call | bytes 1024 | tf_op jit(solution)/shard_map/hops/pallas_call | solution.py:295
  125.4 4.0 %collective-permute-start.15 = (bf16[400,2048]{1,0:T(8,128)(2,1)}, bf16[400,2048]{1,0:T(8,128)(2,1)}, u32[]{:S(2)}, u32[]{:S(2)}) collective-permute-start(bf16[400,2048]{1,0:T(8,128)(2,1)} %get-tuple-element.33.refs_1_.refs_2_), channel_id=1, source_target_pairs={{0,1},{1,2},{2,3},{4,5},{5,6},{6,7},{8,9},{9,10},{10,11},{12,13},{... | collective-permute-start | bytes 4915208 | tf_op jit(solution)/shard_map/ppermute | solution.py:179
  133.4 11.9 %project.2.refs_4_.refs_14_ = f32[768,768]{1,0:T(8,128)} custom-call(s32[11]{0:T(128)} %concatenate.54.ids_ref, bf16[800,2048]{1,0:T(8,128)(2,1)} %gate.22.refs_0_, bf16[800,2048]{1,0:T(8,128)(2,1)} %collective-permute-done.12.refs_1_, bf16[400,2048]{1,0:T(8,128)(2,1)} %pick_plan.5.refs_2_, bf16[400,2048]{1,0:T(8,128)(2,1)} %collective-permute-done.13.refs_3_, ...), custom_call_target="tpu_custom_call" | custom-call | bytes 1024 | tf_op jit(solution)/shard_map/project/pallas_call | solution.py:395
  145.3 16.3 %collective-permute-done.14.refs_0_.down_ref = bf16[400,2048]{1,0:T(8,128)(2,1)} collective-permute-done((bf16[400,2048]{1,0:T(8,128)(2,1)}, bf16[400,2048]{1,0:T(8,128)(2,1)}, u32[]{:S(2)}, u32[]{:S(2)}) %collective-permute-start.14) | collective-permute-done | bytes 1638432 | tf_op jit(solution)/shard_map/ppermute | solution.py:183
  176.4 5.0 %hops.5 = (bf16[384,2048]{1,0:T(8,128)(2,1)}, bf16[384,2048]{1,0:T(8,128)(2,1)}) custom-call(s32[3]{0:T(128)} %pad_add_fusion.1.ids_ref, bf16[1,384,8192]{2,1,0:T(8,128)(2,1)} %pending_ref.5, bf16[400,2048]{1,0:T(8,128)(2,1)} %collective-permute-done.15.refs_3_.up_ref, bf16[400,2048]{1,0:T(8,128)(2,1)} %collective-permute-done.14.refs_0_.down_ref, ...), custom_call_target="tpu_custom_call" | custom-call | bytes 1024 | tf_op jit(solution)/shard_map/hops/pallas_call | solution.py:295
  181.5 4.5 %collective-permute-start.21 = (bf16[384,2048]{1,0:T(8,128)(2,1)}, bf16[384,2048]{1,0:T(8,128)(2,1)}, u32[]{:S(2)}, u32[]{:S(2)}) collective-permute-start(bf16[384,2048]{1,0:T(8,128)(2,1)} %get-tuple-element.42), channel_id=1, source_target_pairs={{0,1},{1,2},{2,3},{4,5},{5,6},{6,7},{8,9},{9,10},{10,11},{12,13},{... | collective-permute-start | bytes 4718600 | tf_op jit(solution)/shard_map/ppermute | solution.py:179
  192.3 13.2 %project.3 = (bf16[4,768,128]{2,1,0:T(8,128)(2,1)}, bf16[2,768,128]{2,1,0:T(8,128)(2,1)}, bf16[2,384,128]{2,1,0:T(8,128)(2,1)}) custom-call(s32[11]{0:T(128)} %concatenate.54.ids_ref, bf16[800,2048]{1,0:T(8,128)(2,1)} %gate.22.refs_0_, bf16[800,2048]{1,0:T(8,128)(2,1)} %collective-permute-done.12.refs_1_, bf16[400,2048]{1,0:T(8,128)(2,1)} %pick_plan.5.refs_2_, ...), custom_call_target="tpu_custom_call" | custom-call | bytes 1024 | tf_op jit(solution)/shard_map/project/pallas_call | solution.py:395
  221.4 19.4 %attend.1.refs_0_.refs_4_ = bf16[768,512]{1,0:T(8,128)(2,1)} custom-call(s32[2,3]{1,0:T(2,128)} %pad_add_fusion.bound_ref, s32[3]{0:T(128)} %pad_add_fusion.1.ids_ref, bf16[4,768,128]{2,1,0:T(8,128)(2,1)} %get-tuple-element.35.refs_4_.q_ref, s32[768,128]{1,0:T(8,128)} %broadcast_in_dim.16.n_ref, s32[768,128]{1,0:T(8,128)} %broadcast_in_dim.17.lo_ref, ...), custom_call_target="tpu_custom_call" | custom-call | bytes 1024 | tf_op jit(solution)/shard_map/attend/pallas_call | solution.py:518
  240.7 5.6 %collective-permute-done.23.refs_3_.refs_1_ = bf16[512,512]{1,0:T(8,128)(2,1)S(1)} collective-permute-done((bf16[512,512]{1,0:T(8,128)(2,1)}, bf16[512,512]{1,0:T(8,128)(2,1)S(1)}, u32[]{:S(2)}, u32[]{:S(2)}) %collective-permute-start.23) | collective-permute-done | bytes 524320 | tf_op jit(solution)/shard_map/ppermute | solution.py:799
  246.4 12.7 %collective-permute-done.24.refs_4_.refs_2_ = bf16[512,512]{1,0:T(8,128)(2,1)S(1)} collective-permute-done((bf16[512,512]{1,0:T(8,128)(2,1)}, bf16[512,512]{1,0:T(8,128)(2,1)S(1)}, u32[]{:S(2)}, u32[]{:S(2)}) %collective-permute-start.24) | collective-permute-done | bytes 524320 | tf_op jit(solution)/shard_map/ppermute | solution.py:799
  269.0 12.2 %collective-permute-start.28 = (bf16[768,512]{1,0:T(8,128)(2,1)}, bf16[768,512]{1,0:T(8,128)(2,1)S(1)}, u32[]{:S(2)}, u32[]{:S(2)}) collective-permute-start(bf16[768,512]{1,0:T(8,128)(2,1)} %gate.29.refs_0_), channel_id=1, source_target_pairs={{0,1},{1,2},{2,3},{4,5},{5,6},{6,7},{8,9},{9,10},{10,11},{12,13},{... | collective-permute-start | bytes 2359304 | tf_op jit(solution)/shard_map/ppermute | solution.py:179
  281.8 13.5 %collective-permute-done.27.refs_0_.refs_2_ = bf16[768,512]{1,0:T(8,128)(2,1)S(1)} collective-permute-done((bf16[768,512]{1,0:T(8,128)(2,1)}, bf16[768,512]{1,0:T(8,128)(2,1)S(1)}, u32[]{:S(2)}, u32[]{:S(2)}) %collective-permute-start.27) | collective-permute-done | bytes 786464 | tf_op jit(solution)/shard_map/ppermute | solution.py:183
  304.4 13.7 %collective-permute-done.32.refs_0_ = bf16[768,512]{1,0:T(8,128)(2,1)} collective-permute-done((bf16[768,512]{1,0:T(8,128)(2,1)}, bf16[768,512]{1,0:T(8,128)(2,1)}, u32[]{:S(2)}, u32[]{:S(2)}) %collective-permute-start.32) | collective-permute-done | bytes 786464 | tf_op jit(solution)/shard_map/ppermute | solution.py:183
  329.9 10.9 %collective-permute-done.39.refs_4_.refs_14_ = bf16[512,1024]{1,0:T(8,128)(2,1)} collective-permute-done((bf16[512,1024]{1,0:T(8,128)(2,1)S(1)}, bf16[512,1024]{1,0:T(8,128)(2,1)}, u32[]{:S(2)}, u32[]{:S(2)}) %collective-permute-start.39) | collective-permute-done | bytes 1048608 | tf_op jit(solution)/shard_map/ppermute | solution.py:175
  347.1 13.2 %out_project.1 = (bf16[384,1024]{1,0:T(8,128)(2,1)}, bf16[384,1024]{1,0:T(8,128)(2,1)}) custom-call(s32[11]{0:T(128)} %concatenate.54.ids_ref, bf16[768,512]{1,0:T(8,128)(2,1)} %gate.29.refs_0_, bf16[768,512]{1,0:T(8,128)(2,1)} %collective-permute-done.26.refs_1_, bf16[768,512]{1,0:T(8,128)(2,1)} %pick_plan.7.refs_2_, ...), custom_call_target="tpu_custom_call" | custom-call | bytes 1024 | tf_op jit(solution)/shard_map/out_project/pallas_call | solution.py:590
  362.8 4.2 %fusion.2 = bf16[384,2048]{1,0:T(8,128)(2,1)} fusion(bf16[384,2048]{1,0:T(8,128)(2,1)S(1)} %copy-done.13, bf16[384,1024]{1,0:T(8,128)(2,1)S(1)} %collective-permute-done.42, bf16[384,1024]{1,0:T(8,128)(2,1)} %get-tuple-element.49, bf16[384,2048]{1,0:T(8,128)(2,1)} %collective-permute-done.22.refs_2_, bf16[384,2048]{1,0:T(8,128)(2,1)} %collective-permute-done.21.refs_1_, ...), kind=kLoop, calls=%fused_computation.5 | loop fusion | flops 16515072 | bytes 9437191 | tf_op jit(solution)/shard_map/convert_element_type | solution.py:850
  (197 shorter events, 116.8 us)
Async XLA Ops:
  9.3 46.4 %collective-permute-start.1 = (bf16[1936,512]{1,0:T(8,128)(2,1)}, bf16[1936,512]{1,0:T(8,128)(2,1)S(1)}, u32[]{:S(2)}, u32[]{:S(2)}) collective-permute-start(bf16[1936,512]{1,0:T(8,128)(2,1)} %get-tuple-element.28.refs_1_.refs_4_.refs_6_.refs_0_), channel_id=1, source_target_pairs={{0,8},{4,12},{8,0},{12,4},{16,24},{20,28},{24,16},{28,20},{1,9},{5... | collective-permute-start | bytes 5947400 | tf_op jit(solution)/shard_map/ppermute | solution.py:175
  12.3 44.9 %collective-permute-start.2 = (bf16[1936,512]{1,0:T(8,128)(2,1)}, bf16[1936,512]{1,0:T(8,128)(2,1)}, u32[]{:S(2)}, u32[]{:S(2)}) collective-permute-start(bf16[1936,512]{1,0:T(8,128)(2,1)} %get-tuple-element.28.refs_1_.refs_4_.refs_6_.refs_0_), channel_id=1, source_target_pairs={{0,16},{4,20},{8,24},{12,28},{16,0},{20,4},{24,8},{28,12},{1,17},{... | collective-permute-start | bytes 5947400 | tf_op jit(solution)/shard_map/ppermute | solution.py:175
  13.8 41.9 %collective-permute-start = (bf16[1936,512]{1,0:T(8,128)(2,1)}, bf16[1936,512]{1,0:T(8,128)(2,1)}, u32[]{:S(2)}, u32[]{:S(2)}) collective-permute-start(bf16[1936,512]{1,0:T(8,128)(2,1)} %get-tuple-element.29), channel_id=1, source_target_pairs={{0,4},{4,0},{8,12},{12,8},{16,20},{20,16},{24,28},{28,24},{1,5},{5... | collective-permute-start | bytes 5947400 | tf_op jit(solution)/shard_map/ppermute | solution.py:175
  18.2 44.6 %collective-permute-start.6 = (bf16[400,2048]{1,0:T(8,128)(2,1)}, bf16[400,2048]{1,0:T(8,128)(2,1)}, u32[]{:S(2)}, u32[]{:S(2)}) collective-permute-start(bf16[400,2048]{1,0:T(8,128)(2,1)} %gate.19.refs_0_), channel_id=1, source_target_pairs={{0,1},{1,2},{2,3},{4,5},{5,6},{6,7},{8,9},{9,10},{10,11},{12,13},{... | collective-permute-start | bytes 4915208 | tf_op jit(solution)/shard_map/ppermute | solution.py:179
  22.9 40.0 %collective-permute-start.7 = (bf16[400,2048]{1,0:T(8,128)(2,1)}, bf16[400,2048]{1,0:T(8,128)(2,1)}, u32[]{:S(2)}, u32[]{:S(2)}) collective-permute-start(bf16[400,2048]{1,0:T(8,128)(2,1)} %gate.19.refs_0_), channel_id=1, source_target_pairs={{3,2},{2,1},{1,0},{7,6},{6,5},{5,4},{11,10},{10,9},{9,8},{15,14},{... | collective-permute-start | bytes 4915208 | tf_op jit(solution)/shard_map/ppermute | solution.py:183
  57.3 52.7 %collective-permute-start.3 = (bf16[1936,512]{1,0:T(8,128)(2,1)}, bf16[1936,512]{1,0:T(8,128)(2,1)S(1)}, u32[]{:S(2)}, u32[]{:S(2)}) collective-permute-start(bf16[1936,512]{1,0:T(8,128)(2,1)} %gate.17.refs_2_.refs_5_.refs_7_.refs_1_), channel_id=1, source_target_pairs={{0,8},{4,12},{8,0},{12,4},{16,24},{20,28},{24,16},{28,20},{1,9},{5... | collective-permute-start | bytes 5947400 | tf_op jit(solution)/shard_map/ppermute | solution.py:175
  58.7 51.3 %collective-permute-start.4 = (bf16[1936,512]{1,0:T(8,128)(2,1)}, bf16[1936,512]{1,0:T(8,128)(2,1)S(1)}, u32[]{:S(2)}, u32[]{:S(2)}) collective-permute-start(bf16[1936,512]{1,0:T(8,128)(2,1)} %gate.17.refs_2_.refs_5_.refs_7_.refs_1_), channel_id=1, source_target_pairs={{0,16},{4,20},{8,24},{12,28},{16,0},{20,4},{24,8},{28,12},{1,17},{... | collective-permute-start | bytes 5947400 | tf_op jit(solution)/shard_map/ppermute | solution.py:175
  67.1 37.5 %collective-permute-start.8 = (bf16[400,2048]{1,0:T(8,128)(2,1)}, bf16[400,2048]{1,0:T(8,128)(2,1)}, u32[]{:S(2)}, u32[]{:S(2)}) collective-permute-start(bf16[400,2048]{1,0:T(8,128)(2,1)} %get-tuple-element.31.refs_3_), channel_id=1, source_target_pairs={{0,1},{1,2},{2,3},{4,5},{5,6},{6,7},{8,9},{9,10},{10,11},{12,13},{... | collective-permute-start | bytes 4915208 | tf_op jit(solution)/shard_map/ppermute | solution.py:179
  71.8 38.1 %collective-permute-start.9 = (bf16[400,2048]{1,0:T(8,128)(2,1)}, bf16[400,2048]{1,0:T(8,128)(2,1)}, u32[]{:S(2)}, u32[]{:S(2)}) collective-permute-start(bf16[400,2048]{1,0:T(8,128)(2,1)} %get-tuple-element.32), channel_id=1, source_target_pairs={{3,2},{2,1},{1,0},{7,6},{6,5},{5,4},{11,10},{10,9},{9,8},{15,14},{... | collective-permute-start | bytes 4915208 | tf_op jit(solution)/shard_map/ppermute | solution.py:183
  121.2 45.4 %collective-permute-start.10 = (bf16[1936,512]{1,0:T(8,128)(2,1)}, bf16[1936,512]{1,0:T(8,128)(2,1)S(1)}, u32[]{:S(2)}, u32[]{:S(2)}) collective-permute-start(bf16[1936,512]{1,0:T(8,128)(2,1)} %gate.20.refs_0_.refs_6_.refs_8_.refs_2_), channel_id=1, source_target_pairs={{0,16},{4,20},{8,24},{12,28},{16,0},{20,4},{24,8},{28,12},{1,17},{... | collective-permute-start | bytes 5947400 | tf_op jit(solution)/shard_map/ppermute | solution.py:175
  121.7 45.2 %collective-permute-start.11 = (bf16[1936,512]{1,0:T(8,128)(2,1)}, bf16[1936,512]{1,0:T(8,128)(2,1)}, u32[]{:S(2)}, u32[]{:S(2)}) collective-permute-start(bf16[1936,512]{1,0:T(8,128)(2,1)} %gate.21.refs_1_.refs_9_.refs_11_.refs_5_), channel_id=1, source_target_pairs={{0,8},{4,12},{8,0},{12,4},{16,24},{20,28},{24,16},{28,20},{1,9},{5... | collective-permute-start | bytes 5947400 | tf_op jit(solution)/shard_map/ppermute | solution.py:175
  122.2 39.4 %collective-permute-start.14 = (bf16[400,2048]{1,0:T(8,128)(2,1)}, bf16[400,2048]{1,0:T(8,128)(2,1)}, u32[]{:S(2)}, u32[]{:S(2)}) collective-permute-start(bf16[400,2048]{1,0:T(8,128)(2,1)} %get-tuple-element.34), channel_id=1, source_target_pairs={{3,2},{2,1},{1,0},{7,6},{6,5},{5,4},{11,10},{10,9},{9,8},{15,14},{... | collective-permute-start | bytes 4915208 | tf_op jit(solution)/shard_map/ppermute | solution.py:183
  125.4 38.5 %collective-permute-start.15 = (bf16[400,2048]{1,0:T(8,128)(2,1)}, bf16[400,2048]{1,0:T(8,128)(2,1)}, u32[]{:S(2)}, u32[]{:S(2)}) collective-permute-start(bf16[400,2048]{1,0:T(8,128)(2,1)} %get-tuple-element.33.refs_1_.refs_2_), channel_id=1, source_target_pairs={{0,1},{1,2},{2,3},{4,5},{5,6},{6,7},{8,9},{9,10},{10,11},{12,13},{... | collective-permute-start | bytes 4915208 | tf_op jit(solution)/shard_map/ppermute | solution.py:179
  174.4 31.1 %collective-permute-start.18 = (bf16[512,512]{1,0:T(8,128)(2,1)}, bf16[512,512]{1,0:T(8,128)(2,1)S(1)}, u32[]{:S(2)}, u32[]{:S(2)}) collective-permute-start(bf16[512,512]{1,0:T(8,128)(2,1)} %gate.23), channel_id=1, source_target_pairs={{0,8},{4,12},{8,0},{12,4},{16,24},{20,28},{24,16},{28,20},{1,9},{5... | collective-permute-start | bytes 1572872 | tf_op jit(solution)/shard_map/ppermute | solution.py:175
  175.0 33.0 %collective-permute-start.19 = (bf16[512,512]{1,0:T(8,128)(2,1)}, bf16[512,512]{1,0:T(8,128)(2,1)S(1)}, u32[]{:S(2)}, u32[]{:S(2)}) collective-permute-start(bf16[512,512]{1,0:T(8,128)(2,1)} %gate.24), channel_id=1, source_target_pairs={{0,16},{4,20},{8,24},{12,28},{16,0},{20,4},{24,8},{28,12},{1,17},{... | collective-permute-start | bytes 1572872 | tf_op jit(solution)/shard_map/ppermute | solution.py:175
  181.5 86.2 %collective-permute-start.21 = (bf16[384,2048]{1,0:T(8,128)(2,1)}, bf16[384,2048]{1,0:T(8,128)(2,1)}, u32[]{:S(2)}, u32[]{:S(2)}) collective-permute-start(bf16[384,2048]{1,0:T(8,128)(2,1)} %get-tuple-element.42), channel_id=1, source_target_pairs={{0,1},{1,2},{2,3},{4,5},{5,6},{6,7},{8,9},{9,10},{10,11},{12,13},{... | collective-permute-start | bytes 4718600 | tf_op jit(solution)/shard_map/ppermute | solution.py:179
  185.9 81.8 %collective-permute-start.22 = (bf16[384,2048]{1,0:T(8,128)(2,1)}, bf16[384,2048]{1,0:T(8,128)(2,1)}, u32[]{:S(2)}, u32[]{:S(2)}) collective-permute-start(bf16[384,2048]{1,0:T(8,128)(2,1)} %get-tuple-element.43), channel_id=1, source_target_pairs={{3,2},{2,1},{1,0},{7,6},{6,5},{5,4},{11,10},{10,9},{9,8},{15,14},{... | collective-permute-start | bytes 4718600 | tf_op jit(solution)/shard_map/ppermute | solution.py:183
  213.7 32.7 %collective-permute-start.23 = (bf16[512,512]{1,0:T(8,128)(2,1)}, bf16[512,512]{1,0:T(8,128)(2,1)S(1)}, u32[]{:S(2)}, u32[]{:S(2)}) collective-permute-start(bf16[512,512]{1,0:T(8,128)(2,1)} %gate.26), channel_id=1, source_target_pairs={{0,1},{1,0},{2,3},{3,2},{4,5},{5,4},{6,7},{7,6},{8,9},{9,8},{10,11... | collective-permute-start | bytes 1572872 | tf_op jit(solution)/shard_map/ppermute | solution.py:799
  216.3 42.8 %collective-permute-start.24 = (bf16[512,512]{1,0:T(8,128)(2,1)}, bf16[512,512]{1,0:T(8,128)(2,1)S(1)}, u32[]{:S(2)}, u32[]{:S(2)}) collective-permute-start(bf16[512,512]{1,0:T(8,128)(2,1)} %gate.27), channel_id=1, source_target_pairs={{0,2},{1,3},{2,0},{3,1},{4,6},{5,7},{6,4},{7,5},{8,10},{9,11},{10,... | collective-permute-start | bytes 1572872 | tf_op jit(solution)/shard_map/ppermute | solution.py:799
  217.6 41.5 %collective-permute-start.25 = (bf16[512,512]{1,0:T(8,128)(2,1)}, bf16[512,512]{1,0:T(8,128)(2,1)S(1)}, u32[]{:S(2)}, u32[]{:S(2)}) collective-permute-start(bf16[512,512]{1,0:T(8,128)(2,1)} %gate.28), channel_id=1, source_target_pairs={{0,3},{1,2},{2,1},{3,0},{4,7},{5,6},{6,5},{7,4},{8,11},{9,10},{10,... | collective-permute-start | bytes 1572872 | tf_op jit(solution)/shard_map/ppermute | solution.py:799
  264.7 32.2 %collective-permute-start.30 = (bf16[512,1024]{1,0:T(8,128)(2,1)}, bf16[512,1024]{1,0:T(8,128)(2,1)S(1)}, u32[]{:S(2)}, u32[]{:S(2)}) collective-permute-start(bf16[512,1024]{1,0:T(8,128)(2,1)} %get-tuple-element.47.refs_8_), channel_id=1, source_target_pairs={{0,8},{4,12},{8,0},{12,4},{16,24},{20,28},{24,16},{28,20},{1,9},{5... | collective-permute-start | bytes 3145736 | tf_op jit(solution)/shard_map/ppermute | solution.py:175
  269.0 31.1 %collective-permute-start.28 = (bf16[768,512]{1,0:T(8,128)(2,1)}, bf16[768,512]{1,0:T(8,128)(2,1)S(1)}, u32[]{:S(2)}, u32[]{:S(2)}) collective-permute-start(bf16[768,512]{1,0:T(8,128)(2,1)} %gate.29.refs_0_), channel_id=1, source_target_pairs={{0,1},{1,2},{2,3},{4,5},{5,6},{6,7},{8,9},{9,10},{10,11},{12,13},{... | collective-permute-start | bytes 2359304 | tf_op jit(solution)/shard_map/ppermute | solution.py:179
  281.2 41.5 %collective-permute-start.35 = (bf16[512,1024]{1,0:T(8,128)(2,1)}, bf16[512,1024]{1,0:T(8,128)(2,1)S(1)}, u32[]{:S(2)}, u32[]{:S(2)}) collective-permute-start(bf16[512,1024]{1,0:T(8,128)(2,1)} %get-tuple-element.48.refs_9_), channel_id=1, source_target_pairs={{0,8},{4,12},{8,0},{12,4},{16,24},{20,28},{24,16},{28,20},{1,9},{5... | collective-permute-start | bytes 3145736 | tf_op jit(solution)/shard_map/ppermute | solution.py:175
  302.9 37.8 %collective-permute-start.39 = (bf16[512,1024]{1,0:T(8,128)(2,1)S(1)}, bf16[512,1024]{1,0:T(8,128)(2,1)}, u32[]{:S(2)}, u32[]{:S(2)}) collective-permute-start(bf16[512,1024]{1,0:T(8,128)(2,1)S(1)} %copy-done.6), channel_id=1, source_target_pairs={{0,16},{4,20},{8,24},{12,28},{16,0},{20,4},{24,8},{28,12},{1,17},{... | collective-permute-start | bytes 3145736 | tf_op jit(solution)/shard_map/ppermute | solution.py:175
  (43 other events, 388.1 us)

commit v7 on v6

--- a/solution.py
+++ b/solution.py
@@ -422,13 +422,13 @@
 
 def absorb(s, v_ext, m, acc):
     new = jnp.maximum(m, jnp.max(s, axis=1, keepdims=True))
-    p = jnp.exp2((s - new).astype(jnp.bfloat16))
+    p = jnp.exp2(s - new).astype(jnp.bfloat16)
     acc = acc * jnp.exp2(m - new) + jnp.dot(p, v_ext, preferred_element_type=jnp.float32)
     return new, acc
 
 
 def attend_kernel(at_old, bound_ref, ids_ref, q_ref, n_ref, lo_ref, before_ref, new_ref, *refs):
-    bundles, (out_ref, k_old, v_ext, kv_near, s_ref, m_ref, acc_ref, sems) = refs[:8], refs[-8:]
+    bundles, (out_ref, k_old, k_turned, v_ext, kv_near, s_ref, m_ref, acc_ref, sems) = refs[:8], refs[-9:]
     halo = before_ref.shape[1]
     b = pl.program_id(0)
     heads, bt = q_ref.shape[0], q_ref.shape[1]
@@ -458,6 +458,8 @@
         kv_near[:, halo:] = new_ref[...]
         for copy in copies:
             copy.wait()
+        for at in range(0, k_old.shape[0], BK):
+            k_turned[:, at : at + BK] = k_old[at : at + BK, :].T
 
     m_ref[...] = jnp.full_like(m_ref, MASKED)
     acc_ref[...] = jnp.zeros_like(acc_ref)
@@ -465,7 +467,7 @@
     def query(g):
         return q_ref[g * CHAIN : (g + 1) * CHAIN].reshape(rows, HD)
 
-    s_ref[...] = scores(query(0), k_old[:BK, :])
+    s_ref[...] = jnp.dot(query(0), k_turned[:, :BK], preferred_element_type=jnp.float32)
 
     def body(kb, masked):
         start = pl.multiple_of(kb * BK, BK)
@@ -476,7 +478,9 @@
         v = v_ext[pl.ds(start, BK), :]
         for g in range(chains):
             at, who = (start, g + 1) if g + 1 < chains else (follow, 0)
-            ahead = scores(query(who), k_old[pl.ds(at, BK), :])
+            ahead = jnp.dot(
+                query(who), k_turned[:, pl.ds(at, BK)], preferred_element_type=jnp.float32
+            )
             if masked:
                 n_rows = jnp.concatenate([n_ref[:, :1]] * CHAIN, axis=0)
                 col = lax.broadcasted_iota(jnp.int32, s.shape, 1) + start
@@ -533,6 +537,7 @@
             out_specs=pl.BlockSpec((BT, heads * HD), lambda b, *_: (b, 0)),
             scratch_shapes=[
                 pltpu.VMEM((keys, HD), jnp.bfloat16),
+                pltpu.VMEM((HD, keys), jnp.bfloat16),
                 pltpu.VMEM((keys, 2 * HD), jnp.bfloat16),
                 pltpu.VMEM((2, halo + tokens, HD), jnp.bfloat16),
                 pltpu.VMEM((rows, BK), jnp.float32),

time: 370 us -> 370 us (level)
  no operation moved by 1% of the time
where the time goes in v7:
time: 370 us; the launch traced here: 367 us
  waiting for transfers between devices  147 us (40%)
  Pallas kernels  109 us (29%)
  starting transfers between devices  71.5 us (19%)
  other arithmetic  19.7 us (5%)
  local copies, waits for them, and re-layouts  16.7 us (5%)
    ppermute x25, waiting for transfers between devices, swap(): return lax.ppermute(x, 'ctx', [(c, c ^ bit) for c in range(N_CTX)])  50.5 us
    ppermute x7, waiting for transfers between devices, hop_down(): return lax.ppermute(v, 'tp', [(N_TP - 1 - i, N_TP - 2 - i) for i in pairs])  48.8 us
    pallas_call x10, Pallas kernels, move(): pl.pallas_call(kernel, out_shape=tuple((jax.ShapeDtypeStruct(shape, jnp.b...  37.8 us
    ppermute x7, starting transfers between devices, hop_up(): return lax.ppermute(v, 'tp', [(i, i + 1) for i in pairs])  33.1 us
    ppermute x7, waiting for transfers between devices, hop_up(): return lax.ppermute(v, 'tp', [(i, i + 1) for i in pairs])  29.2 us
    pallas_call x2, Pallas kernels, project(): pl.pallas_call(functools.partial(project_kernel, slots, len(xs), len(weig...  25.2 us
    ppermute x25, starting transfers between devices, swap(): return lax.ppermute(x, 'ctx', [(c, c ^ bit) for c in range(N_CTX)])  21.7 us
    pallas_call x1, Pallas kernels, attend(): pl.pallas_call(functools.partial(attend_kernel, at_old), out_shape=jax.Sh...  19.5 us
  transfers between devices with their start and end apart: 43, of which 17 were waited for; matrix products, arithmetic and copies ran while one was open for 5% of the time, Pallas kernels for 23%

profile of v7, /device:TPU:0, one launch (start us, length us, event | category | flops | bytes accessed | tf_op | source)
XLA Modules:
  0.0 367.0 jit_solution(12331465983170499347)
XLA Ops:
  4.3 5.0 %first_plan.1 = (bf16[1936,512]{1,0:T(8,128)(2,1)}, bf16[1936,512]{1,0:T(8,128)(2,1)}) custom-call(s32[3]{0:T(128)} %pad_add_fusion.1.ids_ref, bf16[1024,1024]{1,0:T(8,128)(2,1)} %refs_0_.2, bf16[1024,1024]{1,0:T(8,128)(2,1)} %refs_1_.1, bf16[1024,1024]{1,0:T(8,128)(2,1)} %refs_2_.1, bf16[8,768,128]{2,1,0:T(8,128)(2,1)} %refs_3_.1, ...), custom_call_target="tpu_custom_call" | custom-call | bytes 1024 | tf_op jit(solution)/shard_map/first_plan/pallas_call | solution.py:218
  18.2 4.7 %collective-permute-start.6 = (bf16[400,2048]{1,0:T(8,128)(2,1)}, bf16[400,2048]{1,0:T(8,128)(2,1)}, u32[]{:S(2)}, u32[]{:S(2)}) collective-permute-start(bf16[400,2048]{1,0:T(8,128)(2,1)} %gate.19.refs_0_), channel_id=1, source_target_pairs={{0,1},{1,2},{2,3},{4,5},{5,6},{6,7},{8,9},{9,10},{10,11},{12,13},{... | collective-permute-start | bytes 4915208 | tf_op jit(solution)/shard_map/ppermute | solution.py:179
  28.7 27.0 %collective-permute-done.1.refs_1_.refs_0_ = bf16[1936,512]{1,0:T(8,128)(2,1)S(1)} collective-permute-done((bf16[1936,512]{1,0:T(8,128)(2,1)}, bf16[1936,512]{1,0:T(8,128)(2,1)S(1)}, u32[]{:S(2)}, u32[]{:S(2)}) %collective-permute-start.1) | collective-permute-done | bytes 1982496 | tf_op jit(solution)/shard_map/ppermute | solution.py:175
  62.8 4.3 %hops.3 = (bf16[400,2048]{1,0:T(8,128)(2,1)}, bf16[400,2048]{1,0:T(8,128)(2,1)}) custom-call(s32[3]{0:T(128)} %pad_add_fusion.1.ids_ref, bf16[1,384,8192]{2,1,0:T(8,128)(2,1)} %pending_ref.5, bf16[400,2048]{1,0:T(8,128)(2,1)} %collective-permute-done.6.up_ref.refs_1_, bf16[400,2048]{1,0:T(8,128)(2,1)} %collective-permute-done.7.down_ref.refs_2_, ...), custom_call_target="tpu_custom_call" | custom-call | bytes 1024 | tf_op jit(solution)/shard_map/hops/pallas_call | solution.py:295
  67.1 4.7 %collective-permute-start.8 = (bf16[400,2048]{1,0:T(8,128)(2,1)}, bf16[400,2048]{1,0:T(8,128)(2,1)}, u32[]{:S(2)}, u32[]{:S(2)}) collective-permute-start(bf16[400,2048]{1,0:T(8,128)(2,1)} %get-tuple-element.31.refs_3_), channel_id=1, source_target_pairs={{0,1},{1,2},{2,3},{4,5},{5,6},{6,7},{8,9},{9,10},{10,11},{12,13},{... | collective-permute-start | bytes 4915208 | tf_op jit(solution)/shard_map/ppermute | solution.py:179
  73.1 4.7 %near_plan.1.refs_2_.refs_0_ = bf16[800,2048]{1,0:T(8,128)(2,1)} custom-call(s32[3]{0:T(128)} %pad_add_fusion.1.ids_ref, bf16[400,2048]{1,0:T(8,128)(2,1)} %gate.19.refs_0_, bf16[400,2048]{1,0:T(8,128)(2,1)} %collective-permute-done.6.up_ref.refs_1_, bf16[400,2048]{1,0:T(8,128)(2,1)} %collective-permute-done.7.down_ref.refs_2_, ...), custom_call_target="tpu_custom_call" | custom-call | bytes 1024 | tf_op jit(solution)/shard_map/near_plan/pallas_call | solution.py:218
  77.8 26.9 %collective-permute-done.8.refs_3_.refs_2_.up_ref.refs_1_ = bf16[400,2048]{1,0:T(8,128)(2,1)} collective-permute-done((bf16[400,2048]{1,0:T(8,128)(2,1)}, bf16[400,2048]{1,0:T(8,128)(2,1)}, u32[]{:S(2)}, u32[]{:S(2)}) %collective-permute-start.8) | collective-permute-done | bytes 1638432 | tf_op jit(solution)/shard_map/ppermute | solution.py:179
  104.7 5.3 %collective-permute-done.9.refs_4_.refs_3_.down_ref.refs_0_ = bf16[400,2048]{1,0:T(8,128)(2,1)} collective-permute-done((bf16[400,2048]{1,0:T(8,128)(2,1)}, bf16[400,2048]{1,0:T(8,128)(2,1)}, u32[]{:S(2)}, u32[]{:S(2)}) %collective-permute-start.9) | collective-permute-done | bytes 1638432 | tf_op jit(solution)/shard_map/ppermute | solution.py:183
  112.5 4.3 %hops.4 = (bf16[400,2048]{1,0:T(8,128)(2,1)}, bf16[400,2048]{1,0:T(8,128)(2,1)}) custom-call(s32[3]{0:T(128)} %pad_add_fusion.1.ids_ref, bf16[1,384,8192]{2,1,0:T(8,128)(2,1)} %pending_ref.5, bf16[400,2048]{1,0:T(8,128)(2,1)} %collective-permute-done.8.refs_3_.refs_2_.up_ref.refs_1_, ...), custom_call_target="tpu_custom_call" | custom-call | bytes 1024 | tf_op jit(solution)/shard_map/hops/pallas_call | solution.py:295
  125.4 4.0 %collective-permute-start.15 = (bf16[400,2048]{1,0:T(8,128)(2,1)}, bf16[400,2048]{1,0:T(8,128)(2,1)}, u32[]{:S(2)}, u32[]{:S(2)}) collective-permute-start(bf16[400,2048]{1,0:T(8,128)(2,1)} %get-tuple-element.33.refs_1_.refs_2_), channel_id=1, source_target_pairs={{0,1},{1,2},{2,3},{4,5},{5,6},{6,7},{8,9},{9,10},{10,11},{12,13},{... | collective-permute-start | bytes 4915208 | tf_op jit(solution)/shard_map/ppermute | solution.py:179
  133.4 11.9 %project.2.refs_4_.refs_14_ = f32[768,768]{1,0:T(8,128)} custom-call(s32[11]{0:T(128)} %concatenate.54.ids_ref, bf16[800,2048]{1,0:T(8,128)(2,1)} %gate.22.refs_0_, bf16[800,2048]{1,0:T(8,128)(2,1)} %collective-permute-done.12.refs_1_, bf16[400,2048]{1,0:T(8,128)(2,1)} %pick_plan.5.refs_2_, bf16[400,2048]{1,0:T(8,128)(2,1)} %collective-permute-done.13.refs_3_, ...), custom_call_target="tpu_custom_call" | custom-call | bytes 1024 | tf_op jit(solution)/shard_map/project/pallas_call | solution.py:395
  145.3 16.3 %collective-permute-done.14.refs_0_.down_ref = bf16[400,2048]{1,0:T(8,128)(2,1)} collective-permute-done((bf16[400,2048]{1,0:T(8,128)(2,1)}, bf16[400,2048]{1,0:T(8,128)(2,1)}, u32[]{:S(2)}, u32[]{:S(2)}) %collective-permute-start.14) | collective-permute-done | bytes 1638432 | tf_op jit(solution)/shard_map/ppermute | solution.py:183
  176.4 5.0 %hops.5 = (bf16[384,2048]{1,0:T(8,128)(2,1)}, bf16[384,2048]{1,0:T(8,128)(2,1)}) custom-call(s32[3]{0:T(128)} %pad_add_fusion.1.ids_ref, bf16[1,384,8192]{2,1,0:T(8,128)(2,1)} %pending_ref.5, bf16[400,2048]{1,0:T(8,128)(2,1)} %collective-permute-done.15.refs_3_.up_ref, bf16[400,2048]{1,0:T(8,128)(2,1)} %collective-permute-done.14.refs_0_.down_ref, ...), custom_call_target="tpu_custom_call" | custom-call | bytes 1024 | tf_op jit(solution)/shard_map/hops/pallas_call | solution.py:295
  181.5 4.5 %collective-permute-start.21 = (bf16[384,2048]{1,0:T(8,128)(2,1)}, bf16[384,2048]{1,0:T(8,128)(2,1)}, u32[]{:S(2)}, u32[]{:S(2)}) collective-permute-start(bf16[384,2048]{1,0:T(8,128)(2,1)} %get-tuple-element.42), channel_id=1, source_target_pairs={{0,1},{1,2},{2,3},{4,5},{5,6},{6,7},{8,9},{9,10},{10,11},{12,13},{... | collective-permute-start | bytes 4718600 | tf_op jit(solution)/shard_map/ppermute | solution.py:179
  192.3 13.2 %project.3 = (bf16[4,768,128]{2,1,0:T(8,128)(2,1)}, bf16[2,768,128]{2,1,0:T(8,128)(2,1)}, bf16[2,384,128]{2,1,0:T(8,128)(2,1)}) custom-call(s32[11]{0:T(128)} %concatenate.54.ids_ref, bf16[800,2048]{1,0:T(8,128)(2,1)} %gate.22.refs_0_, bf16[800,2048]{1,0:T(8,128)(2,1)} %collective-permute-done.12.refs_1_, bf16[400,2048]{1,0:T(8,128)(2,1)} %pick_plan.5.refs_2_, ...), custom_call_target="tpu_custom_call" | custom-call | bytes 1024 | tf_op jit(solution)/shard_map/project/pallas_call | solution.py:395
  221.4 19.5 %attend.1.refs_0_.refs_4_ = bf16[768,512]{1,0:T(8,128)(2,1)} custom-call(s32[2,3]{1,0:T(2,128)} %pad_add_fusion.bound_ref, s32[3]{0:T(128)} %pad_add_fusion.1.ids_ref, bf16[4,768,128]{2,1,0:T(8,128)(2,1)} %get-tuple-element.35.refs_4_.q_ref, s32[768,128]{1,0:T(8,128)} %broadcast_in_dim.16.n_ref, s32[768,128]{1,0:T(8,128)} %broadcast_in_dim.17.lo_ref, ...), custom_call_target="tpu_custom_call" | custom-call | bytes 1024 | tf_op jit(solution)/shard_map/attend/pallas_call | solution.py:522
  240.9 5.5 %collective-permute-done.23.refs_3_.refs_1_ = bf16[512,512]{1,0:T(8,128)(2,1)S(1)} collective-permute-done((bf16[512,512]{1,0:T(8,128)(2,1)}, bf16[512,512]{1,0:T(8,128)(2,1)S(1)}, u32[]{:S(2)}, u32[]{:S(2)}) %collective-permute-start.23) | collective-permute-done | bytes 524320 | tf_op jit(solution)/shard_map/ppermute | solution.py:804
  246.4 12.7 %collective-permute-done.24.refs_4_.refs_2_ = bf16[512,512]{1,0:T(8,128)(2,1)S(1)} collective-permute-done((bf16[512,512]{1,0:T(8,128)(2,1)}, bf16[512,512]{1,0:T(8,128)(2,1)S(1)}, u32[]{:S(2)}, u32[]{:S(2)}) %collective-permute-start.24) | collective-permute-done | bytes 524320 | tf_op jit(solution)/shard_map/ppermute | solution.py:804
  269.3 11.9 %collective-permute-start.28 = (bf16[768,512]{1,0:T(8,128)(2,1)}, bf16[768,512]{1,0:T(8,128)(2,1)S(1)}, u32[]{:S(2)}, u32[]{:S(2)}) collective-permute-start(bf16[768,512]{1,0:T(8,128)(2,1)} %gate.29.refs_0_), channel_id=1, source_target_pairs={{0,1},{1,2},{2,3},{4,5},{5,6},{6,7},{8,9},{9,10},{10,11},{12,13},{... | collective-permute-start | bytes 2359304 | tf_op jit(solution)/shard_map/ppermute | solution.py:179
  281.8 13.5 %collective-permute-done.27.refs_0_.refs_2_ = bf16[768,512]{1,0:T(8,128)(2,1)S(1)} collective-permute-done((bf16[768,512]{1,0:T(8,128)(2,1)}, bf16[768,512]{1,0:T(8,128)(2,1)S(1)}, u32[]{:S(2)}, u32[]{:S(2)}) %collective-permute-start.27) | collective-permute-done | bytes 786464 | tf_op jit(solution)/shard_map/ppermute | solution.py:183
  304.4 13.7 %collective-permute-done.32.refs_0_ = bf16[768,512]{1,0:T(8,128)(2,1)} collective-permute-done((bf16[768,512]{1,0:T(8,128)(2,1)}, bf16[768,512]{1,0:T(8,128)(2,1)}, u32[]{:S(2)}, u32[]{:S(2)}) %collective-permute-start.32) | collective-permute-done | bytes 786464 | tf_op jit(solution)/shard_map/ppermute | solution.py:183
  329.9 10.9 %collective-permute-done.39.refs_4_.refs_14_ = bf16[512,1024]{1,0:T(8,128)(2,1)} collective-permute-done((bf16[512,1024]{1,0:T(8,128)(2,1)S(1)}, bf16[512,1024]{1,0:T(8,128)(2,1)}, u32[]{:S(2)}, u32[]{:S(2)}) %collective-permute-start.39) | collective-permute-done | bytes 1048608 | tf_op jit(solution)/shard_map/ppermute | solution.py:175
  347.1 13.2 %out_project.1 = (bf16[384,1024]{1,0:T(8,128)(2,1)}, bf16[384,1024]{1,0:T(8,128)(2,1)}) custom-call(s32[11]{0:T(128)} %concatenate.54.ids_ref, bf16[768,512]{1,0:T(8,128)(2,1)} %gate.29.refs_0_, bf16[768,512]{1,0:T(8,128)(2,1)} %collective-permute-done.26.refs_1_, bf16[768,512]{1,0:T(8,128)(2,1)} %pick_plan.7.refs_2_, ...), custom_call_target="tpu_custom_call" | custom-call | bytes 1024 | tf_op jit(solution)/shard_map/out_project/pallas_call | solution.py:595
  362.8 4.2 %fusion.2 = bf16[384,2048]{1,0:T(8,128)(2,1)} fusion(bf16[384,2048]{1,0:T(8,128)(2,1)S(1)} %copy-done.13, bf16[384,1024]{1,0:T(8,128)(2,1)S(1)} %collective-permute-done.42, bf16[384,1024]{1,0:T(8,128)(2,1)} %get-tuple-element.49, bf16[384,2048]{1,0:T(8,128)(2,1)} %collective-permute-done.22.refs_2_, bf16[384,2048]{1,0:T(8,128)(2,1)} %collective-permute-done.21.refs_1_, ...), kind=kLoop, calls=%fused_computation.5 | loop fusion | flops 16515072 | bytes 9437191 | tf_op jit(solution)/shard_map/convert_element_type | solution.py:855
  (197 shorter events, 117.1 us)
Async XLA Ops:
  9.3 46.4 %collective-permute-start.1 = (bf16[1936,512]{1,0:T(8,128)(2,1)}, bf16[1936,512]{1,0:T(8,128)(2,1)S(1)}, u32[]{:S(2)}, u32[]{:S(2)}) collective-permute-start(bf16[1936,512]{1,0:T(8,128)(2,1)} %get-tuple-element.28.refs_1_.refs_4_.refs_6_.refs_0_), channel_id=1, source_target_pairs={{0,8},{4,12},{8,0},{12,4},{16,24},{20,28},{24,16},{28,20},{1,9},{5... | collective-permute-start | bytes 5947400 | tf_op jit(solution)/shard_map/ppermute | solution.py:175
  12.3 44.9 %collective-permute-start.2 = (bf16[1936,512]{1,0:T(8,128)(2,1)}, bf16[1936,512]{1,0:T(8,128)(2,1)}, u32[]{:S(2)}, u32[]{:S(2)}) collective-permute-start(bf16[1936,512]{1,0:T(8,128)(2,1)} %get-tuple-element.28.refs_1_.refs_4_.refs_6_.refs_0_), channel_id=1, source_target_pairs={{0,16},{4,20},{8,24},{12,28},{16,0},{20,4},{24,8},{28,12},{1,17},{... | collective-permute-start | bytes 5947400 | tf_op jit(solution)/shard_map/ppermute | solution.py:175
  13.8 41.9 %collective-permute-start = (bf16[1936,512]{1,0:T(8,128)(2,1)}, bf16[1936,512]{1,0:T(8,128)(2,1)}, u32[]{:S(2)}, u32[]{:S(2)}) collective-permute-start(bf16[1936,512]{1,0:T(8,128)(2,1)} %get-tuple-element.29), channel_id=1, source_target_pairs={{0,4},{4,0},{8,12},{12,8},{16,20},{20,16},{24,28},{28,24},{1,5},{5... | collective-permute-start | bytes 5947400 | tf_op jit(solution)/shard_map/ppermute | solution.py:175
  18.2 44.6 %collective-permute-start.6 = (bf16[400,2048]{1,0:T(8,128)(2,1)}, bf16[400,2048]{1,0:T(8,128)(2,1)}, u32[]{:S(2)}, u32[]{:S(2)}) collective-permute-start(bf16[400,2048]{1,0:T(8,128)(2,1)} %gate.19.refs_0_), channel_id=1, source_target_pairs={{0,1},{1,2},{2,3},{4,5},{5,6},{6,7},{8,9},{9,10},{10,11},{12,13},{... | collective-permute-start | bytes 4915208 | tf_op jit(solution)/shard_map/ppermute | solution.py:179
  22.9 40.0 %collective-permute-start.7 = (bf16[400,2048]{1,0:T(8,128)(2,1)}, bf16[400,2048]{1,0:T(8,128)(2,1)}, u32[]{:S(2)}, u32[]{:S(2)}) collective-permute-start(bf16[400,2048]{1,0:T(8,128)(2,1)} %gate.19.refs_0_), channel_id=1, source_target_pairs={{3,2},{2,1},{1,0},{7,6},{6,5},{5,4},{11,10},{10,9},{9,8},{15,14},{... | collective-permute-start | bytes 4915208 | tf_op jit(solution)/shard_map/ppermute | solution.py:183
  57.3 52.7 %collective-permute-start.3 = (bf16[1936,512]{1,0:T(8,128)(2,1)}, bf16[1936,512]{1,0:T(8,128)(2,1)S(1)}, u32[]{:S(2)}, u32[]{:S(2)}) collective-permute-start(bf16[1936,512]{1,0:T(8,128)(2,1)} %gate.17.refs_2_.refs_5_.refs_7_.refs_1_), channel_id=1, source_target_pairs={{0,8},{4,12},{8,0},{12,4},{16,24},{20,28},{24,16},{28,20},{1,9},{5... | collective-permute-start | bytes 5947400 | tf_op jit(solution)/shard_map/ppermute | solution.py:175
  58.7 51.3 %collective-permute-start.4 = (bf16[1936,512]{1,0:T(8,128)(2,1)}, bf16[1936,512]{1,0:T(8,128)(2,1)S(1)}, u32[]{:S(2)}, u32[]{:S(2)}) collective-permute-start(bf16[1936,512]{1,0:T(8,128)(2,1)} %gate.17.refs_2_.refs_5_.refs_7_.refs_1_), channel_id=1, source_target_pairs={{0,16},{4,20},{8,24},{12,28},{16,0},{20,4},{24,8},{28,12},{1,17},{... | collective-permute-start | bytes 5947400 | tf_op jit(solution)/shard_map/ppermute | solution.py:175
  67.1 37.5 %collective-permute-start.8 = (bf16[400,2048]{1,0:T(8,128)(2,1)}, bf16[400,2048]{1,0:T(8,128)(2,1)}, u32[]{:S(2)}, u32[]{:S(2)}) collective-permute-start(bf16[400,2048]{1,0:T(8,128)(2,1)} %get-tuple-element.31.refs_3_), channel_id=1, source_target_pairs={{0,1},{1,2},{2,3},{4,5},{5,6},{6,7},{8,9},{9,10},{10,11},{12,13},{... | collective-permute-start | bytes 4915208 | tf_op jit(solution)/shard_map/ppermute | solution.py:179
  71.8 38.1 %collective-permute-start.9 = (bf16[400,2048]{1,0:T(8,128)(2,1)}, bf16[400,2048]{1,0:T(8,128)(2,1)}, u32[]{:S(2)}, u32[]{:S(2)}) collective-permute-start(bf16[400,2048]{1,0:T(8,128)(2,1)} %get-tuple-element.32), channel_id=1, source_target_pairs={{3,2},{2,1},{1,0},{7,6},{6,5},{5,4},{11,10},{10,9},{9,8},{15,14},{... | collective-permute-start | bytes 4915208 | tf_op jit(solution)/shard_map/ppermute | solution.py:183
  121.2 45.4 %collective-permute-start.10 = (bf16[1936,512]{1,0:T(8,128)(2,1)}, bf16[1936,512]{1,0:T(8,128)(2,1)S(1)}, u32[]{:S(2)}, u32[]{:S(2)}) collective-permute-start(bf16[1936,512]{1,0:T(8,128)(2,1)} %gate.20.refs_0_.refs_6_.refs_8_.refs_2_), channel_id=1, source_target_pairs={{0,16},{4,20},{8,24},{12,28},{16,0},{20,4},{24,8},{28,12},{1,17},{... | collective-permute-start | bytes 5947400 | tf_op jit(solution)/shard_map/ppermute | solution.py:175
  121.7 45.2 %collective-permute-start.11 = (bf16[1936,512]{1,0:T(8,128)(2,1)}, bf16[1936,512]{1,0:T(8,128)(2,1)}, u32[]{:S(2)}, u32[]{:S(2)}) collective-permute-start(bf16[1936,512]{1,0:T(8,128)(2,1)} %gate.21.refs_1_.refs_9_.refs_11_.refs_5_), channel_id=1, source_target_pairs={{0,8},{4,12},{8,0},{12,4},{16,24},{20,28},{24,16},{28,20},{1,9},{5... | collective-permute-start | bytes 5947400 | tf_op jit(solution)/shard_map/ppermute | solution.py:175
  122.2 39.4 %collective-permute-start.14 = (bf16[400,2048]{1,0:T(8,128)(2,1)}, bf16[400,2048]{1,0:T(8,128)(2,1)}, u32[]{:S(2)}, u32[]{:S(2)}) collective-permute-start(bf16[400,2048]{1,0:T(8,128)(2,1)} %get-tuple-element.34), channel_id=1, source_target_pairs={{3,2},{2,1},{1,0},{7,6},{6,5},{5,4},{11,10},{10,9},{9,8},{15,14},{... | collective-permute-start | bytes 4915208 | tf_op jit(solution)/shard_map/ppermute | solution.py:183
  125.4 38.5 %collective-permute-start.15 = (bf16[400,2048]{1,0:T(8,128)(2,1)}, bf16[400,2048]{1,0:T(8,128)(2,1)}, u32[]{:S(2)}, u32[]{:S(2)}) collective-permute-start(bf16[400,2048]{1,0:T(8,128)(2,1)} %get-tuple-element.33.refs_1_.refs_2_), channel_id=1, source_target_pairs={{0,1},{1,2},{2,3},{4,5},{5,6},{6,7},{8,9},{9,10},{10,11},{12,13},{... | collective-permute-start | bytes 4915208 | tf_op jit(solution)/shard_map/ppermute | solution.py:179
  174.4 31.1 %collective-permute-start.18 = (bf16[512,512]{1,0:T(8,128)(2,1)}, bf16[512,512]{1,0:T(8,128)(2,1)S(1)}, u32[]{:S(2)}, u32[]{:S(2)}) collective-permute-start(bf16[512,512]{1,0:T(8,128)(2,1)} %gate.23), channel_id=1, source_target_pairs={{0,8},{4,12},{8,0},{12,4},{16,24},{20,28},{24,16},{28,20},{1,9},{5... | collective-permute-start | bytes 1572872 | tf_op jit(solution)/shard_map/ppermute | solution.py:175
  175.0 33.0 %collective-permute-start.19 = (bf16[512,512]{1,0:T(8,128)(2,1)}, bf16[512,512]{1,0:T(8,128)(2,1)S(1)}, u32[]{:S(2)}, u32[]{:S(2)}) collective-permute-start(bf16[512,512]{1,0:T(8,128)(2,1)} %gate.24), channel_id=1, source_target_pairs={{0,16},{4,20},{8,24},{12,28},{16,0},{20,4},{24,8},{28,12},{1,17},{... | collective-permute-start | bytes 1572872 | tf_op jit(solution)/shard_map/ppermute | solution.py:175
  181.5 86.6 %collective-permute-start.21 = (bf16[384,2048]{1,0:T(8,128)(2,1)}, bf16[384,2048]{1,0:T(8,128)(2,1)}, u32[]{:S(2)}, u32[]{:S(2)}) collective-permute-start(bf16[384,2048]{1,0:T(8,128)(2,1)} %get-tuple-element.42), channel_id=1, source_target_pairs={{0,1},{1,2},{2,3},{4,5},{5,6},{6,7},{8,9},{9,10},{10,11},{12,13},{... | collective-permute-start | bytes 4718600 | tf_op jit(solution)/shard_map/ppermute | solution.py:179
  185.9 82.1 %collective-permute-start.22 = (bf16[384,2048]{1,0:T(8,128)(2,1)}, bf16[384,2048]{1,0:T(8,128)(2,1)}, u32[]{:S(2)}, u32[]{:S(2)}) collective-permute-start(bf16[384,2048]{1,0:T(8,128)(2,1)} %get-tuple-element.43), channel_id=1, source_target_pairs={{3,2},{2,1},{1,0},{7,6},{6,5},{5,4},{11,10},{10,9},{9,8},{15,14},{... | collective-permute-start | bytes 4718600 | tf_op jit(solution)/shard_map/ppermute | solution.py:183
  213.7 32.7 %collective-permute-start.23 = (bf16[512,512]{1,0:T(8,128)(2,1)}, bf16[512,512]{1,0:T(8,128)(2,1)S(1)}, u32[]{:S(2)}, u32[]{:S(2)}) collective-permute-start(bf16[512,512]{1,0:T(8,128)(2,1)} %gate.26), channel_id=1, source_target_pairs={{0,1},{1,0},{2,3},{3,2},{4,5},{5,4},{6,7},{7,6},{8,9},{9,8},{10,11... | collective-permute-start | bytes 1572872 | tf_op jit(solution)/shard_map/ppermute | solution.py:804
  216.3 42.8 %collective-permute-start.24 = (bf16[512,512]{1,0:T(8,128)(2,1)}, bf16[512,512]{1,0:T(8,128)(2,1)S(1)}, u32[]{:S(2)}, u32[]{:S(2)}) collective-permute-start(bf16[512,512]{1,0:T(8,128)(2,1)} %gate.27), channel_id=1, source_target_pairs={{0,2},{1,3},{2,0},{3,1},{4,6},{5,7},{6,4},{7,5},{8,10},{9,11},{10,... | collective-permute-start | bytes 1572872 | tf_op jit(solution)/shard_map/ppermute | solution.py:804
  217.6 41.5 %collective-permute-start.25 = (bf16[512,512]{1,0:T(8,128)(2,1)}, bf16[512,512]{1,0:T(8,128)(2,1)S(1)}, u32[]{:S(2)}, u32[]{:S(2)}) collective-permute-start(bf16[512,512]{1,0:T(8,128)(2,1)} %gate.28), channel_id=1, source_target_pairs={{0,3},{1,2},{2,1},{3,0},{4,7},{5,6},{6,5},{7,4},{8,11},{9,10},{10,... | collective-permute-start | bytes 1572872 | tf_op jit(solution)/shard_map/ppermute | solution.py:804
  264.7 32.2 %collective-permute-start.30 = (bf16[512,1024]{1,0:T(8,128)(2,1)}, bf16[512,1024]{1,0:T(8,128)(2,1)S(1)}, u32[]{:S(2)}, u32[]{:S(2)}) collective-permute-start(bf16[512,1024]{1,0:T(8,128)(2,1)} %get-tuple-element.47.refs_8_), channel_id=1, source_target_pairs={{0,8},{4,12},{8,0},{12,4},{16,24},{20,28},{24,16},{28,20},{1,9},{5... | collective-permute-start | bytes 3145736 | tf_op jit(solution)/shard_map/ppermute | solution.py:175
  269.3 30.8 %collective-permute-start.28 = (bf16[768,512]{1,0:T(8,128)(2,1)}, bf16[768,512]{1,0:T(8,128)(2,1)S(1)}, u32[]{:S(2)}, u32[]{:S(2)}) collective-permute-start(bf16[768,512]{1,0:T(8,128)(2,1)} %gate.29.refs_0_), channel_id=1, source_target_pairs={{0,1},{1,2},{2,3},{4,5},{5,6},{6,7},{8,9},{9,10},{10,11},{12,13},{... | collective-permute-start | bytes 2359304 | tf_op jit(solution)/shard_map/ppermute | solution.py:179
  281.2 41.5 %collective-permute-start.35 = (bf16[512,1024]{1,0:T(8,128)(2,1)}, bf16[512,1024]{1,0:T(8,128)(2,1)S(1)}, u32[]{:S(2)}, u32[]{:S(2)}) collective-permute-start(bf16[512,1024]{1,0:T(8,128)(2,1)} %get-tuple-element.48.refs_9_), channel_id=1, source_target_pairs={{0,8},{4,12},{8,0},{12,4},{16,24},{20,28},{24,16},{28,20},{1,9},{5... | collective-permute-start | bytes 3145736 | tf_op jit(solution)/shard_map/ppermute | solution.py:175
  302.9 37.8 %collective-permute-start.39 = (bf16[512,1024]{1,0:T(8,128)(2,1)S(1)}, bf16[512,1024]{1,0:T(8,128)(2,1)}, u32[]{:S(2)}, u32[]{:S(2)}) collective-permute-start(bf16[512,1024]{1,0:T(8,128)(2,1)S(1)} %copy-done.6), channel_id=1, source_target_pairs={{0,16},{4,20},{8,24},{12,28},{16,0},{20,4},{24,8},{28,12},{1,17},{... | collective-permute-start | bytes 3145736 | tf_op jit(solution)/shard_map/ppermute | solution.py:175
  (43 other events, 387.8 us)
